TPU v7x, 512 devices: a whole 4x8x8 slice. The times are simulated.
512 devices in a mesh: rx: 32 (over z, x), ry: 16 (over y, core).
Axes of the slice: x: 4, y: 8, z: 8, core: 2. Of those that a mesh axis runs over, the one named last changes fastest.
Arguments:
- start_block: bfloat16 [64, 524288], P(None, ('rx', 'ry')), may hold values from -0.4 to 0.4
- operator_tiles: bfloat16 [4096, 8, 128, 128], P(('rx', 'ry')), may hold values from -0.125 to 0.125
- tile_pattern: int32 [4096, 8], P(('rx', 'ry')), may hold values from 0 to 4095, as said below
Outputs:
- basis_block: float32 [64, 524288], P(None, ('rx', 'ry'))
- factor: float32 [64, 64], replicated
Inputs may be any that keep to these rules, and one draw needn't show every extreme that they name: `tile_pattern`: entry [i, 0] is i. Every entry j of row i has |j - i| <= 16. Entries 1 and 2 of row i are i - 16 and i + 16, reflected at the ends of the range. A row may name a column more than once.
All inputs are finite; a program needn't handle non-finite values.
Results may differ from a plain program's by a relative error of at most 0.015.
Values may be sent and summed in bfloat16 or wider, within the bound.
No kernel may reach another device: no remote copies, remote signals or barrier semaphores. Data moves between devices by JAX's collectives and lax.ppermute only.
A program may use at most 64 MiB of HBM per device.

v0:
```python
import jax
import jax.numpy as jnp
from jax import lax
from jax.sharding import PartitionSpec as P

SPAN = 2
DEG = 12


def shifted(value, axis, steps):
    count = lax.axis_size(axis)
    first, last = (max(0, -steps), min(count, count - steps))
    return lax.ppermute(value, axis, [(source, source + steps) for source in range(first, last)])


def partner_2(block, axis, apart):
    count = lax.axis_size(axis)
    route = []
    for low in range(count):
        high = low | 1 << apart
        if high != low and high < count:
            route += [(low, high), (high, low)]
    return lax.ppermute(block, axis, route)


def shards(start_block, operator_tiles, tile_pattern):
    vectors, node_count = start_block.shape
    rows_local = operator_tiles.shape[0]
    tile_size = operator_tiles.shape[2]
    device_count = lax.axis_size(("rx", "ry"))
    position = lax.axis_index(("rx", "ry"))
    local_index = tile_pattern - (position - SPAN) * rows_local

    def apply_operator(moving_block):
        pieces = []
        for offset in range(SPAN, -SPAN - 1, -1):
            if offset == 0:
                pieces.append(moving_block)
            else:
                pieces.append(shifted(moving_block, ("rx", "ry"), offset))
        window = jnp.concatenate(pieces, axis=1).reshape(
            vectors, (2 * SPAN + 1) * rows_local, tile_size
        )
        picked = jnp.take(window, local_index, axis=1)
        product = jnp.einsum(
            "vrkt,rkst->vrs", picked, operator_tiles, preferred_element_type=jnp.float32
        )
        return product.reshape(vectors, node_count)

    earlier = start_block.astype(jnp.float32)
    current = apply_operator(start_block)

    def chebyshev_step(round_index, carry):
        older, latest = carry
        following = 2.0 * apply_operator(latest.astype(jnp.bfloat16)) - older
        return (latest, following)

    earlier, current = lax.fori_loop(0, DEG - 1, chebyshev_step, (earlier, current))
    node_total = float(node_count * device_count)
    gram_local = (
        lax.dot_general(
            current,
            current,
            (((1,), (1,)), ((), ())),
            precision=lax.Precision.HIGHEST,
            preferred_element_type=jnp.float32,
        )
        / node_total
    )
    lower_factor = jnp.linalg.cholesky(gram_local)
    for bit_number in range(device_count.bit_length() - 1):
        partner = partner_2(lower_factor, ("rx", "ry"), bit_number)
        own_part = jnp.dot(lower_factor, lower_factor.T, precision=lax.Precision.HIGHEST)
        partner_part = jnp.dot(partner, partner.T, precision=lax.Precision.HIGHEST)
        lower_factor = jnp.linalg.cholesky(own_part + partner_part)
    basis_block = lax.linalg.triangular_solve(lower_factor, current, left_side=True, lower=True)
    return (basis_block, lower_factor.T)


def solution(mesh):
    return jax.shard_map(
        shards,
        mesh=mesh,
        in_specs=(P(None, ("rx", "ry")), P(("rx", "ry"), None, None, None), P(("rx", "ry"), None)),
        out_specs=(P(None, ("rx", "ry")), P()),
        check_vma=False,
    )
```

profile of v0, /device:TPU:62, one launch (start us, length us, event | category | flops | bytes accessed | tf_op | source)
XLA Modules:
  0.0 429.7 jit_solution(5681625617456554220)
XLA Ops:
  0.6 3.4 collective-permute-start.4
  6.0 3.6 collective-permute-start.6
  14.0 7.4 %collective-permute-done.7 = bf16[64,1024]{1,0:T(8,128)(2,1)S(1)} collective-permute-done((bf16[64,1024]{1,0:T(8,128)(2,1)}, bf16[64,1024]{1,0:T(8,128)(2,1)S(1)}, u32[]{:S(2)}, u32[]{:S(2)}) %collective-permute-start.7) | collective-permute-done | bytes 131104 | tf_op jit(solution)/shard_map/ppermute | solution.py:13
  22.3 2.5 convolution_bitcast_fusion.1
  24.8 244.8 %while.12 = (s32[]{:T(128)}, f32[64,1024]{1,0:T(8,128)S(1)}, f32[64,1024]{1,0:T(8,128)S(1)}, s32[8,8]{1,0:T(8,128)S(1)}, bf16[8,8,128,128]{3,2,1,0:T(8,128)(2,1)}, /*index=5*/s32[]{:T(128)}) while((s32[]{:T(128)}, f32[64,1024]{1,0:T(8,128)S(1)}, f32[64,1024]{1,0:T(8,128)S(1)}, s32[8,8]{1,0:T(8,128)S(1)}, bf16[8,8,128,128]{3,2,1,0:T(8,128)(2,1)}, ...), condition=%wide.region_1.3_spmd, body=%wide.region_0.0_spmd.sunk | while | flops 135005760 | bytes 12589157 | solution.py:58
  24.9 3.0 collective-permute-start
  29.8 3.6 collective-permute-start.2
  33.5 2.8 collective-permute-start.3
  36.5 8.0 %collective-permute-done.3 = bf16[64,1024]{1,0:T(8,128)(2,1)S(1)} collective-permute-done((bf16[64,1024]{1,0:T(8,128)(2,1)S(1)}, bf16[64,1024]{1,0:T(8,128)(2,1)S(1)}, u32[]{:S(2)}, u32[]{:S(2)}) %collective-permute-start.3) | collective-permute-done | bytes 131104 | tf_op jit(solution)/shard_map/while/body/eval_jaxpr/ppermute | solution.py:13
  45.5 2.5 fusion.102
  52.0 3.6 collective-permute-start.2
  55.6 3.9 collective-permute-start.3
  59.8 6.9 %collective-permute-done.3 = bf16[64,1024]{1,0:T(8,128)(2,1)S(1)} collective-permute-done((bf16[64,1024]{1,0:T(8,128)(2,1)S(1)}, bf16[64,1024]{1,0:T(8,128)(2,1)S(1)}, u32[]{:S(2)}, u32[]{:S(2)}) %collective-permute-start.3) | collective-permute-done | bytes 131104 | tf_op jit(solution)/shard_map/while/body/eval_jaxpr/ppermute | solution.py:13
  67.7 2.5 fusion.102
  74.2 3.6 collective-permute-start.2
  77.8 3.9 collective-permute-start.3
  82.0 6.9 %collective-permute-done.3 = bf16[64,1024]{1,0:T(8,128)(2,1)S(1)} collective-permute-done((bf16[64,1024]{1,0:T(8,128)(2,1)S(1)}, bf16[64,1024]{1,0:T(8,128)(2,1)S(1)}, u32[]{:S(2)}, u32[]{:S(2)}) %collective-permute-start.3) | collective-permute-done | bytes 131104 | tf_op jit(solution)/shard_map/while/body/eval_jaxpr/ppermute | solution.py:13
  96.3 3.6 collective-permute-start.2
  100.0 3.9 collective-permute-start.3
  104.1 6.9 %collective-permute-done.3 = bf16[64,1024]{1,0:T(8,128)(2,1)S(1)} collective-permute-done((bf16[64,1024]{1,0:T(8,128)(2,1)S(1)}, bf16[64,1024]{1,0:T(8,128)(2,1)S(1)}, u32[]{:S(2)}, u32[]{:S(2)}) %collective-permute-start.3) | collective-permute-done | bytes 131104 | tf_op jit(solution)/shard_map/while/body/eval_jaxpr/ppermute | solution.py:13
  112.0 2.5 fusion.102
  118.5 3.6 collective-permute-start.2
  122.1 3.9 collective-permute-start.3
  126.3 6.9 %collective-permute-done.3 = bf16[64,1024]{1,0:T(8,128)(2,1)S(1)} collective-permute-done((bf16[64,1024]{1,0:T(8,128)(2,1)S(1)}, bf16[64,1024]{1,0:T(8,128)(2,1)S(1)}, u32[]{:S(2)}, u32[]{:S(2)}) %collective-permute-start.3) | collective-permute-done | bytes 131104 | tf_op jit(solution)/shard_map/while/body/eval_jaxpr/ppermute | solution.py:13
  134.1 2.5 fusion.102
  140.6 3.6 collective-permute-start.2
  144.3 3.9 collective-permute-start.3
  148.4 6.9 %collective-permute-done.3 = bf16[64,1024]{1,0:T(8,128)(2,1)S(1)} collective-permute-done((bf16[64,1024]{1,0:T(8,128)(2,1)S(1)}, bf16[64,1024]{1,0:T(8,128)(2,1)S(1)}, u32[]{:S(2)}, u32[]{:S(2)}) %collective-permute-start.3) | collective-permute-done | bytes 131104 | tf_op jit(solution)/shard_map/while/body/eval_jaxpr/ppermute | solution.py:13
  156.3 2.5 fusion.102
  162.8 3.6 collective-permute-start.2
  166.4 3.9 collective-permute-start.3
  170.6 6.9 %collective-permute-done.3 = bf16[64,1024]{1,0:T(8,128)(2,1)S(1)} collective-permute-done((bf16[64,1024]{1,0:T(8,128)(2,1)S(1)}, bf16[64,1024]{1,0:T(8,128)(2,1)S(1)}, u32[]{:S(2)}, u32[]{:S(2)}) %collective-permute-start.3) | collective-permute-done | bytes 131104 | tf_op jit(solution)/shard_map/while/body/eval_jaxpr/ppermute | solution.py:13
  178.5 2.5 fusion.102
  184.9 3.6 collective-permute-start.2
  188.6 3.9 collective-permute-start.3
  192.7 6.9 %collective-permute-done.3 = bf16[64,1024]{1,0:T(8,128)(2,1)S(1)} collective-permute-done((bf16[64,1024]{1,0:T(8,128)(2,1)S(1)}, bf16[64,1024]{1,0:T(8,128)(2,1)S(1)}, u32[]{:S(2)}, u32[]{:S(2)}) %collective-permute-start.3) | collective-permute-done | bytes 131104 | tf_op jit(solution)/shard_map/while/body/eval_jaxpr/ppermute | solution.py:13
  207.1 3.6 collective-permute-start.2
  210.7 3.9 collective-permute-start.3
  214.9 6.9 %collective-permute-done.3 = bf16[64,1024]{1,0:T(8,128)(2,1)S(1)} collective-permute-done((bf16[64,1024]{1,0:T(8,128)(2,1)S(1)}, bf16[64,1024]{1,0:T(8,128)(2,1)S(1)}, u32[]{:S(2)}, u32[]{:S(2)}) %collective-permute-start.3) | collective-permute-done | bytes 131104 | tf_op jit(solution)/shard_map/while/body/eval_jaxpr/ppermute | solution.py:13
  229.2 3.6 collective-permute-start.2
  232.9 3.9 collective-permute-start.3
  237.0 6.9 %collective-permute-done.3 = bf16[64,1024]{1,0:T(8,128)(2,1)S(1)} collective-permute-done((bf16[64,1024]{1,0:T(8,128)(2,1)S(1)}, bf16[64,1024]{1,0:T(8,128)(2,1)S(1)}, u32[]{:S(2)}, u32[]{:S(2)}) %collective-permute-start.3) | collective-permute-done | bytes 131104 | tf_op jit(solution)/shard_map/while/body/eval_jaxpr/ppermute | solution.py:13
  251.4 3.6 collective-permute-start.2
  255.0 3.9 collective-permute-start.3
  259.2 6.9 %collective-permute-done.3 = bf16[64,1024]{1,0:T(8,128)(2,1)S(1)} collective-permute-done((bf16[64,1024]{1,0:T(8,128)(2,1)S(1)}, bf16[64,1024]{1,0:T(8,128)(2,1)S(1)}, u32[]{:S(2)}, u32[]{:S(2)}) %collective-permute-start.3) | collective-permute-done | bytes 131104 | tf_op jit(solution)/shard_map/while/body/eval_jaxpr/ppermute | solution.py:13
  270.1 5.8 %cholesky.164 = f32[64,64]{1,0:T(8,128)S(1)} custom-call(f32[64,64]{1,0:T(8,128)S(1)} %fusion.22), custom_call_target="Cholesky" | custom-call | tf_op jit(solution)/shard_map/jit(cholesky)/cholesky | solution.py:70
  280.7 5.8 %cholesky.175 = f32[64,64]{1,0:T(8,128)S(1)} custom-call(f32[64,64]{1,0:T(8,128)S(1)} %fusion.21), custom_call_target="Cholesky" | custom-call | tf_op jit(solution)/shard_map/jit(cholesky)/cholesky | solution.py:75
  290.0 3.7 collective-permute-done.9
  294.0 5.8 %cholesky.186 = f32[64,64]{1,0:T(8,128)S(1)} custom-call(f32[64,64]{1,0:T(8,128)S(1)} %fusion.20), custom_call_target="Cholesky" | custom-call | tf_op jit(solution)/shard_map/jit(cholesky)/cholesky | solution.py:75
  303.3 4.6 %collective-permute-done.10 = f32[64,64]{1,0:T(8,128)S(1)} collective-permute-done((f32[64,64]{1,0:T(8,128)S(1)}, f32[64,64]{1,0:T(8,128)S(1)}, u32[]{:S(2)}, u32[]{:S(2)}) %collective-permute-start.10) | collective-permute-done | bytes 16416 | tf_op jit(solution)/shard_map/ppermute | solution.py:23
  308.2 5.8 %cholesky.197 = f32[64,64]{1,0:T(8,128)S(1)} custom-call(f32[64,64]{1,0:T(8,128)S(1)} %fusion.19), custom_call_target="Cholesky" | custom-call | tf_op jit(solution)/shard_map/jit(cholesky)/cholesky | solution.py:75
  317.5 7.6 %collective-permute-done.11 = f32[64,64]{1,0:T(8,128)S(1)} collective-permute-done((f32[64,64]{1,0:T(8,128)S(1)}, f32[64,64]{1,0:T(8,128)S(1)}, u32[]{:S(2)}, u32[]{:S(2)}) %collective-permute-start.11) | collective-permute-done | bytes 16416 | tf_op jit(solution)/shard_map/ppermute | solution.py:23
  325.4 5.8 %cholesky.208 = f32[64,64]{1,0:T(8,128)S(1)} custom-call(f32[64,64]{1,0:T(8,128)S(1)} %fusion.18), custom_call_target="Cholesky" | custom-call | tf_op jit(solution)/shard_map/jit(cholesky)/cholesky | solution.py:75
  334.7 3.7 collective-permute-done.12
  338.6 5.8 %cholesky.219 = f32[64,64]{1,0:T(8,128)S(1)} custom-call(f32[64,64]{1,0:T(8,128)S(1)} %fusion.17), custom_call_target="Cholesky" | custom-call | tf_op jit(solution)/shard_map/jit(cholesky)/cholesky | solution.py:75
  348.1 5.0 %collective-permute-done.13 = f32[64,64]{1,0:T(8,128)S(1)} collective-permute-done((f32[64,64]{1,0:T(8,128)S(1)}, f32[64,64]{1,0:T(8,128)S(1)}, u32[]{:S(2)}, u32[]{:S(2)}) %collective-permute-start.13) | collective-permute-done | bytes 16416 | tf_op jit(solution)/shard_map/ppermute | solution.py:23
  353.4 5.8 %cholesky.230 = f32[64,64]{1,0:T(8,128)S(1)} custom-call(f32[64,64]{1,0:T(8,128)S(1)} %fusion.16), custom_call_target="Cholesky" | custom-call | tf_op jit(solution)/shard_map/jit(cholesky)/cholesky | solution.py:75
  360.6 4.3 collective-permute-start.14
  367.1 5.8 %cholesky.241 = f32[64,64]{1,0:T(8,128)S(1)} custom-call(f32[64,64]{1,0:T(8,128)S(1)} %fusion.15), custom_call_target="Cholesky" | custom-call | tf_op jit(solution)/shard_map/jit(cholesky)/cholesky | solution.py:75
  374.3 21.8 %collective-permute-start.15 = (f32[64,64]{1,0:T(8,128)S(1)}, f32[64,64]{1,0:T(8,128)S(1)}, u32[]{:S(2)}, u32[]{:S(2)}) collective-permute-start(f32[64,64]{1,0:T(8,128)S(1)} %select_select_fusion.2), channel_id=1, source_target_pairs={{0,128},{128,0},{1,129},{129,1},{2,130},{130,2},{3,131},{131,3},{4... | collective-permute-start | bytes 49160 | tf_op jit(solution)/shard_map/ppermute | solution.py:23
  398.3 5.8 %cholesky.252 = f32[64,64]{1,0:T(8,128)S(1)} custom-call(f32[64,64]{1,0:T(8,128)S(1)} %fusion.14), custom_call_target="Cholesky" | custom-call | tf_op jit(solution)/shard_map/jit(cholesky)/cholesky | solution.py:75
  407.6 8.0 %collective-permute-done.16 = f32[64,64]{1,0:T(8,128)S(1)} collective-permute-done((f32[64,64]{1,0:T(8,128)S(1)}, f32[64,64]{1,0:T(8,128)S(1)}, u32[]{:S(2)}, u32[]{:S(2)}) %collective-permute-start.16) | collective-permute-done | bytes 16416 | tf_op jit(solution)/shard_map/ppermute | solution.py:23
  415.8 5.8 %cholesky.263 = f32[64,64]{1,0:T(8,128)S(1)} custom-call(f32[64,64]{1,0:T(8,128)S(1)} %fusion.13), custom_call_target="Cholesky" | custom-call | tf_op jit(solution)/shard_map/jit(cholesky)/cholesky | solution.py:75
  423.0 4.9 %custom-call.5 = f32[1,64,64]{1,2,0:T(8,128)S(1)} custom-call(f32[1,64,64]{2,1,0:T(8,128)S(1)} %get-tuple-element.53), custom_call_target="InvertDiagBlocksLowerTriangular" | custom-call | tf_op jit(solution)/shard_map/triangular_solve | solution.py:76
  (322 shorter events, 110.5 us)
Async XLA Ops:
  0.6 12.2 %collective-permute-start.4 = (bf16[64,1024]{1,0:T(8,128)(2,1)}, bf16[64,1024]{1,0:T(8,128)(2,1)S(1)}, u32[]{:S(2)}, u32[]{:S(2)}) collective-permute-start(bf16[64,1024]{1,0:T(8,128)(2,1)} %param.8), channel_id=1, source_target_pairs={{0,2},{1,3},{2,4},{3,5},{4,6},{5,7},{6,8},{7,9},{8,10},{9,11},{10,... | collective-permute-start | bytes 393224 | tf_op jit(solution)/shard_map/ppermute | solution.py:13
  4.0 8.9 %collective-permute-start.5 = (bf16[64,1024]{1,0:T(8,128)(2,1)}, bf16[64,1024]{1,0:T(8,128)(2,1)S(1)}, u32[]{:S(2)}, u32[]{:S(2)}) collective-permute-start(bf16[64,1024]{1,0:T(8,128)(2,1)} %param.8), channel_id=1, source_target_pairs={{0,1},{1,2},{2,3},{3,4},{4,5},{5,6},{6,7},{7,8},{8,9},{9,10},{10,1... | collective-permute-start | bytes 393224 | tf_op jit(solution)/shard_map/ppermute | solution.py:13
  6.0 8.0 %collective-permute-start.6 = (bf16[64,1024]{1,0:T(8,128)(2,1)}, bf16[64,1024]{1,0:T(8,128)(2,1)S(1)}, u32[]{:S(2)}, u32[]{:S(2)}) collective-permute-start(bf16[64,1024]{1,0:T(8,128)(2,1)} %param.8), channel_id=1, source_target_pairs={{1,0},{2,1},{3,2},{4,3},{5,4},{6,5},{7,6},{8,7},{9,8},{10,9},{11,1... | collective-permute-start | bytes 393224 | tf_op jit(solution)/shard_map/ppermute | solution.py:13
  9.6 11.7 %collective-permute-start.7 = (bf16[64,1024]{1,0:T(8,128)(2,1)}, bf16[64,1024]{1,0:T(8,128)(2,1)S(1)}, u32[]{:S(2)}, u32[]{:S(2)}) collective-permute-start(bf16[64,1024]{1,0:T(8,128)(2,1)} %param.8), channel_id=1, source_target_pairs={{2,0},{3,1},{4,2},{5,3},{6,4},{7,5},{8,6},{9,7},{10,8},{11,9},{12,... | collective-permute-start | bytes 393224 | tf_op jit(solution)/shard_map/ppermute | solution.py:13
  24.9 11.6 %collective-permute-start = (bf16[64,1024]{1,0:T(8,128)(2,1)S(1)}, bf16[64,1024]{1,0:T(8,128)(2,1)S(1)}, u32[]{:S(2)}, u32[]{:S(2)}) collective-permute-start(bf16[64,1024]{1,0:T(8,128)(2,1)S(1)} %convert_element_type.12), channel_id=1, source_target_pairs={{0,2},{1,3},{2,4},{3,5},{4,6},{5,7},{6,8},{7,9},{8,10},{9,11},{10,... | collective-permute-start | bytes 393224 | tf_op jit(solution)/shard_map/while/body/eval_jaxpr/ppermute | solution.py:13
  27.9 8.5 %collective-permute-start.1 = (bf16[64,1024]{1,0:T(8,128)(2,1)S(1)}, bf16[64,1024]{1,0:T(8,128)(2,1)S(1)}, u32[]{:S(2)}, u32[]{:S(2)}) collective-permute-start(bf16[64,1024]{1,0:T(8,128)(2,1)S(1)} %convert_element_type.12), channel_id=1, source_target_pairs={{0,1},{1,2},{2,3},{3,4},{4,5},{5,6},{6,7},{7,8},{8,9},{9,10},{10,1... | collective-permute-start | bytes 393224 | tf_op jit(solution)/shard_map/while/body/eval_jaxpr/ppermute | solution.py:13
  29.8 6.7 %collective-permute-start.2 = (bf16[64,1024]{1,0:T(8,128)(2,1)S(1)}, bf16[64,1024]{1,0:T(8,128)(2,1)S(1)}, u32[]{:S(2)}, u32[]{:S(2)}) collective-permute-start(bf16[64,1024]{1,0:T(8,128)(2,1)S(1)} %convert_element_type.12), channel_id=1, source_target_pairs={{1,0},{2,1},{3,2},{4,3},{5,4},{6,5},{7,6},{8,7},{9,8},{10,9},{11,1... | collective-permute-start | bytes 393224 | tf_op jit(solution)/shard_map/while/body/eval_jaxpr/ppermute | solution.py:13
  33.5 11.1 %collective-permute-start.3 = (bf16[64,1024]{1,0:T(8,128)(2,1)S(1)}, bf16[64,1024]{1,0:T(8,128)(2,1)S(1)}, u32[]{:S(2)}, u32[]{:S(2)}) collective-permute-start(bf16[64,1024]{1,0:T(8,128)(2,1)S(1)} %convert_element_type.12), channel_id=1, source_target_pairs={{2,0},{3,1},{4,2},{5,3},{6,4},{7,5},{8,6},{9,7},{10,8},{11,9},{12,... | collective-permute-start | bytes 393224 | tf_op jit(solution)/shard_map/while/body/eval_jaxpr/ppermute | solution.py:13
  48.1 11.6 %collective-permute-start = (bf16[64,1024]{1,0:T(8,128)(2,1)S(1)}, bf16[64,1024]{1,0:T(8,128)(2,1)S(1)}, u32[]{:S(2)}, u32[]{:S(2)}) collective-permute-start(bf16[64,1024]{1,0:T(8,128)(2,1)S(1)} %convert_element_type.12), channel_id=1, source_target_pairs={{0,2},{1,3},{2,4},{3,5},{4,6},{5,7},{6,8},{7,9},{8,10},{9,11},{10,... | collective-permute-start | bytes 393224 | tf_op jit(solution)/shard_map/while/body/eval_jaxpr/ppermute | solution.py:13
  50.1 9.7 %collective-permute-start.1 = (bf16[64,1024]{1,0:T(8,128)(2,1)S(1)}, bf16[64,1024]{1,0:T(8,128)(2,1)S(1)}, u32[]{:S(2)}, u32[]{:S(2)}) collective-permute-start(bf16[64,1024]{1,0:T(8,128)(2,1)S(1)} %convert_element_type.12), channel_id=1, source_target_pairs={{0,1},{1,2},{2,3},{3,4},{4,5},{5,6},{6,7},{7,8},{8,9},{9,10},{10,1... | collective-permute-start | bytes 393224 | tf_op jit(solution)/shard_map/while/body/eval_jaxpr/ppermute | solution.py:13
  52.0 7.8 %collective-permute-start.2 = (bf16[64,1024]{1,0:T(8,128)(2,1)S(1)}, bf16[64,1024]{1,0:T(8,128)(2,1)S(1)}, u32[]{:S(2)}, u32[]{:S(2)}) collective-permute-start(bf16[64,1024]{1,0:T(8,128)(2,1)S(1)} %convert_element_type.12), channel_id=1, source_target_pairs={{1,0},{2,1},{3,2},{4,3},{5,4},{6,5},{7,6},{8,7},{9,8},{10,9},{11,1... | collective-permute-start | bytes 393224 | tf_op jit(solution)/shard_map/while/body/eval_jaxpr/ppermute | solution.py:13
  55.6 11.1 %collective-permute-start.3 = (bf16[64,1024]{1,0:T(8,128)(2,1)S(1)}, bf16[64,1024]{1,0:T(8,128)(2,1)S(1)}, u32[]{:S(2)}, u32[]{:S(2)}) collective-permute-start(bf16[64,1024]{1,0:T(8,128)(2,1)S(1)} %convert_element_type.12), channel_id=1, source_target_pairs={{2,0},{3,1},{4,2},{5,3},{6,4},{7,5},{8,6},{9,7},{10,8},{11,9},{12,... | collective-permute-start | bytes 393224 | tf_op jit(solution)/shard_map/while/body/eval_jaxpr/ppermute | solution.py:13
  70.3 11.6 %collective-permute-start = (bf16[64,1024]{1,0:T(8,128)(2,1)S(1)}, bf16[64,1024]{1,0:T(8,128)(2,1)S(1)}, u32[]{:S(2)}, u32[]{:S(2)}) collective-permute-start(bf16[64,1024]{1,0:T(8,128)(2,1)S(1)} %convert_element_type.12), channel_id=1, source_target_pairs={{0,2},{1,3},{2,4},{3,5},{4,6},{5,7},{6,8},{7,9},{8,10},{9,11},{10,... | collective-permute-start | bytes 393224 | tf_op jit(solution)/shard_map/while/body/eval_jaxpr/ppermute | solution.py:13
  72.2 9.7 %collective-permute-start.1 = (bf16[64,1024]{1,0:T(8,128)(2,1)S(1)}, bf16[64,1024]{1,0:T(8,128)(2,1)S(1)}, u32[]{:S(2)}, u32[]{:S(2)}) collective-permute-start(bf16[64,1024]{1,0:T(8,128)(2,1)S(1)} %convert_element_type.12), channel_id=1, source_target_pairs={{0,1},{1,2},{2,3},{3,4},{4,5},{5,6},{6,7},{7,8},{8,9},{9,10},{10,1... | collective-permute-start | bytes 393224 | tf_op jit(solution)/shard_map/while/body/eval_jaxpr/ppermute | solution.py:13
  74.2 7.8 %collective-permute-start.2 = (bf16[64,1024]{1,0:T(8,128)(2,1)S(1)}, bf16[64,1024]{1,0:T(8,128)(2,1)S(1)}, u32[]{:S(2)}, u32[]{:S(2)}) collective-permute-start(bf16[64,1024]{1,0:T(8,128)(2,1)S(1)} %convert_element_type.12), channel_id=1, source_target_pairs={{1,0},{2,1},{3,2},{4,3},{5,4},{6,5},{7,6},{8,7},{9,8},{10,9},{11,1... | collective-permute-start | bytes 393224 | tf_op jit(solution)/shard_map/while/body/eval_jaxpr/ppermute | solution.py:13
  77.8 11.1 %collective-permute-start.3 = (bf16[64,1024]{1,0:T(8,128)(2,1)S(1)}, bf16[64,1024]{1,0:T(8,128)(2,1)S(1)}, u32[]{:S(2)}, u32[]{:S(2)}) collective-permute-start(bf16[64,1024]{1,0:T(8,128)(2,1)S(1)} %convert_element_type.12), channel_id=1, source_target_pairs={{2,0},{3,1},{4,2},{5,3},{6,4},{7,5},{8,6},{9,7},{10,8},{11,9},{12,... | collective-permute-start | bytes 393224 | tf_op jit(solution)/shard_map/while/body/eval_jaxpr/ppermute | solution.py:13
  92.5 11.6 %collective-permute-start = (bf16[64,1024]{1,0:T(8,128)(2,1)S(1)}, bf16[64,1024]{1,0:T(8,128)(2,1)S(1)}, u32[]{:S(2)}, u32[]{:S(2)}) collective-permute-start(bf16[64,1024]{1,0:T(8,128)(2,1)S(1)} %convert_element_type.12), channel_id=1, source_target_pairs={{0,2},{1,3},{2,4},{3,5},{4,6},{5,7},{6,8},{7,9},{8,10},{9,11},{10,... | collective-permute-start | bytes 393224 | tf_op jit(solution)/shard_map/while/body/eval_jaxpr/ppermute | solution.py:13
  94.4 9.7 %collective-permute-start.1 = (bf16[64,1024]{1,0:T(8,128)(2,1)S(1)}, bf16[64,1024]{1,0:T(8,128)(2,1)S(1)}, u32[]{:S(2)}, u32[]{:S(2)}) collective-permute-start(bf16[64,1024]{1,0:T(8,128)(2,1)S(1)} %convert_element_type.12), channel_id=1, source_target_pairs={{0,1},{1,2},{2,3},{3,4},{4,5},{5,6},{6,7},{7,8},{8,9},{9,10},{10,1... | collective-permute-start | bytes 393224 | tf_op jit(solution)/shard_map/while/body/eval_jaxpr/ppermute | solution.py:13
  96.3 7.8 %collective-permute-start.2 = (bf16[64,1024]{1,0:T(8,128)(2,1)S(1)}, bf16[64,1024]{1,0:T(8,128)(2,1)S(1)}, u32[]{:S(2)}, u32[]{:S(2)}) collective-permute-start(bf16[64,1024]{1,0:T(8,128)(2,1)S(1)} %convert_element_type.12), channel_id=1, source_target_pairs={{1,0},{2,1},{3,2},{4,3},{5,4},{6,5},{7,6},{8,7},{9,8},{10,9},{11,1... | collective-permute-start | bytes 393224 | tf_op jit(solution)/shard_map/while/body/eval_jaxpr/ppermute | solution.py:13
  100.0 11.1 %collective-permute-start.3 = (bf16[64,1024]{1,0:T(8,128)(2,1)S(1)}, bf16[64,1024]{1,0:T(8,128)(2,1)S(1)}, u32[]{:S(2)}, u32[]{:S(2)}) collective-permute-start(bf16[64,1024]{1,0:T(8,128)(2,1)S(1)} %convert_element_type.12), channel_id=1, source_target_pairs={{2,0},{3,1},{4,2},{5,3},{6,4},{7,5},{8,6},{9,7},{10,8},{11,9},{12,... | collective-permute-start | bytes 393224 | tf_op jit(solution)/shard_map/while/body/eval_jaxpr/ppermute | solution.py:13
  114.6 11.6 %collective-permute-start = (bf16[64,1024]{1,0:T(8,128)(2,1)S(1)}, bf16[64,1024]{1,0:T(8,128)(2,1)S(1)}, u32[]{:S(2)}, u32[]{:S(2)}) collective-permute-start(bf16[64,1024]{1,0:T(8,128)(2,1)S(1)} %convert_element_type.12), channel_id=1, source_target_pairs={{0,2},{1,3},{2,4},{3,5},{4,6},{5,7},{6,8},{7,9},{8,10},{9,11},{10,... | collective-permute-start | bytes 393224 | tf_op jit(solution)/shard_map/while/body/eval_jaxpr/ppermute | solution.py:13
  116.5 9.7 %collective-permute-start.1 = (bf16[64,1024]{1,0:T(8,128)(2,1)S(1)}, bf16[64,1024]{1,0:T(8,128)(2,1)S(1)}, u32[]{:S(2)}, u32[]{:S(2)}) collective-permute-start(bf16[64,1024]{1,0:T(8,128)(2,1)S(1)} %convert_element_type.12), channel_id=1, source_target_pairs={{0,1},{1,2},{2,3},{3,4},{4,5},{5,6},{6,7},{7,8},{8,9},{9,10},{10,1... | collective-permute-start | bytes 393224 | tf_op jit(solution)/shard_map/while/body/eval_jaxpr/ppermute | solution.py:13
  118.5 7.8 %collective-permute-start.2 = (bf16[64,1024]{1,0:T(8,128)(2,1)S(1)}, bf16[64,1024]{1,0:T(8,128)(2,1)S(1)}, u32[]{:S(2)}, u32[]{:S(2)}) collective-permute-start(bf16[64,1024]{1,0:T(8,128)(2,1)S(1)} %convert_element_type.12), channel_id=1, source_target_pairs={{1,0},{2,1},{3,2},{4,3},{5,4},{6,5},{7,6},{8,7},{9,8},{10,9},{11,1... | collective-permute-start | bytes 393224 | tf_op jit(solution)/shard_map/while/body/eval_jaxpr/ppermute | solution.py:13
  122.1 11.1 %collective-permute-start.3 = (bf16[64,1024]{1,0:T(8,128)(2,1)S(1)}, bf16[64,1024]{1,0:T(8,128)(2,1)S(1)}, u32[]{:S(2)}, u32[]{:S(2)}) collective-permute-start(bf16[64,1024]{1,0:T(8,128)(2,1)S(1)} %convert_element_type.12), channel_id=1, source_target_pairs={{2,0},{3,1},{4,2},{5,3},{6,4},{7,5},{8,6},{9,7},{10,8},{11,9},{12,... | collective-permute-start | bytes 393224 | tf_op jit(solution)/shard_map/while/body/eval_jaxpr/ppermute | solution.py:13
  136.8 11.6 %collective-permute-start = (bf16[64,1024]{1,0:T(8,128)(2,1)S(1)}, bf16[64,1024]{1,0:T(8,128)(2,1)S(1)}, u32[]{:S(2)}, u32[]{:S(2)}) collective-permute-start(bf16[64,1024]{1,0:T(8,128)(2,1)S(1)} %convert_element_type.12), channel_id=1, source_target_pairs={{0,2},{1,3},{2,4},{3,5},{4,6},{5,7},{6,8},{7,9},{8,10},{9,11},{10,... | collective-permute-start | bytes 393224 | tf_op jit(solution)/shard_map/while/body/eval_jaxpr/ppermute | solution.py:13
  138.7 9.7 %collective-permute-start.1 = (bf16[64,1024]{1,0:T(8,128)(2,1)S(1)}, bf16[64,1024]{1,0:T(8,128)(2,1)S(1)}, u32[]{:S(2)}, u32[]{:S(2)}) collective-permute-start(bf16[64,1024]{1,0:T(8,128)(2,1)S(1)} %convert_element_type.12), channel_id=1, source_target_pairs={{0,1},{1,2},{2,3},{3,4},{4,5},{5,6},{6,7},{7,8},{8,9},{9,10},{10,1... | collective-permute-start | bytes 393224 | tf_op jit(solution)/shard_map/while/body/eval_jaxpr/ppermute | solution.py:13
  140.6 7.8 %collective-permute-start.2 = (bf16[64,1024]{1,0:T(8,128)(2,1)S(1)}, bf16[64,1024]{1,0:T(8,128)(2,1)S(1)}, u32[]{:S(2)}, u32[]{:S(2)}) collective-permute-start(bf16[64,1024]{1,0:T(8,128)(2,1)S(1)} %convert_element_type.12), channel_id=1, source_target_pairs={{1,0},{2,1},{3,2},{4,3},{5,4},{6,5},{7,6},{8,7},{9,8},{10,9},{11,1... | collective-permute-start | bytes 393224 | tf_op jit(solution)/shard_map/while/body/eval_jaxpr/ppermute | solution.py:13
  144.3 11.1 %collective-permute-start.3 = (bf16[64,1024]{1,0:T(8,128)(2,1)S(1)}, bf16[64,1024]{1,0:T(8,128)(2,1)S(1)}, u32[]{:S(2)}, u32[]{:S(2)}) collective-permute-start(bf16[64,1024]{1,0:T(8,128)(2,1)S(1)} %convert_element_type.12), channel_id=1, source_target_pairs={{2,0},{3,1},{4,2},{5,3},{6,4},{7,5},{8,6},{9,7},{10,8},{11,9},{12,... | collective-permute-start | bytes 393224 | tf_op jit(solution)/shard_map/while/body/eval_jaxpr/ppermute | solution.py:13
  158.9 11.6 %collective-permute-start = (bf16[64,1024]{1,0:T(8,128)(2,1)S(1)}, bf16[64,1024]{1,0:T(8,128)(2,1)S(1)}, u32[]{:S(2)}, u32[]{:S(2)}) collective-permute-start(bf16[64,1024]{1,0:T(8,128)(2,1)S(1)} %convert_element_type.12), channel_id=1, source_target_pairs={{0,2},{1,3},{2,4},{3,5},{4,6},{5,7},{6,8},{7,9},{8,10},{9,11},{10,... | collective-permute-start | bytes 393224 | tf_op jit(solution)/shard_map/while/body/eval_jaxpr/ppermute | solution.py:13
  160.8 9.7 %collective-permute-start.1 = (bf16[64,1024]{1,0:T(8,128)(2,1)S(1)}, bf16[64,1024]{1,0:T(8,128)(2,1)S(1)}, u32[]{:S(2)}, u32[]{:S(2)}) collective-permute-start(bf16[64,1024]{1,0:T(8,128)(2,1)S(1)} %convert_element_type.12), channel_id=1, source_target_pairs={{0,1},{1,2},{2,3},{3,4},{4,5},{5,6},{6,7},{7,8},{8,9},{9,10},{10,1... | collective-permute-start | bytes 393224 | tf_op jit(solution)/shard_map/while/body/eval_jaxpr/ppermute | solution.py:13
  162.8 7.8 %collective-permute-start.2 = (bf16[64,1024]{1,0:T(8,128)(2,1)S(1)}, bf16[64,1024]{1,0:T(8,128)(2,1)S(1)}, u32[]{:S(2)}, u32[]{:S(2)}) collective-permute-start(bf16[64,1024]{1,0:T(8,128)(2,1)S(1)} %convert_element_type.12), channel_id=1, source_target_pairs={{1,0},{2,1},{3,2},{4,3},{5,4},{6,5},{7,6},{8,7},{9,8},{10,9},{11,1... | collective-permute-start | bytes 393224 | tf_op jit(solution)/shard_map/while/body/eval_jaxpr/ppermute | solution.py:13
  166.4 11.1 %collective-permute-start.3 = (bf16[64,1024]{1,0:T(8,128)(2,1)S(1)}, bf16[64,1024]{1,0:T(8,128)(2,1)S(1)}, u32[]{:S(2)}, u32[]{:S(2)}) collective-permute-start(bf16[64,1024]{1,0:T(8,128)(2,1)S(1)} %convert_element_type.12), channel_id=1, source_target_pairs={{2,0},{3,1},{4,2},{5,3},{6,4},{7,5},{8,6},{9,7},{10,8},{11,9},{12,... | collective-permute-start | bytes 393224 | tf_op jit(solution)/shard_map/while/body/eval_jaxpr/ppermute | solution.py:13
  181.1 11.6 %collective-permute-start = (bf16[64,1024]{1,0:T(8,128)(2,1)S(1)}, bf16[64,1024]{1,0:T(8,128)(2,1)S(1)}, u32[]{:S(2)}, u32[]{:S(2)}) collective-permute-start(bf16[64,1024]{1,0:T(8,128)(2,1)S(1)} %convert_element_type.12), channel_id=1, source_target_pairs={{0,2},{1,3},{2,4},{3,5},{4,6},{5,7},{6,8},{7,9},{8,10},{9,11},{10,... | collective-permute-start | bytes 393224 | tf_op jit(solution)/shard_map/while/body/eval_jaxpr/ppermute | solution.py:13
  183.0 9.7 %collective-permute-start.1 = (bf16[64,1024]{1,0:T(8,128)(2,1)S(1)}, bf16[64,1024]{1,0:T(8,128)(2,1)S(1)}, u32[]{:S(2)}, u32[]{:S(2)}) collective-permute-start(bf16[64,1024]{1,0:T(8,128)(2,1)S(1)} %convert_element_type.12), channel_id=1, source_target_pairs={{0,1},{1,2},{2,3},{3,4},{4,5},{5,6},{6,7},{7,8},{8,9},{9,10},{10,1... | collective-permute-start | bytes 393224 | tf_op jit(solution)/shard_map/while/body/eval_jaxpr/ppermute | solution.py:13
  184.9 7.8 %collective-permute-start.2 = (bf16[64,1024]{1,0:T(8,128)(2,1)S(1)}, bf16[64,1024]{1,0:T(8,128)(2,1)S(1)}, u32[]{:S(2)}, u32[]{:S(2)}) collective-permute-start(bf16[64,1024]{1,0:T(8,128)(2,1)S(1)} %convert_element_type.12), channel_id=1, source_target_pairs={{1,0},{2,1},{3,2},{4,3},{5,4},{6,5},{7,6},{8,7},{9,8},{10,9},{11,1... | collective-permute-start | bytes 393224 | tf_op jit(solution)/shard_map/while/body/eval_jaxpr/ppermute | solution.py:13
  188.6 11.1 %collective-permute-start.3 = (bf16[64,1024]{1,0:T(8,128)(2,1)S(1)}, bf16[64,1024]{1,0:T(8,128)(2,1)S(1)}, u32[]{:S(2)}, u32[]{:S(2)}) collective-permute-start(bf16[64,1024]{1,0:T(8,128)(2,1)S(1)} %convert_element_type.12), channel_id=1, source_target_pairs={{2,0},{3,1},{4,2},{5,3},{6,4},{7,5},{8,6},{9,7},{10,8},{11,9},{12,... | collective-permute-start | bytes 393224 | tf_op jit(solution)/shard_map/while/body/eval_jaxpr/ppermute | solution.py:13
  203.2 11.6 %collective-permute-start = (bf16[64,1024]{1,0:T(8,128)(2,1)S(1)}, bf16[64,1024]{1,0:T(8,128)(2,1)S(1)}, u32[]{:S(2)}, u32[]{:S(2)}) collective-permute-start(bf16[64,1024]{1,0:T(8,128)(2,1)S(1)} %convert_element_type.12), channel_id=1, source_target_pairs={{0,2},{1,3},{2,4},{3,5},{4,6},{5,7},{6,8},{7,9},{8,10},{9,11},{10,... | collective-permute-start | bytes 393224 | tf_op jit(solution)/shard_map/while/body/eval_jaxpr/ppermute | solution.py:13
  205.2 9.7 %collective-permute-start.1 = (bf16[64,1024]{1,0:T(8,128)(2,1)S(1)}, bf16[64,1024]{1,0:T(8,128)(2,1)S(1)}, u32[]{:S(2)}, u32[]{:S(2)}) collective-permute-start(bf16[64,1024]{1,0:T(8,128)(2,1)S(1)} %convert_element_type.12), channel_id=1, source_target_pairs={{0,1},{1,2},{2,3},{3,4},{4,5},{5,6},{6,7},{7,8},{8,9},{9,10},{10,1... | collective-permute-start | bytes 393224 | tf_op jit(solution)/shard_map/while/body/eval_jaxpr/ppermute | solution.py:13
  207.1 7.8 %collective-permute-start.2 = (bf16[64,1024]{1,0:T(8,128)(2,1)S(1)}, bf16[64,1024]{1,0:T(8,128)(2,1)S(1)}, u32[]{:S(2)}, u32[]{:S(2)}) collective-permute-start(bf16[64,1024]{1,0:T(8,128)(2,1)S(1)} %convert_element_type.12), channel_id=1, source_target_pairs={{1,0},{2,1},{3,2},{4,3},{5,4},{6,5},{7,6},{8,7},{9,8},{10,9},{11,1... | collective-permute-start | bytes 393224 | tf_op jit(solution)/shard_map/while/body/eval_jaxpr/ppermute | solution.py:13
  210.7 11.1 %collective-permute-start.3 = (bf16[64,1024]{1,0:T(8,128)(2,1)S(1)}, bf16[64,1024]{1,0:T(8,128)(2,1)S(1)}, u32[]{:S(2)}, u32[]{:S(2)}) collective-permute-start(bf16[64,1024]{1,0:T(8,128)(2,1)S(1)} %convert_element_type.12), channel_id=1, source_target_pairs={{2,0},{3,1},{4,2},{5,3},{6,4},{7,5},{8,6},{9,7},{10,8},{11,9},{12,... | collective-permute-start | bytes 393224 | tf_op jit(solution)/shard_map/while/body/eval_jaxpr/ppermute | solution.py:13
  225.4 11.6 %collective-permute-start = (bf16[64,1024]{1,0:T(8,128)(2,1)S(1)}, bf16[64,1024]{1,0:T(8,128)(2,1)S(1)}, u32[]{:S(2)}, u32[]{:S(2)}) collective-permute-start(bf16[64,1024]{1,0:T(8,128)(2,1)S(1)} %convert_element_type.12), channel_id=1, source_target_pairs={{0,2},{1,3},{2,4},{3,5},{4,6},{5,7},{6,8},{7,9},{8,10},{9,11},{10,... | collective-permute-start | bytes 393224 | tf_op jit(solution)/shard_map/while/body/eval_jaxpr/ppermute | solution.py:13
  227.3 9.7 %collective-permute-start.1 = (bf16[64,1024]{1,0:T(8,128)(2,1)S(1)}, bf16[64,1024]{1,0:T(8,128)(2,1)S(1)}, u32[]{:S(2)}, u32[]{:S(2)}) collective-permute-start(bf16[64,1024]{1,0:T(8,128)(2,1)S(1)} %convert_element_type.12), channel_id=1, source_target_pairs={{0,1},{1,2},{2,3},{3,4},{4,5},{5,6},{6,7},{7,8},{8,9},{9,10},{10,1... | collective-permute-start | bytes 393224 | tf_op jit(solution)/shard_map/while/body/eval_jaxpr/ppermute | solution.py:13
  229.2 7.8 %collective-permute-start.2 = (bf16[64,1024]{1,0:T(8,128)(2,1)S(1)}, bf16[64,1024]{1,0:T(8,128)(2,1)S(1)}, u32[]{:S(2)}, u32[]{:S(2)}) collective-permute-start(bf16[64,1024]{1,0:T(8,128)(2,1)S(1)} %convert_element_type.12), channel_id=1, source_target_pairs={{1,0},{2,1},{3,2},{4,3},{5,4},{6,5},{7,6},{8,7},{9,8},{10,9},{11,1... | collective-permute-start | bytes 393224 | tf_op jit(solution)/shard_map/while/body/eval_jaxpr/ppermute | solution.py:13
  232.9 11.1 %collective-permute-start.3 = (bf16[64,1024]{1,0:T(8,128)(2,1)S(1)}, bf16[64,1024]{1,0:T(8,128)(2,1)S(1)}, u32[]{:S(2)}, u32[]{:S(2)}) collective-permute-start(bf16[64,1024]{1,0:T(8,128)(2,1)S(1)} %convert_element_type.12), channel_id=1, source_target_pairs={{2,0},{3,1},{4,2},{5,3},{6,4},{7,5},{8,6},{9,7},{10,8},{11,9},{12,... | collective-permute-start | bytes 393224 | tf_op jit(solution)/shard_map/while/body/eval_jaxpr/ppermute | solution.py:13
  247.5 11.6 %collective-permute-start = (bf16[64,1024]{1,0:T(8,128)(2,1)S(1)}, bf16[64,1024]{1,0:T(8,128)(2,1)S(1)}, u32[]{:S(2)}, u32[]{:S(2)}) collective-permute-start(bf16[64,1024]{1,0:T(8,128)(2,1)S(1)} %convert_element_type.12), channel_id=1, source_target_pairs={{0,2},{1,3},{2,4},{3,5},{4,6},{5,7},{6,8},{7,9},{8,10},{9,11},{10,... | collective-permute-start | bytes 393224 | tf_op jit(solution)/shard_map/while/body/eval_jaxpr/ppermute | solution.py:13
  249.5 9.7 %collective-permute-start.1 = (bf16[64,1024]{1,0:T(8,128)(2,1)S(1)}, bf16[64,1024]{1,0:T(8,128)(2,1)S(1)}, u32[]{:S(2)}, u32[]{:S(2)}) collective-permute-start(bf16[64,1024]{1,0:T(8,128)(2,1)S(1)} %convert_element_type.12), channel_id=1, source_target_pairs={{0,1},{1,2},{2,3},{3,4},{4,5},{5,6},{6,7},{7,8},{8,9},{9,10},{10,1... | collective-permute-start | bytes 393224 | tf_op jit(solution)/shard_map/while/body/eval_jaxpr/ppermute | solution.py:13
  251.4 7.8 %collective-permute-start.2 = (bf16[64,1024]{1,0:T(8,128)(2,1)S(1)}, bf16[64,1024]{1,0:T(8,128)(2,1)S(1)}, u32[]{:S(2)}, u32[]{:S(2)}) collective-permute-start(bf16[64,1024]{1,0:T(8,128)(2,1)S(1)} %convert_element_type.12), channel_id=1, source_target_pairs={{1,0},{2,1},{3,2},{4,3},{5,4},{6,5},{7,6},{8,7},{9,8},{10,9},{11,1... | collective-permute-start | bytes 393224 | tf_op jit(solution)/shard_map/while/body/eval_jaxpr/ppermute | solution.py:13
  255.0 11.1 %collective-permute-start.3 = (bf16[64,1024]{1,0:T(8,128)(2,1)S(1)}, bf16[64,1024]{1,0:T(8,128)(2,1)S(1)}, u32[]{:S(2)}, u32[]{:S(2)}) collective-permute-start(bf16[64,1024]{1,0:T(8,128)(2,1)S(1)} %convert_element_type.12), channel_id=1, source_target_pairs={{2,0},{3,1},{4,2},{5,3},{6,4},{7,5},{8,6},{9,7},{10,8},{11,9},{12,... | collective-permute-start | bytes 393224 | tf_op jit(solution)/shard_map/while/body/eval_jaxpr/ppermute | solution.py:13
  277.3 3.1 collective-permute-start.8
  287.9 5.8 %collective-permute-start.9 = (f32[64,64]{1,0:T(8,128)S(1)}, f32[64,64]{1,0:T(8,128)S(1)}, u32[]{:S(2)}, u32[]{:S(2)}) collective-permute-start(f32[64,64]{1,0:T(8,128)S(1)} %select_select_fusion.8), channel_id=1, source_target_pairs={{0,2},{2,0},{1,3},{3,1},{4,6},{6,4},{5,7},{7,5},{8,10},{10,8},{9,1... | collective-permute-start | bytes 49160 | tf_op jit(solution)/shard_map/ppermute | solution.py:23
  301.2 6.7 %collective-permute-start.10 = (f32[64,64]{1,0:T(8,128)S(1)}, f32[64,64]{1,0:T(8,128)S(1)}, u32[]{:S(2)}, u32[]{:S(2)}) collective-permute-start(f32[64,64]{1,0:T(8,128)S(1)} %select_select_fusion.7), channel_id=1, source_target_pairs={{0,4},{4,0},{1,5},{5,1},{2,6},{6,2},{3,7},{7,3},{8,12},{12,8},{9,1... | collective-permute-start | bytes 49160 | tf_op jit(solution)/shard_map/ppermute | solution.py:23
  315.4 9.7 %collective-permute-start.11 = (f32[64,64]{1,0:T(8,128)S(1)}, f32[64,64]{1,0:T(8,128)S(1)}, u32[]{:S(2)}, u32[]{:S(2)}) collective-permute-start(f32[64,64]{1,0:T(8,128)S(1)} %select_select_fusion.6), channel_id=1, source_target_pairs={{0,8},{8,0},{1,9},{9,1},{2,10},{10,2},{3,11},{11,3},{4,12},{12,4},... | collective-permute-start | bytes 49160 | tf_op jit(solution)/shard_map/ppermute | solution.py:23
  332.5 5.8 %collective-permute-start.12 = (f32[64,64]{1,0:T(8,128)S(1)}, f32[64,64]{1,0:T(8,128)S(1)}, u32[]{:S(2)}, u32[]{:S(2)}) collective-permute-start(f32[64,64]{1,0:T(8,128)S(1)} %select_select_fusion.5), channel_id=1, source_target_pairs={{0,16},{16,0},{1,17},{17,1},{2,18},{18,2},{3,19},{19,3},{4,20},{20... | collective-permute-start | bytes 49160 | tf_op jit(solution)/shard_map/ppermute | solution.py:23
  345.8 7.3 %collective-permute-start.13 = (f32[64,64]{1,0:T(8,128)S(1)}, f32[64,64]{1,0:T(8,128)S(1)}, u32[]{:S(2)}, u32[]{:S(2)}) collective-permute-start(f32[64,64]{1,0:T(8,128)S(1)} %select_select_fusion.4), channel_id=1, source_target_pairs={{0,32},{32,0},{1,33},{33,1},{2,34},{34,2},{3,35},{35,3},{4,36},{36... | collective-permute-start | bytes 49160 | tf_op jit(solution)/shard_map/ppermute | solution.py:23
  360.6 6.2 %collective-permute-start.14 = (f32[64,64]{1,0:T(8,128)S(1)}, f32[64,64]{1,0:T(8,128)S(1)}, u32[]{:S(2)}, u32[]{:S(2)}) collective-permute-start(f32[64,64]{1,0:T(8,128)S(1)} %select_select_fusion.3), channel_id=1, source_target_pairs={{0,64},{64,0},{1,65},{65,1},{2,66},{66,2},{3,67},{67,3},{4,68},{68... | collective-permute-start | bytes 49160 | tf_op jit(solution)/shard_map/ppermute | solution.py:23
  374.3 23.7 %collective-permute-start.15 = (f32[64,64]{1,0:T(8,128)S(1)}, f32[64,64]{1,0:T(8,128)S(1)}, u32[]{:S(2)}, u32[]{:S(2)}) collective-permute-start(f32[64,64]{1,0:T(8,128)S(1)} %select_select_fusion.2), channel_id=1, source_target_pairs={{0,128},{128,0},{1,129},{129,1},{2,130},{130,2},{3,131},{131,3},{4... | collective-permute-start | bytes 49160 | tf_op jit(solution)/shard_map/ppermute | solution.py:23
  405.4 10.1 %collective-permute-start.16 = (f32[64,64]{1,0:T(8,128)S(1)}, f32[64,64]{1,0:T(8,128)S(1)}, u32[]{:S(2)}, u32[]{:S(2)}) collective-permute-start(f32[64,64]{1,0:T(8,128)S(1)} %select_select_fusion.1), channel_id=1, source_target_pairs={{0,256},{256,0},{1,257},{257,1},{2,258},{258,2},{3,259},{259,3},{4... | collective-permute-start | bytes 49160 | tf_op jit(solution)/shard_map/ppermute | solution.py:23
where the time goes:
time: 432 us; the launch traced here: 430 us
  starting transfers between devices  177 us (41%)
  waiting for transfers between devices  122 us (28%)
  other arithmetic  79.5 us (18%)
  matrix products  34.5 us (8%)
  local copies, waits for them, and re-layouts  14.4 us (3%)
    ppermute x48, starting transfers between devices, shifted(): lax.ppermute(value, axis, [(source, source + steps) for source in range(f...  137 us
    ppermute x48, waiting for transfers between devices, shifted(): lax.ppermute(value, axis, [(source, source + steps) for source in range(f...  84.8 us
    another operation x27, other arithmetic, shards(): lower_factor = jnp.linalg.cholesky(own_part + partner_part)  58.7 us
    ppermute x9, starting transfers between devices, partner_2(): return lax.ppermute(block, axis, route)  39.7 us
    ppermute x9, waiting for transfers between devices, partner_2(): return lax.ppermute(block, axis, route)  36.9 us
    dot_general x12, matrix products, apply_operator(): jnp.einsum('vrkt,rkst->vrs', picked, operator_tiles, preferred_element_ty...  29.7 us
    gather x12, local copies, waits for them, and re-layouts, apply_operator(): picked = jnp.take(window, local_index, axis=1)  9.01 us
  transfers between devices with their start and end apart: 57, of which 21 were waited for; matrix products, arithmetic and copies ran while one was open for 1% of the time, Pallas kernels for 0%

commit v1 on v0

v1 whole, which is shorter than its diff:
```python
import functools

import jax
import jax.numpy as jnp
from jax import lax
from jax.experimental import pallas as pl
from jax.experimental.pallas import tpu as pltpu
from jax.sharding import PartitionSpec as P

DEG = 12
AXES = ("rx", "ry")
VMEM = pl.BlockSpec(memory_space=pltpu.VMEM)
SMEM = pl.BlockSpec(memory_space=pltpu.SMEM)
LIMIT = 32 * 2**20


def moved(value, steps):
    count = lax.axis_size(AXES)
    first, last = max(0, -steps), min(count, count - steps)
    return lax.ppermute(value, AXES, [(source, source + steps) for source in range(first, last)])


def swapped(value):
    count = lax.axis_size(AXES)
    return lax.ppermute(value, AXES, [(source, source ^ 1) for source in range(count)])


def turn_kernel(tiles_ref, out_ref):
    rows, slots = tiles_ref.shape[:2]
    for row in range(rows):
        for slot in range(slots):
            out_ref[row, slot] = tiles_ref[row, slot].T


def turned(tiles):
    return pl.pallas_call(
        turn_kernel,
        in_specs=[VMEM],
        out_specs=VMEM,
        out_shape=jax.ShapeDtypeStruct(tiles.shape, tiles.dtype),
        compiler_params=pltpu.CompilerParams(vmem_limit_bytes=LIMIT),
        name="turn_tiles",
    )(tiles)


def step_kernel(first, index_ref, left_ref, own_ref, right_ref, near_ref, far_ref, *rest):
    older_ref, latest_ref, rounded_ref, window = (None, *rest) if first else rest
    count = own_ref.shape[0]
    window[0:count] = left_ref[...]
    window[count : 2 * count] = own_ref[...]
    window[2 * count : 3 * count] = right_ref[...]
    half, slots = near_ref.shape[:2]
    for row in range(count):
        tiles_ref, at = (near_ref, row) if row < half else (far_ref, row - half)
        total = None
        for slot in range(0, slots, 2):
            vectors = jnp.concatenate(
                [window[index_ref[row, slot]], window[index_ref[row, slot + 1]]], axis=1
            )
            tiles = jnp.concatenate([tiles_ref[at, slot], tiles_ref[at, slot + 1]], axis=0)
            part = jnp.dot(vectors, tiles, preferred_element_type=jnp.float32)
            total = part if total is None else total + part
        if not first:
            total = 2.0 * total - older_ref[row]
        latest_ref[row] = total
        rounded_ref[row] = total.astype(jnp.bfloat16)


def step(index, left, own, right, near, far, older=None):
    first = older is None
    flops = 2 * own.size * own.shape[2] * near.shape[1]
    return pl.pallas_call(
        functools.partial(step_kernel, first),
        in_specs=[SMEM] + [VMEM] * (5 if first else 6),
        out_specs=[VMEM, VMEM],
        out_shape=[
            jax.ShapeDtypeStruct(own.shape, jnp.float32),
            jax.ShapeDtypeStruct(own.shape, jnp.bfloat16),
        ],
        scratch_shapes=[pltpu.VMEM((3 * own.shape[0],) + own.shape[1:], jnp.bfloat16)],
        compiler_params=pltpu.CompilerParams(vmem_limit_bytes=LIMIT),
        cost_estimate=pl.CostEstimate(flops=flops, bytes_accessed=4 * near.size, transcendentals=0),
        name="first_step" if first else "step",
    )(index, left, own, right, near, far, *(() if first else (older,)))


def gram_kernel(scale, core_ref, mine_ref, theirs_ref, block_ref, gram_ref):
    tiles, half, width = mine_ref.shape
    even = core_ref[0] == 0
    for tile in range(tiles):
        mine, theirs = mine_ref[tile], theirs_ref[tile]
        columns = pl.ds(tile * width, width)
        block_ref[0:half, columns] = jnp.where(even, mine, theirs)
        block_ref[half : 2 * half, columns] = jnp.where(even, theirs, mine)
    block = block_ref[...]
    gram_ref[...] = scale * lax.dot_general(
        block,
        block,
        (((1,), (1,)), ((), ())),
        precision=lax.Precision.HIGHEST,
        preferred_element_type=jnp.float32,
    )


def gram_of(core, mine, theirs, scale):
    tiles, half, width = mine.shape
    return pl.pallas_call(
        functools.partial(gram_kernel, scale),
        in_specs=[SMEM, VMEM, VMEM],
        out_specs=[VMEM, VMEM],
        out_shape=[
            jax.ShapeDtypeStruct((2 * half, tiles * width), jnp.float32),
            jax.ShapeDtypeStruct((2 * half, 2 * half), jnp.float32),
        ],
        compiler_params=pltpu.CompilerParams(vmem_limit_bytes=LIMIT),
        name="gram",
    )(core, mine, theirs)


def finish_kernel(gram_ref, block_ref, basis_ref, factor_ref, rows):
    size = gram_ref.shape[0]
    row_of = lax.broadcasted_iota(jnp.int32, (8, 2 * size), 0)
    lane_of = lax.broadcasted_iota(jnp.int32, (8, 2 * size), 1)
    groups = []
    for group in range(size // 8):
        unit = (lane_of == row_of + (8 * group + size)).astype(jnp.float32)
        groups.append(
            jnp.concatenate([gram_ref[8 * group : 8 * group + 8, :], unit[:, size:]], axis=1)
        )
    for pivot in range(size):
        at, inner = divmod(pivot, 8)
        pivot_row = groups[at][inner : inner + 1, :]
        diagonal = pivot_row[:, pivot : pivot + 1]
        rows[pivot : pivot + 1, :] = pivot_row * lax.rsqrt(diagonal)
        scaled = pivot_row * (1.0 / diagonal)
        for group in range(at, size // 8):
            column = groups[group][:, pivot : pivot + 1]
            if group == at:
                if inner == 7:
                    continue
                column = jnp.where(row_of[:, :1] > inner, column, 0.0)
            groups[group] = groups[group] - column * scaled
    upper = lax.broadcasted_iota(jnp.int32, (size, size), 0) <= lax.broadcasted_iota(
        jnp.int32, (size, size), 1
    )
    done = rows[...]
    factor_ref[...] = jnp.where(upper, done[:, :size], 0.0)
    basis_ref[...] = jnp.dot(
        done[:, size:],
        block_ref[...],
        precision=lax.Precision.HIGHEST,
        preferred_element_type=jnp.float32,
    )


def finish(gram, block):
    size = gram.shape[0]
    return pl.pallas_call(
        finish_kernel,
        in_specs=[VMEM, VMEM],
        out_specs=[VMEM, VMEM],
        out_shape=[
            jax.ShapeDtypeStruct(block.shape, jnp.float32),
            jax.ShapeDtypeStruct(gram.shape, jnp.float32),
        ],
        scratch_shapes=[pltpu.VMEM((size, 2 * size), jnp.float32)],
        compiler_params=pltpu.CompilerParams(vmem_limit_bytes=LIMIT),
        name="factor_and_solve",
    )(gram, block)


def summed(gram):
    size = gram.shape[0]
    inner, outer = lax.axis_size("ry"), lax.axis_size("rx")
    part = lax.all_to_all(gram.reshape(inner, size // inner * size), "ry", 0, 0, tiled=True)
    part = jnp.sum(part, axis=0)
    part = lax.all_to_all(jnp.broadcast_to(part, (outer,) + part.shape), "rx", 0, 0, tiled=True)
    part = jnp.sum(part, axis=0)
    part = lax.all_to_all(jnp.broadcast_to(part, (inner,) + part.shape), "ry", 0, 0, tiled=True)
    return part.reshape(size, size)


def shards(start_block, operator_tiles, tile_pattern):
    vectors, node_count = start_block.shape
    rows_local, _, tile_size = operator_tiles.shape[:3]
    half = vectors // 2
    device_count = lax.axis_size(AXES)
    position = lax.axis_index(AXES)
    core = position % 2
    chip_rows = 2 * rows_local

    start_tiles = start_block.reshape(vectors, rows_local, tile_size).transpose(1, 0, 2)
    low, high = start_tiles[:, :half], start_tiles[:, half:]
    mine = jnp.where(core == 0, low, high)
    theirs = swapped(jnp.where(core == 0, high, low))
    rounded = jnp.concatenate([mine, theirs], axis=0)

    near = turned(operator_tiles)
    far = swapped(near)
    pattern = jnp.concatenate([tile_pattern, swapped(tile_pattern)], axis=0)
    index = jnp.clip(pattern - (position // 2 - 1) * chip_rows, 0, 3 * chip_rows - 1)
    index = index ^ (core * rows_local)

    earlier = rounded.astype(jnp.float32)
    latest, rounded = step(index, moved(rounded, 2), rounded, moved(rounded, -2), near, far)
    for _ in range(DEG - 1):
        following, next_rounded = step(
            index, moved(rounded, 2), rounded, moved(rounded, -2), near, far, earlier
        )
        earlier, latest, rounded = latest, following, next_rounded

    block, gram = gram_of(
        core.reshape(1),
        latest[:rows_local],
        swapped(latest[rows_local:]),
        1.0 / (node_count * device_count),
    )
    return finish(summed(gram), block)


def solution(mesh):
    return jax.shard_map(
        shards,
        mesh=mesh,
        in_specs=(P(None, AXES), P(AXES, None, None, None), P(AXES, None)),
        out_specs=(P(None, AXES), P()),
        check_vma=False,
    )
```

time: 432 us -> 269 us (0.62)
  the two profiles are of different devices: /device:TPU:62 before, /device:TPU:1 now
where the time goes in v1:
time: 269 us; the launch traced here: 268 us
  starting transfers between devices  103 us (38%)
  blocking collectives  96.9 us (36%)
  Pallas kernels  37.7 us (14%)
  waiting for transfers between devices  27 us (10%)
    ppermute x24, starting transfers between devices, moved(): lax.ppermute(value, AXES, [(source, source + steps) for source in range(f...  73.8 us
    all_to_all x1, blocking collectives, summed(): lax.all_to_all(jnp.broadcast_to(part, (outer,) + part.shape), 'rx', 0, 0,...  61.8 us
    pallas_call x12, Pallas kernels, step(): pl.pallas_call(functools.partial(step_kernel, first), in_specs=[SMEM] + [...  30.3 us
    ppermute x4, starting transfers between devices, swapped(): lax.ppermute(value, AXES, [(source, source ^ 1) for source in range(count)])  29 us
    all_to_all x1, blocking collectives, summed(): lax.all_to_all(gram.reshape(inner, size // inner * size), 'ry', 0, 0, til...  23.5 us
    ppermute x24, waiting for transfers between devices, moved(): lax.ppermute(value, AXES, [(source, source + steps) for source in range(f...  23.4 us
    all_to_all x1, blocking collectives, summed(): lax.all_to_all(jnp.broadcast_to(part, (inner,) + part.shape), 'ry', 0, 0,...  11.6 us
    pallas_call x1, Pallas kernels, finish(): pl.pallas_call(finish_kernel, in_specs=[VMEM, VMEM], out_specs=[VMEM, VME...  6.43 us
  transfers between devices with their start and end apart: 28, of which 25 were waited for; matrix products, arithmetic and copies ran while one was open for 0% of the time, Pallas kernels for 0%

profile of v1, /device:TPU:1, one launch (start us, length us, event | category | flops | bytes accessed | tf_op | source)
XLA Modules:
  0.0 267.5 jit_solution(16244687381590618775)
XLA Ops:
  0.7 1.6 copy-done.1
  2.3 0.6 turn_tiles.1.near_ref
  2.9 8.8 %collective-permute-start.4 = (bf16[8,8,128,128]{3,2,1,0:T(8,128)(2,1)S(1)}, bf16[8,8,128,128]{3,2,1,0:T(8,128)(2,1)}, u32[]{:S(2)}, u32[]{:S(2)}) collective-permute-start(bf16[8,8,128,128]{3,2,1,0:T(8,128)(2,1)S(1)} %turn_tiles.1.near_ref), channel_id=1, source_target_pairs={{0,1},{1,0},{2,3},{3,2},{4,5},{5,4},{6,7},{7,6},{8,9},{9,8},{10,11... | collective-permute-start | bytes 6291464 | tf_op jit(solution)/shard_map/ppermute | solution.py:25
  11.8 1.9 collective-permute-start.1
  13.7 1.8 collective-permute-done.1
  15.6 1.3 collective-permute-start.3
  16.9 4.0 %collective-permute-start.2 = (bf16[16,32,128]{2,1,0:T(8,128)(2,1)S(1)}, bf16[16,32,128]{2,1,0:T(8,128)(2,1)S(1)}, u32[]{:S(2)}, u32[]{:S(2)}) collective-permute-start(bf16[16,32,128]{2,1,0:T(8,128)(2,1)S(1)} %get-tuple-element.53.own_ref), channel_id=1, source_target_pairs={{0,2},{1,3},{2,4},{3,5},{4,6},{5,7},{6,8},{7,9},{8,10},{9,11},{10,... | collective-permute-start | bytes 393224 | tf_op jit(solution)/shard_map/ppermute | solution.py:20
  20.9 2.8 %collective-permute-start = (s32[8,8]{1,0:T(8,128)S(1)}, s32[8,8]{1,0:T(8,128)S(1)}, u32[]{:S(2)}, u32[]{:S(2)}) collective-permute-start(s32[8,8]{1,0:T(8,128)S(1)} %copy-done.2), channel_id=1, source_target_pairs={{0,1},{1,0},{2,3},{3,2},{4,5},{5,4},{6,7},{7,6},{8,9},{9,8},{10,11... | collective-permute-start | bytes 776 | tf_op jit(solution)/shard_map/ppermute | solution.py:25
  23.7 0.8 collective-permute-done
  24.6 2.4 first_step.1
  27.0 1.3 collective-permute-start.6
  28.3 4.0 %collective-permute-start.5 = (bf16[16,32,128]{2,1,0:T(8,128)(2,1)S(1)}, bf16[16,32,128]{2,1,0:T(8,128)(2,1)S(1)}, u32[]{:S(2)}, u32[]{:S(2)}) collective-permute-start(bf16[16,32,128]{2,1,0:T(8,128)(2,1)S(1)} %get-tuple-element.26.own_ref), channel_id=1, source_target_pairs={{0,2},{1,3},{2,4},{3,5},{4,6},{5,7},{6,8},{7,9},{8,10},{9,11},{10,... | collective-permute-start | bytes 393224 | tf_op jit(solution)/shard_map/ppermute | solution.py:20
  32.3 1.2 collective-permute-done.6.right_ref
  33.5 0.7 collective-permute-done.5.left_ref
  34.2 2.4 step.11
  36.6 1.3 collective-permute-start.8
  37.9 4.9 %collective-permute-start.7 = (bf16[16,32,128]{2,1,0:T(8,128)(2,1)S(1)}, bf16[16,32,128]{2,1,0:T(8,128)(2,1)S(1)}, u32[]{:S(2)}, u32[]{:S(2)}) collective-permute-start(bf16[16,32,128]{2,1,0:T(8,128)(2,1)S(1)} %get-tuple-element.27.own_ref), channel_id=1, source_target_pairs={{0,2},{1,3},{2,4},{3,5},{4,6},{5,7},{6,8},{7,9},{8,10},{9,11},{10,... | collective-permute-start | bytes 393224 | tf_op jit(solution)/shard_map/ppermute | solution.py:20
  43.2 1.5 collective-permute-done.7.left_ref
  44.7 2.4 step.12
  47.1 1.3 collective-permute-start.10
  48.4 4.7 %collective-permute-start.9 = (bf16[16,32,128]{2,1,0:T(8,128)(2,1)S(1)}, bf16[16,32,128]{2,1,0:T(8,128)(2,1)S(1)}, u32[]{:S(2)}, u32[]{:S(2)}) collective-permute-start(bf16[16,32,128]{2,1,0:T(8,128)(2,1)S(1)} %get-tuple-element.29.own_ref), channel_id=1, source_target_pairs={{0,2},{1,3},{2,4},{3,5},{4,6},{5,7},{6,8},{7,9},{8,10},{9,11},{10,... | collective-permute-start | bytes 393224 | tf_op jit(solution)/shard_map/ppermute | solution.py:20
  53.6 1.5 collective-permute-done.9.left_ref
  55.1 2.4 step.13
  57.5 1.3 collective-permute-start.12
  58.8 4.7 %collective-permute-start.11 = (bf16[16,32,128]{2,1,0:T(8,128)(2,1)S(1)}, bf16[16,32,128]{2,1,0:T(8,128)(2,1)S(1)}, u32[]{:S(2)}, u32[]{:S(2)}) collective-permute-start(bf16[16,32,128]{2,1,0:T(8,128)(2,1)S(1)} %get-tuple-element.31.own_ref), channel_id=1, source_target_pairs={{0,2},{1,3},{2,4},{3,5},{4,6},{5,7},{6,8},{7,9},{8,10},{9,11},{10,... | collective-permute-start | bytes 393224 | tf_op jit(solution)/shard_map/ppermute | solution.py:20
  63.9 1.5 collective-permute-done.11.left_ref
  65.4 2.4 step.14
  67.9 1.3 collective-permute-start.14
  69.2 4.4 %collective-permute-start.13 = (bf16[16,32,128]{2,1,0:T(8,128)(2,1)S(1)}, bf16[16,32,128]{2,1,0:T(8,128)(2,1)S(1)}, u32[]{:S(2)}, u32[]{:S(2)}) collective-permute-start(bf16[16,32,128]{2,1,0:T(8,128)(2,1)S(1)} %get-tuple-element.33.own_ref), channel_id=1, source_target_pairs={{0,2},{1,3},{2,4},{3,5},{4,6},{5,7},{6,8},{7,9},{8,10},{9,11},{10,... | collective-permute-start | bytes 393224 | tf_op jit(solution)/shard_map/ppermute | solution.py:20
  74.0 1.5 collective-permute-done.13.left_ref
  75.5 2.4 step.15
  77.9 1.3 collective-permute-start.16
  79.2 4.4 %collective-permute-start.15 = (bf16[16,32,128]{2,1,0:T(8,128)(2,1)S(1)}, bf16[16,32,128]{2,1,0:T(8,128)(2,1)S(1)}, u32[]{:S(2)}, u32[]{:S(2)}) collective-permute-start(bf16[16,32,128]{2,1,0:T(8,128)(2,1)S(1)} %get-tuple-element.35.own_ref), channel_id=1, source_target_pairs={{0,2},{1,3},{2,4},{3,5},{4,6},{5,7},{6,8},{7,9},{8,10},{9,11},{10,... | collective-permute-start | bytes 393224 | tf_op jit(solution)/shard_map/ppermute | solution.py:20
  84.1 1.5 collective-permute-done.15.left_ref
  85.6 2.4 step.16
  88.0 1.3 collective-permute-start.18
  89.3 4.4 %collective-permute-start.17 = (bf16[16,32,128]{2,1,0:T(8,128)(2,1)S(1)}, bf16[16,32,128]{2,1,0:T(8,128)(2,1)S(1)}, u32[]{:S(2)}, u32[]{:S(2)}) collective-permute-start(bf16[16,32,128]{2,1,0:T(8,128)(2,1)S(1)} %get-tuple-element.37.own_ref), channel_id=1, source_target_pairs={{0,2},{1,3},{2,4},{3,5},{4,6},{5,7},{6,8},{7,9},{8,10},{9,11},{10,... | collective-permute-start | bytes 393224 | tf_op jit(solution)/shard_map/ppermute | solution.py:20
  93.7 0.4 collective-permute-done.18.right_ref
  94.1 1.5 collective-permute-done.17.left_ref
  95.6 2.4 step.17
  98.1 1.3 collective-permute-start.20
  99.4 5.3 %collective-permute-start.19 = (bf16[16,32,128]{2,1,0:T(8,128)(2,1)S(1)}, bf16[16,32,128]{2,1,0:T(8,128)(2,1)S(1)}, u32[]{:S(2)}, u32[]{:S(2)}) collective-permute-start(bf16[16,32,128]{2,1,0:T(8,128)(2,1)S(1)} %get-tuple-element.39.own_ref), channel_id=1, source_target_pairs={{0,2},{1,3},{2,4},{3,5},{4,6},{5,7},{6,8},{7,9},{8,10},{9,11},{10,... | collective-permute-start | bytes 393224 | tf_op jit(solution)/shard_map/ppermute | solution.py:20
  105.1 1.5 collective-permute-done.19.left_ref
  106.6 2.4 step.18
  109.0 1.3 collective-permute-start.22
  110.3 5.6 %collective-permute-start.21 = (bf16[16,32,128]{2,1,0:T(8,128)(2,1)S(1)}, bf16[16,32,128]{2,1,0:T(8,128)(2,1)S(1)}, u32[]{:S(2)}, u32[]{:S(2)}) collective-permute-start(bf16[16,32,128]{2,1,0:T(8,128)(2,1)S(1)} %get-tuple-element.41.own_ref), channel_id=1, source_target_pairs={{0,2},{1,3},{2,4},{3,5},{4,6},{5,7},{6,8},{7,9},{8,10},{9,11},{10,... | collective-permute-start | bytes 393224 | tf_op jit(solution)/shard_map/ppermute | solution.py:20
  116.3 1.5 collective-permute-done.21.left_ref
  117.9 2.4 step.19
  120.3 1.3 collective-permute-start.24
  121.6 5.7 %collective-permute-start.23 = (bf16[16,32,128]{2,1,0:T(8,128)(2,1)S(1)}, bf16[16,32,128]{2,1,0:T(8,128)(2,1)S(1)}, u32[]{:S(2)}, u32[]{:S(2)}) collective-permute-start(bf16[16,32,128]{2,1,0:T(8,128)(2,1)S(1)} %get-tuple-element.43.own_ref), channel_id=1, source_target_pairs={{0,2},{1,3},{2,4},{3,5},{4,6},{5,7},{6,8},{7,9},{8,10},{9,11},{10,... | collective-permute-start | bytes 393224 | tf_op jit(solution)/shard_map/ppermute | solution.py:20
  127.2 1.0 collective-permute-done.24.right_ref
  128.3 1.8 collective-permute-done.23.left_ref
  130.0 3.1 %step.20 = (f32[16,32,128]{2,1,0:T(8,128)}, bf16[16,32,128]{2,1,0:T(8,128)(2,1)S(1)}) custom-call(s32[16,8]{1,0:T(8,128)S(1)} %fusion.1.index_ref, bf16[16,32,128]{2,1,0:T(8,128)(2,1)S(1)} %collective-permute-done.23.left_ref, bf16[16,32,128]{2,1,0:T(8,128)(2,1)S(1)} %get-tuple-element.43.own_ref, ...), custom_call_target="tpu_custom_call" | custom-call | flops 134217728 | bytes 4194304 | tf_op jit(solution)/shard_map/step/pallas_call | solution.py:72
  133.1 1.3 collective-permute-start.26
  134.4 6.2 %collective-permute-start.25 = (bf16[16,32,128]{2,1,0:T(8,128)(2,1)S(1)}, bf16[16,32,128]{2,1,0:T(8,128)(2,1)S(1)}, u32[]{:S(2)}, u32[]{:S(2)}) collective-permute-start(bf16[16,32,128]{2,1,0:T(8,128)(2,1)S(1)} %get-tuple-element.45.own_ref), channel_id=1, source_target_pairs={{0,2},{1,3},{2,4},{3,5},{4,6},{5,7},{6,8},{7,9},{8,10},{9,11},{10,... | collective-permute-start | bytes 393224 | tf_op jit(solution)/shard_map/ppermute | solution.py:20
  140.7 1.5 collective-permute-done.26.right_ref
  142.2 1.8 collective-permute-done.25.left_ref
  144.0 3.1 %step.21 = (f32[16,32,128]{2,1,0:T(8,128)S(1)}, bf16[16,32,128]{2,1,0:T(8,128)(2,1)}) custom-call(s32[16,8]{1,0:T(8,128)S(1)} %fusion.1.index_ref, bf16[16,32,128]{2,1,0:T(8,128)(2,1)S(1)} %collective-permute-done.25.left_ref, bf16[16,32,128]{2,1,0:T(8,128)(2,1)S(1)} %get-tuple-element.45.own_ref, ...), custom_call_target="tpu_custom_call" | custom-call | flops 134217728 | bytes 4194304 | tf_op jit(solution)/shard_map/step/pallas_call | solution.py:72
  147.1 15.5 %collective-permute-start.27 = (f32[8,32,128]{2,1,0:T(8,128)S(1)}, f32[8,32,128]{2,1,0:T(8,128)S(1)}, u32[]{:S(2)}, u32[]{:S(2)}) collective-permute-start(f32[8,32,128]{2,1,0:T(8,128)S(1)} %get-tuple-element.50), channel_id=1, source_target_pairs={{0,1},{1,0},{2,3},{3,2},{4,5},{5,4},{6,7},{7,6},{8,9},{9,8},{10,11... | collective-permute-start | bytes 393224 | tf_op jit(solution)/shard_map/ppermute | solution.py:25
  162.6 1.0 collective-permute-done.27.theirs_ref
  164.0 23.5 %all_to_all.22 = f32[16,1,256]{2,1,0:T(1,128)S(1)} all-to-all(f32[16,1,256]{2,1,0:T(1,128)S(1)} %all_to_all.18), channel_id=1, replica_groups=mesh['rx'=32,'ry'=16] {'ry'}, dimensions={0} | all-to-all | bytes 32768 | tf_op jit(solution)/shard_map/all_to_all | solution.py:175
  187.5 61.8 %all_to_all.23 = f32[32,1,256]{2,1,0:T(1,128)S(1)} all-to-all(f32[32,1,256]{2,1,0:T(1,128)S(1)} %broadcast_in_dim.6), channel_id=1, replica_groups=mesh['rx'=32,'ry'=16] {'rx'}, dimensions={0} | all-to-all | bytes 65536 | tf_op jit(solution)/shard_map/all_to_all | solution.py:177
  249.4 11.6 %all_to_all.24 = f32[16,1,256]{2,1,0:T(1,128)S(1)} all-to-all(f32[16,1,256]{2,1,0:T(1,128)S(1)} %broadcast_in_dim.7), channel_id=1, replica_groups=mesh['rx'=32,'ry'=16] {'ry'}, dimensions={0} | all-to-all | bytes 32768 | tf_op jit(solution)/shard_map/all_to_all | solution.py:179
  261.1 6.4 %factor_and_solve.1 = (f32[64,1024]{1,0:T(8,128)}, f32[64,64]{1,0:T(8,128)}) custom-call(f32[64,64]{1,0:T(8,128)S(1)} %reshape.28.gram_ref, f32[64,1024]{1,0:T(8,128)S(1)} %get-tuple-element.49.block_ref), custom_call_target="tpu_custom_call" | custom-call | tf_op jit(solution)/shard_map/factor_and_solve/pallas_call | solution.py:158
  (28 shorter events, 3.7 us)
Async XLA Ops:
  0.6 11.1 %copy-start = (bf16[64,1024]{1,0:T(8,128)(2,1)S(1)}, bf16[64,1024]{1,0:T(8,128)(2,1)}, u32[]{:S(2)}) copy-start(bf16[64,1024]{1,0:T(8,128)(2,1)} %param.3) | copy-start | bytes 393220
  0.6 1.6 copy-start.1
  2.3 18.6 %copy-start.2 = (s32[8,8]{1,0:T(8,128)S(1)}, s32[8,8]{1,0:T(8,128)}, u32[]{:S(2)}) copy-start(s32[8,8]{1,0:T(8,128)} %param.5) | copy-start | bytes 772
  2.9 21.7 %collective-permute-start.4 = (bf16[8,8,128,128]{3,2,1,0:T(8,128)(2,1)S(1)}, bf16[8,8,128,128]{3,2,1,0:T(8,128)(2,1)}, u32[]{:S(2)}, u32[]{:S(2)}) collective-permute-start(bf16[8,8,128,128]{3,2,1,0:T(8,128)(2,1)S(1)} %turn_tiles.1.near_ref), channel_id=1, source_target_pairs={{0,1},{1,0},{2,3},{3,2},{4,5},{5,4},{6,7},{7,6},{8,9},{9,8},{10,11... | collective-permute-start | bytes 6291464 | tf_op jit(solution)/shard_map/ppermute | solution.py:25
  11.8 3.8 %collective-permute-start.1 = (bf16[8,32,128]{2,1,0:T(8,128)(2,1)S(1)}, bf16[8,32,128]{2,1,0:T(8,128)(2,1)S(1)}, u32[]{:S(2)}, u32[]{:S(2)}) collective-permute-start(bf16[8,32,128]{2,1,0:T(8,128)(2,1)S(1)} %get-tuple-element.55), channel_id=1, source_target_pairs={{0,1},{1,0},{2,3},{3,2},{4,5},{5,4},{6,7},{7,6},{8,9},{9,8},{10,11... | collective-permute-start | bytes 196616 | tf_op jit(solution)/shard_map/ppermute | solution.py:25
  15.6 9.0 %collective-permute-start.3 = (bf16[16,32,128]{2,1,0:T(8,128)(2,1)S(1)}, bf16[16,32,128]{2,1,0:T(8,128)(2,1)S(1)}, u32[]{:S(2)}, u32[]{:S(2)}) collective-permute-start(bf16[16,32,128]{2,1,0:T(8,128)(2,1)S(1)} %get-tuple-element.53.own_ref), channel_id=1, source_target_pairs={{2,0},{3,1},{4,2},{5,3},{6,4},{7,5},{8,6},{9,7},{10,8},{11,9},{12,... | collective-permute-start | bytes 393224 | tf_op jit(solution)/shard_map/ppermute | solution.py:20
  16.9 7.7 %collective-permute-start.2 = (bf16[16,32,128]{2,1,0:T(8,128)(2,1)S(1)}, bf16[16,32,128]{2,1,0:T(8,128)(2,1)S(1)}, u32[]{:S(2)}, u32[]{:S(2)}) collective-permute-start(bf16[16,32,128]{2,1,0:T(8,128)(2,1)S(1)} %get-tuple-element.53.own_ref), channel_id=1, source_target_pairs={{0,2},{1,3},{2,4},{3,5},{4,6},{5,7},{6,8},{7,9},{8,10},{9,11},{10,... | collective-permute-start | bytes 393224 | tf_op jit(solution)/shard_map/ppermute | solution.py:20
  20.9 3.7 %collective-permute-start = (s32[8,8]{1,0:T(8,128)S(1)}, s32[8,8]{1,0:T(8,128)S(1)}, u32[]{:S(2)}, u32[]{:S(2)}) collective-permute-start(s32[8,8]{1,0:T(8,128)S(1)} %copy-done.2), channel_id=1, source_target_pairs={{0,1},{1,0},{2,3},{3,2},{4,5},{5,4},{6,7},{7,6},{8,9},{9,8},{10,11... | collective-permute-start | bytes 776 | tf_op jit(solution)/shard_map/ppermute | solution.py:25
  27.0 6.5 %collective-permute-start.6 = (bf16[16,32,128]{2,1,0:T(8,128)(2,1)S(1)}, bf16[16,32,128]{2,1,0:T(8,128)(2,1)S(1)}, u32[]{:S(2)}, u32[]{:S(2)}) collective-permute-start(bf16[16,32,128]{2,1,0:T(8,128)(2,1)S(1)} %get-tuple-element.26.own_ref), channel_id=1, source_target_pairs={{2,0},{3,1},{4,2},{5,3},{6,4},{7,5},{8,6},{9,7},{10,8},{11,9},{12,... | collective-permute-start | bytes 393224 | tf_op jit(solution)/shard_map/ppermute | solution.py:20
  28.3 5.9 %collective-permute-start.5 = (bf16[16,32,128]{2,1,0:T(8,128)(2,1)S(1)}, bf16[16,32,128]{2,1,0:T(8,128)(2,1)S(1)}, u32[]{:S(2)}, u32[]{:S(2)}) collective-permute-start(bf16[16,32,128]{2,1,0:T(8,128)(2,1)S(1)} %get-tuple-element.26.own_ref), channel_id=1, source_target_pairs={{0,2},{1,3},{2,4},{3,5},{4,6},{5,7},{6,8},{7,9},{8,10},{9,11},{10,... | collective-permute-start | bytes 393224 | tf_op jit(solution)/shard_map/ppermute | solution.py:20
  36.6 6.6 %collective-permute-start.8 = (bf16[16,32,128]{2,1,0:T(8,128)(2,1)S(1)}, bf16[16,32,128]{2,1,0:T(8,128)(2,1)S(1)}, u32[]{:S(2)}, u32[]{:S(2)}) collective-permute-start(bf16[16,32,128]{2,1,0:T(8,128)(2,1)S(1)} %get-tuple-element.27.own_ref), channel_id=1, source_target_pairs={{2,0},{3,1},{4,2},{5,3},{6,4},{7,5},{8,6},{9,7},{10,8},{11,9},{12,... | collective-permute-start | bytes 393224 | tf_op jit(solution)/shard_map/ppermute | solution.py:20
  37.9 6.8 %collective-permute-start.7 = (bf16[16,32,128]{2,1,0:T(8,128)(2,1)S(1)}, bf16[16,32,128]{2,1,0:T(8,128)(2,1)S(1)}, u32[]{:S(2)}, u32[]{:S(2)}) collective-permute-start(bf16[16,32,128]{2,1,0:T(8,128)(2,1)S(1)} %get-tuple-element.27.own_ref), channel_id=1, source_target_pairs={{0,2},{1,3},{2,4},{3,5},{4,6},{5,7},{6,8},{7,9},{8,10},{9,11},{10,... | collective-permute-start | bytes 393224 | tf_op jit(solution)/shard_map/ppermute | solution.py:20
  47.1 6.4 %collective-permute-start.10 = (bf16[16,32,128]{2,1,0:T(8,128)(2,1)S(1)}, bf16[16,32,128]{2,1,0:T(8,128)(2,1)S(1)}, u32[]{:S(2)}, u32[]{:S(2)}) collective-permute-start(bf16[16,32,128]{2,1,0:T(8,128)(2,1)S(1)} %get-tuple-element.29.own_ref), channel_id=1, source_target_pairs={{2,0},{3,1},{4,2},{5,3},{6,4},{7,5},{8,6},{9,7},{10,8},{11,9},{12,... | collective-permute-start | bytes 393224 | tf_op jit(solution)/shard_map/ppermute | solution.py:20
  48.4 6.6 %collective-permute-start.9 = (bf16[16,32,128]{2,1,0:T(8,128)(2,1)S(1)}, bf16[16,32,128]{2,1,0:T(8,128)(2,1)S(1)}, u32[]{:S(2)}, u32[]{:S(2)}) collective-permute-start(bf16[16,32,128]{2,1,0:T(8,128)(2,1)S(1)} %get-tuple-element.29.own_ref), channel_id=1, source_target_pairs={{0,2},{1,3},{2,4},{3,5},{4,6},{5,7},{6,8},{7,9},{8,10},{9,11},{10,... | collective-permute-start | bytes 393224 | tf_op jit(solution)/shard_map/ppermute | solution.py:20
  57.5 6.4 %collective-permute-start.12 = (bf16[16,32,128]{2,1,0:T(8,128)(2,1)S(1)}, bf16[16,32,128]{2,1,0:T(8,128)(2,1)S(1)}, u32[]{:S(2)}, u32[]{:S(2)}) collective-permute-start(bf16[16,32,128]{2,1,0:T(8,128)(2,1)S(1)} %get-tuple-element.31.own_ref), channel_id=1, source_target_pairs={{2,0},{3,1},{4,2},{5,3},{6,4},{7,5},{8,6},{9,7},{10,8},{11,9},{12,... | collective-permute-start | bytes 393224 | tf_op jit(solution)/shard_map/ppermute | solution.py:20
  58.8 6.6 %collective-permute-start.11 = (bf16[16,32,128]{2,1,0:T(8,128)(2,1)S(1)}, bf16[16,32,128]{2,1,0:T(8,128)(2,1)S(1)}, u32[]{:S(2)}, u32[]{:S(2)}) collective-permute-start(bf16[16,32,128]{2,1,0:T(8,128)(2,1)S(1)} %get-tuple-element.31.own_ref), channel_id=1, source_target_pairs={{0,2},{1,3},{2,4},{3,5},{4,6},{5,7},{6,8},{7,9},{8,10},{9,11},{10,... | collective-permute-start | bytes 393224 | tf_op jit(solution)/shard_map/ppermute | solution.py:20
  67.9 6.1 %collective-permute-start.14 = (bf16[16,32,128]{2,1,0:T(8,128)(2,1)S(1)}, bf16[16,32,128]{2,1,0:T(8,128)(2,1)S(1)}, u32[]{:S(2)}, u32[]{:S(2)}) collective-permute-start(bf16[16,32,128]{2,1,0:T(8,128)(2,1)S(1)} %get-tuple-element.33.own_ref), channel_id=1, source_target_pairs={{2,0},{3,1},{4,2},{5,3},{6,4},{7,5},{8,6},{9,7},{10,8},{11,9},{12,... | collective-permute-start | bytes 393224 | tf_op jit(solution)/shard_map/ppermute | solution.py:20
  69.2 6.3 %collective-permute-start.13 = (bf16[16,32,128]{2,1,0:T(8,128)(2,1)S(1)}, bf16[16,32,128]{2,1,0:T(8,128)(2,1)S(1)}, u32[]{:S(2)}, u32[]{:S(2)}) collective-permute-start(bf16[16,32,128]{2,1,0:T(8,128)(2,1)S(1)} %get-tuple-element.33.own_ref), channel_id=1, source_target_pairs={{0,2},{1,3},{2,4},{3,5},{4,6},{5,7},{6,8},{7,9},{8,10},{9,11},{10,... | collective-permute-start | bytes 393224 | tf_op jit(solution)/shard_map/ppermute | solution.py:20
  77.9 6.1 %collective-permute-start.16 = (bf16[16,32,128]{2,1,0:T(8,128)(2,1)S(1)}, bf16[16,32,128]{2,1,0:T(8,128)(2,1)S(1)}, u32[]{:S(2)}, u32[]{:S(2)}) collective-permute-start(bf16[16,32,128]{2,1,0:T(8,128)(2,1)S(1)} %get-tuple-element.35.own_ref), channel_id=1, source_target_pairs={{2,0},{3,1},{4,2},{5,3},{6,4},{7,5},{8,6},{9,7},{10,8},{11,9},{12,... | collective-permute-start | bytes 393224 | tf_op jit(solution)/shard_map/ppermute | solution.py:20
  79.2 6.3 %collective-permute-start.15 = (bf16[16,32,128]{2,1,0:T(8,128)(2,1)S(1)}, bf16[16,32,128]{2,1,0:T(8,128)(2,1)S(1)}, u32[]{:S(2)}, u32[]{:S(2)}) collective-permute-start(bf16[16,32,128]{2,1,0:T(8,128)(2,1)S(1)} %get-tuple-element.35.own_ref), channel_id=1, source_target_pairs={{0,2},{1,3},{2,4},{3,5},{4,6},{5,7},{6,8},{7,9},{8,10},{9,11},{10,... | collective-permute-start | bytes 393224 | tf_op jit(solution)/shard_map/ppermute | solution.py:20
  88.0 6.1 %collective-permute-start.18 = (bf16[16,32,128]{2,1,0:T(8,128)(2,1)S(1)}, bf16[16,32,128]{2,1,0:T(8,128)(2,1)S(1)}, u32[]{:S(2)}, u32[]{:S(2)}) collective-permute-start(bf16[16,32,128]{2,1,0:T(8,128)(2,1)S(1)} %get-tuple-element.37.own_ref), channel_id=1, source_target_pairs={{2,0},{3,1},{4,2},{5,3},{6,4},{7,5},{8,6},{9,7},{10,8},{11,9},{12,... | collective-permute-start | bytes 393224 | tf_op jit(solution)/shard_map/ppermute | solution.py:20
  89.3 6.3 %collective-permute-start.17 = (bf16[16,32,128]{2,1,0:T(8,128)(2,1)S(1)}, bf16[16,32,128]{2,1,0:T(8,128)(2,1)S(1)}, u32[]{:S(2)}, u32[]{:S(2)}) collective-permute-start(bf16[16,32,128]{2,1,0:T(8,128)(2,1)S(1)} %get-tuple-element.37.own_ref), channel_id=1, source_target_pairs={{0,2},{1,3},{2,4},{3,5},{4,6},{5,7},{6,8},{7,9},{8,10},{9,11},{10,... | collective-permute-start | bytes 393224 | tf_op jit(solution)/shard_map/ppermute | solution.py:20
  98.1 7.0 %collective-permute-start.20 = (bf16[16,32,128]{2,1,0:T(8,128)(2,1)S(1)}, bf16[16,32,128]{2,1,0:T(8,128)(2,1)S(1)}, u32[]{:S(2)}, u32[]{:S(2)}) collective-permute-start(bf16[16,32,128]{2,1,0:T(8,128)(2,1)S(1)} %get-tuple-element.39.own_ref), channel_id=1, source_target_pairs={{2,0},{3,1},{4,2},{5,3},{6,4},{7,5},{8,6},{9,7},{10,8},{11,9},{12,... | collective-permute-start | bytes 393224 | tf_op jit(solution)/shard_map/ppermute | solution.py:20
  99.4 7.2 %collective-permute-start.19 = (bf16[16,32,128]{2,1,0:T(8,128)(2,1)S(1)}, bf16[16,32,128]{2,1,0:T(8,128)(2,1)S(1)}, u32[]{:S(2)}, u32[]{:S(2)}) collective-permute-start(bf16[16,32,128]{2,1,0:T(8,128)(2,1)S(1)} %get-tuple-element.39.own_ref), channel_id=1, source_target_pairs={{0,2},{1,3},{2,4},{3,5},{4,6},{5,7},{6,8},{7,9},{8,10},{9,11},{10,... | collective-permute-start | bytes 393224 | tf_op jit(solution)/shard_map/ppermute | solution.py:20
  109.0 7.3 %collective-permute-start.22 = (bf16[16,32,128]{2,1,0:T(8,128)(2,1)S(1)}, bf16[16,32,128]{2,1,0:T(8,128)(2,1)S(1)}, u32[]{:S(2)}, u32[]{:S(2)}) collective-permute-start(bf16[16,32,128]{2,1,0:T(8,128)(2,1)S(1)} %get-tuple-element.41.own_ref), channel_id=1, source_target_pairs={{2,0},{3,1},{4,2},{5,3},{6,4},{7,5},{8,6},{9,7},{10,8},{11,9},{12,... | collective-permute-start | bytes 393224 | tf_op jit(solution)/shard_map/ppermute | solution.py:20
  110.3 7.6 %collective-permute-start.21 = (bf16[16,32,128]{2,1,0:T(8,128)(2,1)S(1)}, bf16[16,32,128]{2,1,0:T(8,128)(2,1)S(1)}, u32[]{:S(2)}, u32[]{:S(2)}) collective-permute-start(bf16[16,32,128]{2,1,0:T(8,128)(2,1)S(1)} %get-tuple-element.41.own_ref), channel_id=1, source_target_pairs={{0,2},{1,3},{2,4},{3,5},{4,6},{5,7},{6,8},{7,9},{8,10},{9,11},{10,... | collective-permute-start | bytes 393224 | tf_op jit(solution)/shard_map/ppermute | solution.py:20
  120.3 8.0 %collective-permute-start.24 = (bf16[16,32,128]{2,1,0:T(8,128)(2,1)S(1)}, bf16[16,32,128]{2,1,0:T(8,128)(2,1)S(1)}, u32[]{:S(2)}, u32[]{:S(2)}) collective-permute-start(bf16[16,32,128]{2,1,0:T(8,128)(2,1)S(1)} %get-tuple-element.43.own_ref), channel_id=1, source_target_pairs={{2,0},{3,1},{4,2},{5,3},{6,4},{7,5},{8,6},{9,7},{10,8},{11,9},{12,... | collective-permute-start | bytes 393224 | tf_op jit(solution)/shard_map/ppermute | solution.py:20
  121.6 8.4 %collective-permute-start.23 = (bf16[16,32,128]{2,1,0:T(8,128)(2,1)S(1)}, bf16[16,32,128]{2,1,0:T(8,128)(2,1)S(1)}, u32[]{:S(2)}, u32[]{:S(2)}) collective-permute-start(bf16[16,32,128]{2,1,0:T(8,128)(2,1)S(1)} %get-tuple-element.43.own_ref), channel_id=1, source_target_pairs={{0,2},{1,3},{2,4},{3,5},{4,6},{5,7},{6,8},{7,9},{8,10},{9,11},{10,... | collective-permute-start | bytes 393224 | tf_op jit(solution)/shard_map/ppermute | solution.py:20
  133.1 9.0 %collective-permute-start.26 = (bf16[16,32,128]{2,1,0:T(8,128)(2,1)S(1)}, bf16[16,32,128]{2,1,0:T(8,128)(2,1)S(1)}, u32[]{:S(2)}, u32[]{:S(2)}) collective-permute-start(bf16[16,32,128]{2,1,0:T(8,128)(2,1)S(1)} %get-tuple-element.45.own_ref), channel_id=1, source_target_pairs={{2,0},{3,1},{4,2},{5,3},{6,4},{7,5},{8,6},{9,7},{10,8},{11,9},{12,... | collective-permute-start | bytes 393224 | tf_op jit(solution)/shard_map/ppermute | solution.py:20
  134.4 9.5 %collective-permute-start.25 = (bf16[16,32,128]{2,1,0:T(8,128)(2,1)S(1)}, bf16[16,32,128]{2,1,0:T(8,128)(2,1)S(1)}, u32[]{:S(2)}, u32[]{:S(2)}) collective-permute-start(bf16[16,32,128]{2,1,0:T(8,128)(2,1)S(1)} %get-tuple-element.45.own_ref), channel_id=1, source_target_pairs={{0,2},{1,3},{2,4},{3,5},{4,6},{5,7},{6,8},{7,9},{8,10},{9,11},{10,... | collective-permute-start | bytes 393224 | tf_op jit(solution)/shard_map/ppermute | solution.py:20
  147.1 16.5 %collective-permute-start.27 = (f32[8,32,128]{2,1,0:T(8,128)S(1)}, f32[8,32,128]{2,1,0:T(8,128)S(1)}, u32[]{:S(2)}, u32[]{:S(2)}) collective-permute-start(f32[8,32,128]{2,1,0:T(8,128)S(1)} %get-tuple-element.50), channel_id=1, source_target_pairs={{0,1},{1,0},{2,3},{3,2},{4,5},{5,4},{6,7},{7,6},{8,9},{9,8},{10,11... | collective-permute-start | bytes 393224 | tf_op jit(solution)/shard_map/ppermute | solution.py:25

commit v2 on v1

--- a/solution.py
+++ b/solution.py
@@ -11,13 +11,16 @@
 AXES = ("rx", "ry")
 VMEM = pl.BlockSpec(memory_space=pltpu.VMEM)
 SMEM = pl.BlockSpec(memory_space=pltpu.SMEM)
-LIMIT = 32 * 2**20
-
-
-def moved(value, steps):
+LIMIT = 16 * 2**20
+
+
+def traded(value, first):
     count = lax.axis_size(AXES)
-    first, last = max(0, -steps), min(count, count - steps)
-    return lax.ppermute(value, AXES, [(source, source + steps) for source in range(first, last)])
+    route = []
+    for low in range(2 * first, count - 2, 4):
+        for core in (0, 1):
+            route += [(low + core, low + core + 2), (low + core + 2, low + core)]
+    return lax.ppermute(value, AXES, route)
 
 
 def swapped(value):
@@ -25,39 +28,39 @@
     return lax.ppermute(value, AXES, [(source, source ^ 1) for source in range(count)])
 
 
-def turn_kernel(tiles_ref, out_ref):
-    rows, slots = tiles_ref.shape[:2]
+def turn_kernel(near_ref, far_ref, out_ref):
+    rows, slots = near_ref.shape[:2]
     for row in range(rows):
         for slot in range(slots):
-            out_ref[row, slot] = tiles_ref[row, slot].T
-
-
-def turned(tiles):
+            out_ref[row, slot] = near_ref[row, slot].T
+            out_ref[rows + row, slot] = far_ref[row, slot].T
+
+
+def turned(near, far):
     return pl.pallas_call(
         turn_kernel,
-        in_specs=[VMEM],
+        in_specs=[VMEM, VMEM],
         out_specs=VMEM,
-        out_shape=jax.ShapeDtypeStruct(tiles.shape, tiles.dtype),
+        out_shape=jax.ShapeDtypeStruct((2 * near.shape[0],) + near.shape[1:], near.dtype),
         compiler_params=pltpu.CompilerParams(vmem_limit_bytes=LIMIT),
         name="turn_tiles",
-    )(tiles)
-
-
-def step_kernel(first, index_ref, left_ref, own_ref, right_ref, near_ref, far_ref, *rest):
+    )(near, far)
+
+
+def step_kernel(first, index_ref, even_ref, own_ref, odd_ref, tiles_ref, *rest):
     older_ref, latest_ref, rounded_ref, window = (None, *rest) if first else rest
     count = own_ref.shape[0]
-    window[0:count] = left_ref[...]
+    window[0:count] = odd_ref[...]
     window[count : 2 * count] = own_ref[...]
-    window[2 * count : 3 * count] = right_ref[...]
-    half, slots = near_ref.shape[:2]
+    window[2 * count : 3 * count] = even_ref[...]
+    slots = tiles_ref.shape[1]
     for row in range(count):
-        tiles_ref, at = (near_ref, row) if row < half else (far_ref, row - half)
         total = None
         for slot in range(0, slots, 2):
             vectors = jnp.concatenate(
                 [window[index_ref[row, slot]], window[index_ref[row, slot + 1]]], axis=1
             )
-            tiles = jnp.concatenate([tiles_ref[at, slot], tiles_ref[at, slot + 1]], axis=0)
+            tiles = jnp.concatenate([tiles_ref[row, slot], tiles_ref[row, slot + 1]], axis=0)
             part = jnp.dot(vectors, tiles, preferred_element_type=jnp.float32)
             total = part if total is None else total + part
         if not first:
@@ -66,12 +69,12 @@
         rounded_ref[row] = total.astype(jnp.bfloat16)
 
 
-def step(index, left, own, right, near, far, older=None):
+def step(index, even, own, odd, tiles, older=None):
     first = older is None
-    flops = 2 * own.size * own.shape[2] * near.shape[1]
+    flops = 2 * own.size * own.shape[2] * tiles.shape[1]
     return pl.pallas_call(
         functools.partial(step_kernel, first),
-        in_specs=[SMEM] + [VMEM] * (5 if first else 6),
+        in_specs=[SMEM] + [VMEM] * (4 if first else 5),
         out_specs=[VMEM, VMEM],
         out_shape=[
             jax.ShapeDtypeStruct(own.shape, jnp.float32),
@@ -79,9 +82,9 @@
         ],
         scratch_shapes=[pltpu.VMEM((3 * own.shape[0],) + own.shape[1:], jnp.bfloat16)],
         compiler_params=pltpu.CompilerParams(vmem_limit_bytes=LIMIT),
-        cost_estimate=pl.CostEstimate(flops=flops, bytes_accessed=4 * near.size, transcendentals=0),
+        cost_estimate=pl.CostEstimate(flops=flops, bytes_accessed=2 * tiles.size, transcendentals=0),
         name="first_step" if first else "step",
-    )(index, left, own, right, near, far, *(() if first else (older,)))
+    )(index, even, own, odd, tiles, *(() if first else (older,)))
 
 
 def gram_kernel(scale, core_ref, mine_ref, theirs_ref, block_ref, gram_ref):
@@ -186,27 +189,37 @@
     half = vectors // 2
     device_count = lax.axis_size(AXES)
     position = lax.axis_index(AXES)
-    core = position % 2
+    chip, core = position // 2, position % 2
     chip_rows = 2 * rows_local
 
+    row_ids = jnp.arange(rows_local, dtype=jnp.int32)[:, None]
+    away = tile_pattern - (position * rows_local + row_ids)
     start_tiles = start_block.reshape(vectors, rows_local, tile_size).transpose(1, 0, 2)
     low, high = start_tiles[:, :half], start_tiles[:, half:]
-    mine = jnp.where(core == 0, low, high)
-    theirs = swapped(jnp.where(core == 0, high, low))
-    rounded = jnp.concatenate([mine, theirs], axis=0)
-
-    near = turned(operator_tiles)
-    far = swapped(near)
-    pattern = jnp.concatenate([tile_pattern, swapped(tile_pattern)], axis=0)
-    index = jnp.clip(pattern - (position // 2 - 1) * chip_rows, 0, 3 * chip_rows - 1)
-    index = index ^ (core * rows_local)
+    slots = away.shape[1]
+    packed = jnp.zeros((1, half, tile_size), jnp.bfloat16)
+    packed = packed.at[0, :rows_local, :slots].set(away.astype(jnp.bfloat16))
+    theirs = swapped(jnp.concatenate([jnp.where(core == 0, high, low), packed], axis=0))
+    rounded = jnp.concatenate([jnp.where(core == 0, low, high), theirs[:rows_local]], axis=0)
+    far_away = theirs[rows_local, :rows_local, :slots].astype(jnp.int32)
+
+    tiles = turned(operator_tiles, swapped(operator_tiles))
+
+    far_rows = (position ^ 1) * rows_local + row_ids
+    columns = jnp.concatenate([tile_pattern, far_away + far_rows], axis=0)
+    index = jnp.clip(columns - (chip - 1) * chip_rows, 0, 3 * chip_rows - 1)
+    place, inner = index // chip_rows, (index % chip_rows) ^ (core * rows_local)
+    index = jnp.where(chip % 2 == 1, 2 - place, place) * chip_rows + inner
+
+    def neighbours(own):
+        odd = traded(own, 1)
+        even = traded(own, 0)
+        return even, own, odd
 
     earlier = rounded.astype(jnp.float32)
-    latest, rounded = step(index, moved(rounded, 2), rounded, moved(rounded, -2), near, far)
+    latest, rounded = step(index, *neighbours(rounded), tiles)
     for _ in range(DEG - 1):
-        following, next_rounded = step(
-            index, moved(rounded, 2), rounded, moved(rounded, -2), near, far, earlier
-        )
+        following, next_rounded = step(index, *neighbours(rounded), tiles, earlier)
         earlier, latest, rounded = latest, following, next_rounded
 
     block, gram = gram_of(

time: 269 us -> 234 us (0.87)
  blocking collectives: 96.9 us -> 67.5 us
  Pallas kernels: 37.7 us -> 27.1 us
  waiting for transfers between devices: 27 us -> 32 us
    all_to_all x1, blocking collectives: 61.8 us -> 38.6 us  [summed(): lax.all_to_all(jnp.broadcast_to(part, (outer,) + part.shape), 'rx', 0, 0,...]
    pallas_call x12, Pallas kernels: 30.3 us -> 19.2 us  [step(): pl.pallas_call(functools.partial(step_kernel, first), in_specs=[SMEM] + [...]
    ppermute x24, waiting for transfers between devices: 23.4 us -> 29.8 us  [traded(): return lax.ppermute(value, AXES, route)]
    all_to_all x1, blocking collectives: 23.5 us -> 17.3 us  [summed(): lax.all_to_all(gram.reshape(inner, size // inner * size), 'ry', 0, 0, til...]
    ppermute x4 -> x3, starting transfers between devices: 29 us -> 28.3 us  [swapped(): lax.ppermute(value, AXES, [(source, source ^ 1) for source in range(count)])]
  transfers between devices with their start and end apart: 28 -> 27, of which waited for: 25 -> 14; matrix products, arithmetic and copies ran while one was open for 0% -> 1% of each run, Pallas kernels for 0% -> 0%
where the time goes in v2:
time: 234 us; the launch traced here: 233 us
  starting transfers between devices  101 us (43%)
  blocking collectives  67.5 us (29%)
  waiting for transfers between devices  32 us (14%)
  Pallas kernels  27.1 us (12%)
    ppermute x24, starting transfers between devices, traded(): return lax.ppermute(value, AXES, route)  73 us
    all_to_all x1, blocking collectives, summed(): lax.all_to_all(jnp.broadcast_to(part, (outer,) + part.shape), 'rx', 0, 0,...  38.6 us
    ppermute x24, waiting for transfers between devices, traded(): return lax.ppermute(value, AXES, route)  29.8 us
    ppermute x3, starting transfers between devices, swapped(): lax.ppermute(value, AXES, [(source, source ^ 1) for source in range(count)])  28.3 us
    pallas_call x12, Pallas kernels, step(): pl.pallas_call(functools.partial(step_kernel, first), in_specs=[SMEM] + [...  19.2 us
    all_to_all x1, blocking collectives, summed(): lax.all_to_all(gram.reshape(inner, size // inner * size), 'ry', 0, 0, til...  17.3 us
    all_to_all x1, blocking collectives, summed(): lax.all_to_all(jnp.broadcast_to(part, (inner,) + part.shape), 'ry', 0, 0,...  11.6 us
    pallas_call x1, Pallas kernels, finish(): pl.pallas_call(finish_kernel, in_specs=[VMEM, VMEM], out_specs=[VMEM, VME...  6.43 us
  transfers between devices with their start and end apart: 27, of which 14 were waited for; matrix products, arithmetic and copies ran while one was open for 1% of the time, Pallas kernels for 0%

profile of v2, /device:TPU:1, one launch (start us, length us, event | category | flops | bytes accessed | tf_op | source)
XLA Modules:
  0.0 232.5 jit_solution(5830966144706939551)
XLA Ops:
  0.6 8.9 %collective-permute-start.3 = (bf16[8,8,128,128]{3,2,1,0:T(8,128)(2,1)}, bf16[8,8,128,128]{3,2,1,0:T(8,128)(2,1)S(1)}, u32[]{:S(2)}, u32[]{:S(2)}) collective-permute-start(bf16[8,8,128,128]{3,2,1,0:T(8,128)(2,1)} %near_ref.1), channel_id=1, source_target_pairs={{0,1},{1,0},{2,3},{3,2},{4,5},{5,4},{6,7},{7,6},{8,9},{9,8},{10,11... | collective-permute-start | bytes 6291464 | tf_op jit(solution)/shard_map/ppermute | solution.py:28
  9.6 0.8 fusion.10
  10.4 1.9 collective-permute-start
  12.4 1.2 collective-permute-done
  13.6 0.7 collective-permute-start.2
  14.3 1.9 collective-permute-start.1
  16.3 0.7 fusion.3.index_ref
  17.0 1.6 copy-done.1
  18.6 1.1 turn_tiles.1.tiles_ref
  19.8 1.3 collective-permute-done.1.even_ref
  21.1 1.5 first_step.1
  22.5 0.7 collective-permute-start.5
  23.2 4.1 %collective-permute-start.4 = (bf16[16,32,128]{2,1,0:T(8,128)(2,1)S(1)}, bf16[16,32,128]{2,1,0:T(8,128)(2,1)S(1)}, u32[]{:S(2)}, u32[]{:S(2)}) collective-permute-start(bf16[16,32,128]{2,1,0:T(8,128)(2,1)S(1)} %get-tuple-element.38.own_ref), channel_id=1, source_target_pairs={{0,2},{2,0},{1,3},{3,1},{4,6},{6,4},{5,7},{7,5},{8,10},{10,8},{9,1... | collective-permute-start | bytes 393224 | tf_op jit(solution)/shard_map/ppermute | solution.py:23
  27.3 2.6 %collective-permute-done.4.even_ref = bf16[16,32,128]{2,1,0:T(8,128)(2,1)S(1)} collective-permute-done((bf16[16,32,128]{2,1,0:T(8,128)(2,1)S(1)}, bf16[16,32,128]{2,1,0:T(8,128)(2,1)S(1)}, u32[]{:S(2)}, u32[]{:S(2)}) %collective-permute-start.4) | collective-permute-done | bytes 131104 | tf_op jit(solution)/shard_map/ppermute | solution.py:23
  30.0 1.5 step.11
  31.5 0.7 collective-permute-start.7
  32.1 5.1 %collective-permute-start.6 = (bf16[16,32,128]{2,1,0:T(8,128)(2,1)S(1)}, bf16[16,32,128]{2,1,0:T(8,128)(2,1)S(1)}, u32[]{:S(2)}, u32[]{:S(2)}) collective-permute-start(bf16[16,32,128]{2,1,0:T(8,128)(2,1)S(1)} %get-tuple-element.39.own_ref), channel_id=1, source_target_pairs={{0,2},{2,0},{1,3},{3,1},{4,6},{6,4},{5,7},{7,5},{8,10},{10,8},{9,1... | collective-permute-start | bytes 393224 | tf_op jit(solution)/shard_map/ppermute | solution.py:23
  37.3 2.3 %collective-permute-done.6.even_ref = bf16[16,32,128]{2,1,0:T(8,128)(2,1)S(1)} collective-permute-done((bf16[16,32,128]{2,1,0:T(8,128)(2,1)S(1)}, bf16[16,32,128]{2,1,0:T(8,128)(2,1)S(1)}, u32[]{:S(2)}, u32[]{:S(2)}) %collective-permute-start.6) | collective-permute-done | bytes 131104 | tf_op jit(solution)/shard_map/ppermute | solution.py:23
  39.6 1.5 step.12
  41.1 0.7 collective-permute-start.9
  41.8 6.0 %collective-permute-start.8 = (bf16[16,32,128]{2,1,0:T(8,128)(2,1)S(1)}, bf16[16,32,128]{2,1,0:T(8,128)(2,1)S(1)}, u32[]{:S(2)}, u32[]{:S(2)}) collective-permute-start(bf16[16,32,128]{2,1,0:T(8,128)(2,1)S(1)} %get-tuple-element.41.own_ref), channel_id=1, source_target_pairs={{0,2},{2,0},{1,3},{3,1},{4,6},{6,4},{5,7},{7,5},{8,10},{10,8},{9,1... | collective-permute-start | bytes 393224 | tf_op jit(solution)/shard_map/ppermute | solution.py:23
  47.8 2.3 %collective-permute-done.8.even_ref = bf16[16,32,128]{2,1,0:T(8,128)(2,1)S(1)} collective-permute-done((bf16[16,32,128]{2,1,0:T(8,128)(2,1)S(1)}, bf16[16,32,128]{2,1,0:T(8,128)(2,1)S(1)}, u32[]{:S(2)}, u32[]{:S(2)}) %collective-permute-start.8) | collective-permute-done | bytes 131104 | tf_op jit(solution)/shard_map/ppermute | solution.py:23
  50.1 1.5 step.13
  51.6 0.7 collective-permute-start.11
  52.3 5.1 %collective-permute-start.10 = (bf16[16,32,128]{2,1,0:T(8,128)(2,1)S(1)}, bf16[16,32,128]{2,1,0:T(8,128)(2,1)S(1)}, u32[]{:S(2)}, u32[]{:S(2)}) collective-permute-start(bf16[16,32,128]{2,1,0:T(8,128)(2,1)S(1)} %get-tuple-element.43.own_ref), channel_id=1, source_target_pairs={{0,2},{2,0},{1,3},{3,1},{4,6},{6,4},{5,7},{7,5},{8,10},{10,8},{9,1... | collective-permute-start | bytes 393224 | tf_op jit(solution)/shard_map/ppermute | solution.py:23
  57.4 2.3 %collective-permute-done.10.even_ref = bf16[16,32,128]{2,1,0:T(8,128)(2,1)S(1)} collective-permute-done((bf16[16,32,128]{2,1,0:T(8,128)(2,1)S(1)}, bf16[16,32,128]{2,1,0:T(8,128)(2,1)S(1)}, u32[]{:S(2)}, u32[]{:S(2)}) %collective-permute-start.10) | collective-permute-done | bytes 131104 | tf_op jit(solution)/shard_map/ppermute | solution.py:23
  59.7 1.5 step.14
  61.2 0.7 collective-permute-start.13
  61.9 7.7 %collective-permute-start.12 = (bf16[16,32,128]{2,1,0:T(8,128)(2,1)S(1)}, bf16[16,32,128]{2,1,0:T(8,128)(2,1)S(1)}, u32[]{:S(2)}, u32[]{:S(2)}) collective-permute-start(bf16[16,32,128]{2,1,0:T(8,128)(2,1)S(1)} %get-tuple-element.45.own_ref), channel_id=1, source_target_pairs={{0,2},{2,0},{1,3},{3,1},{4,6},{6,4},{5,7},{7,5},{8,10},{10,8},{9,1... | collective-permute-start | bytes 393224 | tf_op jit(solution)/shard_map/ppermute | solution.py:23
  69.6 2.3 %collective-permute-done.12.even_ref = bf16[16,32,128]{2,1,0:T(8,128)(2,1)S(1)} collective-permute-done((bf16[16,32,128]{2,1,0:T(8,128)(2,1)S(1)}, bf16[16,32,128]{2,1,0:T(8,128)(2,1)S(1)}, u32[]{:S(2)}, u32[]{:S(2)}) %collective-permute-start.12) | collective-permute-done | bytes 131104 | tf_op jit(solution)/shard_map/ppermute | solution.py:23
  71.9 1.5 step.15
  73.4 0.7 collective-permute-start.15
  74.1 4.6 %collective-permute-start.14 = (bf16[16,32,128]{2,1,0:T(8,128)(2,1)S(1)}, bf16[16,32,128]{2,1,0:T(8,128)(2,1)S(1)}, u32[]{:S(2)}, u32[]{:S(2)}) collective-permute-start(bf16[16,32,128]{2,1,0:T(8,128)(2,1)S(1)} %get-tuple-element.47.own_ref), channel_id=1, source_target_pairs={{0,2},{2,0},{1,3},{3,1},{4,6},{6,4},{5,7},{7,5},{8,10},{10,8},{9,1... | collective-permute-start | bytes 393224 | tf_op jit(solution)/shard_map/ppermute | solution.py:23
  78.7 2.3 %collective-permute-done.14.even_ref = bf16[16,32,128]{2,1,0:T(8,128)(2,1)S(1)} collective-permute-done((bf16[16,32,128]{2,1,0:T(8,128)(2,1)S(1)}, bf16[16,32,128]{2,1,0:T(8,128)(2,1)S(1)}, u32[]{:S(2)}, u32[]{:S(2)}) %collective-permute-start.14) | collective-permute-done | bytes 131104 | tf_op jit(solution)/shard_map/ppermute | solution.py:23
  81.1 1.5 step.16
  82.5 0.7 collective-permute-start.17
  83.2 7.0 %collective-permute-start.16 = (bf16[16,32,128]{2,1,0:T(8,128)(2,1)S(1)}, bf16[16,32,128]{2,1,0:T(8,128)(2,1)S(1)}, u32[]{:S(2)}, u32[]{:S(2)}) collective-permute-start(bf16[16,32,128]{2,1,0:T(8,128)(2,1)S(1)} %get-tuple-element.49.own_ref), channel_id=1, source_target_pairs={{0,2},{2,0},{1,3},{3,1},{4,6},{6,4},{5,7},{7,5},{8,10},{10,8},{9,1... | collective-permute-start | bytes 393224 | tf_op jit(solution)/shard_map/ppermute | solution.py:23
  90.2 2.3 %collective-permute-done.16.even_ref = bf16[16,32,128]{2,1,0:T(8,128)(2,1)S(1)} collective-permute-done((bf16[16,32,128]{2,1,0:T(8,128)(2,1)S(1)}, bf16[16,32,128]{2,1,0:T(8,128)(2,1)S(1)}, u32[]{:S(2)}, u32[]{:S(2)}) %collective-permute-start.16) | collective-permute-done | bytes 131104 | tf_op jit(solution)/shard_map/ppermute | solution.py:23
  92.5 1.5 step.17
  94.0 0.7 collective-permute-start.19
  94.7 5.3 %collective-permute-start.18 = (bf16[16,32,128]{2,1,0:T(8,128)(2,1)S(1)}, bf16[16,32,128]{2,1,0:T(8,128)(2,1)S(1)}, u32[]{:S(2)}, u32[]{:S(2)}) collective-permute-start(bf16[16,32,128]{2,1,0:T(8,128)(2,1)S(1)} %get-tuple-element.51.own_ref), channel_id=1, source_target_pairs={{0,2},{2,0},{1,3},{3,1},{4,6},{6,4},{5,7},{7,5},{8,10},{10,8},{9,1... | collective-permute-start | bytes 393224 | tf_op jit(solution)/shard_map/ppermute | solution.py:23
  100.0 3.5 %collective-permute-done.18.even_ref = bf16[16,32,128]{2,1,0:T(8,128)(2,1)S(1)} collective-permute-done((bf16[16,32,128]{2,1,0:T(8,128)(2,1)S(1)}, bf16[16,32,128]{2,1,0:T(8,128)(2,1)S(1)}, u32[]{:S(2)}, u32[]{:S(2)}) %collective-permute-start.18) | collective-permute-done | bytes 131104 | tf_op jit(solution)/shard_map/ppermute | solution.py:23
  103.5 1.5 step.18
  105.0 0.7 collective-permute-start.21
  105.6 5.5 %collective-permute-start.20 = (bf16[16,32,128]{2,1,0:T(8,128)(2,1)S(1)}, bf16[16,32,128]{2,1,0:T(8,128)(2,1)S(1)}, u32[]{:S(2)}, u32[]{:S(2)}) collective-permute-start(bf16[16,32,128]{2,1,0:T(8,128)(2,1)S(1)} %get-tuple-element.53.own_ref), channel_id=1, source_target_pairs={{0,2},{2,0},{1,3},{3,1},{4,6},{6,4},{5,7},{7,5},{8,10},{10,8},{9,1... | collective-permute-start | bytes 393224 | tf_op jit(solution)/shard_map/ppermute | solution.py:23
  111.1 3.7 %collective-permute-done.20.even_ref = bf16[16,32,128]{2,1,0:T(8,128)(2,1)S(1)} collective-permute-done((bf16[16,32,128]{2,1,0:T(8,128)(2,1)S(1)}, bf16[16,32,128]{2,1,0:T(8,128)(2,1)S(1)}, u32[]{:S(2)}, u32[]{:S(2)}) %collective-permute-start.20) | collective-permute-done | bytes 131104 | tf_op jit(solution)/shard_map/ppermute | solution.py:23
  114.9 1.5 step.19
  116.4 0.7 collective-permute-start.23
  117.0 6.7 %collective-permute-start.22 = (bf16[16,32,128]{2,1,0:T(8,128)(2,1)S(1)}, bf16[16,32,128]{2,1,0:T(8,128)(2,1)S(1)}, u32[]{:S(2)}, u32[]{:S(2)}) collective-permute-start(bf16[16,32,128]{2,1,0:T(8,128)(2,1)S(1)} %get-tuple-element.55.own_ref), channel_id=1, source_target_pairs={{0,2},{2,0},{1,3},{3,1},{4,6},{6,4},{5,7},{7,5},{8,10},{10,8},{9,1... | collective-permute-start | bytes 393224 | tf_op jit(solution)/shard_map/ppermute | solution.py:23
  123.7 2.3 %collective-permute-done.22.even_ref = bf16[16,32,128]{2,1,0:T(8,128)(2,1)S(1)} collective-permute-done((bf16[16,32,128]{2,1,0:T(8,128)(2,1)S(1)}, bf16[16,32,128]{2,1,0:T(8,128)(2,1)S(1)}, u32[]{:S(2)}, u32[]{:S(2)}) %collective-permute-start.22) | collective-permute-done | bytes 131104 | tf_op jit(solution)/shard_map/ppermute | solution.py:23
  126.0 2.2 step.20
  128.2 0.7 collective-permute-start.25
  128.9 6.1 %collective-permute-start.24 = (bf16[16,32,128]{2,1,0:T(8,128)(2,1)S(1)}, bf16[16,32,128]{2,1,0:T(8,128)(2,1)S(1)}, u32[]{:S(2)}, u32[]{:S(2)}) collective-permute-start(bf16[16,32,128]{2,1,0:T(8,128)(2,1)S(1)} %get-tuple-element.57.own_ref), channel_id=1, source_target_pairs={{0,2},{2,0},{1,3},{3,1},{4,6},{6,4},{5,7},{7,5},{8,10},{10,8},{9,1... | collective-permute-start | bytes 393224 | tf_op jit(solution)/shard_map/ppermute | solution.py:23
  135.0 2.3 %collective-permute-done.24.even_ref = bf16[16,32,128]{2,1,0:T(8,128)(2,1)S(1)} collective-permute-done((bf16[16,32,128]{2,1,0:T(8,128)(2,1)S(1)}, bf16[16,32,128]{2,1,0:T(8,128)(2,1)S(1)}, u32[]{:S(2)}, u32[]{:S(2)}) %collective-permute-start.24) | collective-permute-done | bytes 131104 | tf_op jit(solution)/shard_map/ppermute | solution.py:23
  137.3 2.2 step.21
  139.5 17.5 %collective-permute-start.26 = (f32[8,32,128]{2,1,0:T(8,128)S(1)}, f32[8,32,128]{2,1,0:T(8,128)S(1)}, u32[]{:S(2)}, u32[]{:S(2)}) collective-permute-start(f32[8,32,128]{2,1,0:T(8,128)S(1)} %get-tuple-element.62), channel_id=1, source_target_pairs={{0,1},{1,0},{2,3},{3,2},{4,5},{5,4},{6,7},{7,6},{8,9},{9,8},{10,11... | collective-permute-start | bytes 393224 | tf_op jit(solution)/shard_map/ppermute | solution.py:28
  157.0 1.0 collective-permute-done.26.theirs_ref
  157.9 0.4 gram.1
  158.3 0.1 all_to_all.18
  158.4 17.3 %all_to_all.22 = f32[16,1,256]{2,1,0:T(1,128)S(1)} all-to-all(f32[16,1,256]{2,1,0:T(1,128)S(1)} %all_to_all.18), channel_id=1, replica_groups=mesh['rx'=32,'ry'=16] {'ry'}, dimensions={0} | all-to-all | bytes 32768 | tf_op jit(solution)/shard_map/all_to_all | solution.py:178
  175.7 38.6 %all_to_all.23 = f32[32,1,256]{2,1,0:T(1,128)S(1)} all-to-all(f32[32,1,256]{2,1,0:T(1,128)S(1)} %broadcast_in_dim.8), channel_id=1, replica_groups=mesh['rx'=32,'ry'=16] {'rx'}, dimensions={0} | all-to-all | bytes 65536 | tf_op jit(solution)/shard_map/all_to_all | solution.py:180
  214.4 11.6 %all_to_all.24 = f32[16,1,256]{2,1,0:T(1,128)S(1)} all-to-all(f32[16,1,256]{2,1,0:T(1,128)S(1)} %broadcast_in_dim.9), channel_id=1, replica_groups=mesh['rx'=32,'ry'=16] {'ry'}, dimensions={0} | all-to-all | bytes 32768 | tf_op jit(solution)/shard_map/all_to_all | solution.py:182
  226.0 0.1 reshape.80.gram_ref
  226.1 6.4 %factor_and_solve.1 = (f32[64,1024]{1,0:T(8,128)}, f32[64,64]{1,0:T(8,128)}) custom-call(f32[64,64]{1,0:T(8,128)S(1)} %reshape.80.gram_ref, f32[64,1024]{1,0:T(8,128)S(1)} %get-tuple-element.61.block_ref), custom_call_target="tpu_custom_call" | custom-call | tf_op jit(solution)/shard_map/factor_and_solve/pallas_call | solution.py:161
  (30 shorter events, 0.4 us)
Async XLA Ops:
  0.6 9.7 %copy-start = (bf16[64,1024]{1,0:T(8,128)(2,1)S(1)}, bf16[64,1024]{1,0:T(8,128)(2,1)}, u32[]{:S(2)}) copy-start(bf16[64,1024]{1,0:T(8,128)(2,1)} %param.5) | copy-start | bytes 393220
  0.6 16.4 %collective-permute-start.3 = (bf16[8,8,128,128]{3,2,1,0:T(8,128)(2,1)}, bf16[8,8,128,128]{3,2,1,0:T(8,128)(2,1)S(1)}, u32[]{:S(2)}, u32[]{:S(2)}) collective-permute-start(bf16[8,8,128,128]{3,2,1,0:T(8,128)(2,1)} %near_ref.1), channel_id=1, source_target_pairs={{0,1},{1,0},{2,3},{3,2},{4,5},{5,4},{6,7},{7,6},{8,9},{9,8},{10,11... | collective-permute-start | bytes 6291464 | tf_op jit(solution)/shard_map/ppermute | solution.py:28
  10.4 3.2 %collective-permute-start = (bf16[9,32,128]{2,1,0:T(8,128)(2,1)S(1)}, bf16[9,32,128]{2,1,0:T(8,128)(2,1)S(1)}, u32[]{:S(2)}, u32[]{:S(2)}) collective-permute-start(bf16[9,32,128]{2,1,0:T(8,128)(2,1)S(1)} %fusion.1), channel_id=1, source_target_pairs={{0,1},{1,0},{2,3},{3,2},{4,5},{5,4},{6,7},{7,6},{8,9},{9,8},{10,11... | collective-permute-start | bytes 221192 | tf_op jit(solution)/shard_map/ppermute | solution.py:28
  13.6 6.1 %collective-permute-start.2 = (bf16[16,32,128]{2,1,0:T(8,128)(2,1)S(1)}, bf16[16,32,128]{2,1,0:T(8,128)(2,1)S(1)}, u32[]{:S(2)}, u32[]{:S(2)}) collective-permute-start(bf16[16,32,128]{2,1,0:T(8,128)(2,1)S(1)} %get-tuple-element.65.own_ref), channel_id=1, source_target_pairs={{2,4},{4,2},{3,5},{5,3},{6,8},{8,6},{7,9},{9,7},{10,12},{12,10},{1... | collective-permute-start | bytes 393224 | tf_op jit(solution)/shard_map/ppermute | solution.py:23
  14.3 6.8 %collective-permute-start.1 = (bf16[16,32,128]{2,1,0:T(8,128)(2,1)S(1)}, bf16[16,32,128]{2,1,0:T(8,128)(2,1)S(1)}, u32[]{:S(2)}, u32[]{:S(2)}) collective-permute-start(bf16[16,32,128]{2,1,0:T(8,128)(2,1)S(1)} %get-tuple-element.65.own_ref), channel_id=1, source_target_pairs={{0,2},{2,0},{1,3},{3,1},{4,6},{6,4},{5,7},{7,5},{8,10},{10,8},{9,1... | collective-permute-start | bytes 393224 | tf_op jit(solution)/shard_map/ppermute | solution.py:23
  17.0 1.6 copy-start.1
  22.5 4.8 %collective-permute-start.5 = (bf16[16,32,128]{2,1,0:T(8,128)(2,1)S(1)}, bf16[16,32,128]{2,1,0:T(8,128)(2,1)S(1)}, u32[]{:S(2)}, u32[]{:S(2)}) collective-permute-start(bf16[16,32,128]{2,1,0:T(8,128)(2,1)S(1)} %get-tuple-element.38.own_ref), channel_id=1, source_target_pairs={{2,4},{4,2},{3,5},{5,3},{6,8},{8,6},{7,9},{9,7},{10,12},{12,10},{1... | collective-permute-start | bytes 393224 | tf_op jit(solution)/shard_map/ppermute | solution.py:23
  23.2 6.8 %collective-permute-start.4 = (bf16[16,32,128]{2,1,0:T(8,128)(2,1)S(1)}, bf16[16,32,128]{2,1,0:T(8,128)(2,1)S(1)}, u32[]{:S(2)}, u32[]{:S(2)}) collective-permute-start(bf16[16,32,128]{2,1,0:T(8,128)(2,1)S(1)} %get-tuple-element.38.own_ref), channel_id=1, source_target_pairs={{0,2},{2,0},{1,3},{3,1},{4,6},{6,4},{5,7},{7,5},{8,10},{10,8},{9,1... | collective-permute-start | bytes 393224 | tf_op jit(solution)/shard_map/ppermute | solution.py:23
  31.5 5.8 %collective-permute-start.7 = (bf16[16,32,128]{2,1,0:T(8,128)(2,1)S(1)}, bf16[16,32,128]{2,1,0:T(8,128)(2,1)S(1)}, u32[]{:S(2)}, u32[]{:S(2)}) collective-permute-start(bf16[16,32,128]{2,1,0:T(8,128)(2,1)S(1)} %get-tuple-element.39.own_ref), channel_id=1, source_target_pairs={{2,4},{4,2},{3,5},{5,3},{6,8},{8,6},{7,9},{9,7},{10,12},{12,10},{1... | collective-permute-start | bytes 393224 | tf_op jit(solution)/shard_map/ppermute | solution.py:23
  32.1 7.5 %collective-permute-start.6 = (bf16[16,32,128]{2,1,0:T(8,128)(2,1)S(1)}, bf16[16,32,128]{2,1,0:T(8,128)(2,1)S(1)}, u32[]{:S(2)}, u32[]{:S(2)}) collective-permute-start(bf16[16,32,128]{2,1,0:T(8,128)(2,1)S(1)} %get-tuple-element.39.own_ref), channel_id=1, source_target_pairs={{0,2},{2,0},{1,3},{3,1},{4,6},{6,4},{5,7},{7,5},{8,10},{10,8},{9,1... | collective-permute-start | bytes 393224 | tf_op jit(solution)/shard_map/ppermute | solution.py:23
  41.1 6.7 %collective-permute-start.9 = (bf16[16,32,128]{2,1,0:T(8,128)(2,1)S(1)}, bf16[16,32,128]{2,1,0:T(8,128)(2,1)S(1)}, u32[]{:S(2)}, u32[]{:S(2)}) collective-permute-start(bf16[16,32,128]{2,1,0:T(8,128)(2,1)S(1)} %get-tuple-element.41.own_ref), channel_id=1, source_target_pairs={{2,4},{4,2},{3,5},{5,3},{6,8},{8,6},{7,9},{9,7},{10,12},{12,10},{1... | collective-permute-start | bytes 393224 | tf_op jit(solution)/shard_map/ppermute | solution.py:23
  41.8 8.3 %collective-permute-start.8 = (bf16[16,32,128]{2,1,0:T(8,128)(2,1)S(1)}, bf16[16,32,128]{2,1,0:T(8,128)(2,1)S(1)}, u32[]{:S(2)}, u32[]{:S(2)}) collective-permute-start(bf16[16,32,128]{2,1,0:T(8,128)(2,1)S(1)} %get-tuple-element.41.own_ref), channel_id=1, source_target_pairs={{0,2},{2,0},{1,3},{3,1},{4,6},{6,4},{5,7},{7,5},{8,10},{10,8},{9,1... | collective-permute-start | bytes 393224 | tf_op jit(solution)/shard_map/ppermute | solution.py:23
  51.6 5.8 %collective-permute-start.11 = (bf16[16,32,128]{2,1,0:T(8,128)(2,1)S(1)}, bf16[16,32,128]{2,1,0:T(8,128)(2,1)S(1)}, u32[]{:S(2)}, u32[]{:S(2)}) collective-permute-start(bf16[16,32,128]{2,1,0:T(8,128)(2,1)S(1)} %get-tuple-element.43.own_ref), channel_id=1, source_target_pairs={{2,4},{4,2},{3,5},{5,3},{6,8},{8,6},{7,9},{9,7},{10,12},{12,10},{1... | collective-permute-start | bytes 393224 | tf_op jit(solution)/shard_map/ppermute | solution.py:23
  52.3 7.4 %collective-permute-start.10 = (bf16[16,32,128]{2,1,0:T(8,128)(2,1)S(1)}, bf16[16,32,128]{2,1,0:T(8,128)(2,1)S(1)}, u32[]{:S(2)}, u32[]{:S(2)}) collective-permute-start(bf16[16,32,128]{2,1,0:T(8,128)(2,1)S(1)} %get-tuple-element.43.own_ref), channel_id=1, source_target_pairs={{0,2},{2,0},{1,3},{3,1},{4,6},{6,4},{5,7},{7,5},{8,10},{10,8},{9,1... | collective-permute-start | bytes 393224 | tf_op jit(solution)/shard_map/ppermute | solution.py:23
  61.2 8.4 %collective-permute-start.13 = (bf16[16,32,128]{2,1,0:T(8,128)(2,1)S(1)}, bf16[16,32,128]{2,1,0:T(8,128)(2,1)S(1)}, u32[]{:S(2)}, u32[]{:S(2)}) collective-permute-start(bf16[16,32,128]{2,1,0:T(8,128)(2,1)S(1)} %get-tuple-element.45.own_ref), channel_id=1, source_target_pairs={{2,4},{4,2},{3,5},{5,3},{6,8},{8,6},{7,9},{9,7},{10,12},{12,10},{1... | collective-permute-start | bytes 393224 | tf_op jit(solution)/shard_map/ppermute | solution.py:23
  61.9 10.1 %collective-permute-start.12 = (bf16[16,32,128]{2,1,0:T(8,128)(2,1)S(1)}, bf16[16,32,128]{2,1,0:T(8,128)(2,1)S(1)}, u32[]{:S(2)}, u32[]{:S(2)}) collective-permute-start(bf16[16,32,128]{2,1,0:T(8,128)(2,1)S(1)} %get-tuple-element.45.own_ref), channel_id=1, source_target_pairs={{0,2},{2,0},{1,3},{3,1},{4,6},{6,4},{5,7},{7,5},{8,10},{10,8},{9,1... | collective-permute-start | bytes 393224 | tf_op jit(solution)/shard_map/ppermute | solution.py:23
  73.4 5.3 %collective-permute-start.15 = (bf16[16,32,128]{2,1,0:T(8,128)(2,1)S(1)}, bf16[16,32,128]{2,1,0:T(8,128)(2,1)S(1)}, u32[]{:S(2)}, u32[]{:S(2)}) collective-permute-start(bf16[16,32,128]{2,1,0:T(8,128)(2,1)S(1)} %get-tuple-element.47.own_ref), channel_id=1, source_target_pairs={{2,4},{4,2},{3,5},{5,3},{6,8},{8,6},{7,9},{9,7},{10,12},{12,10},{1... | collective-permute-start | bytes 393224 | tf_op jit(solution)/shard_map/ppermute | solution.py:23
  74.1 7.0 %collective-permute-start.14 = (bf16[16,32,128]{2,1,0:T(8,128)(2,1)S(1)}, bf16[16,32,128]{2,1,0:T(8,128)(2,1)S(1)}, u32[]{:S(2)}, u32[]{:S(2)}) collective-permute-start(bf16[16,32,128]{2,1,0:T(8,128)(2,1)S(1)} %get-tuple-element.47.own_ref), channel_id=1, source_target_pairs={{0,2},{2,0},{1,3},{3,1},{4,6},{6,4},{5,7},{7,5},{8,10},{10,8},{9,1... | collective-permute-start | bytes 393224 | tf_op jit(solution)/shard_map/ppermute | solution.py:23
  82.5 7.7 %collective-permute-start.17 = (bf16[16,32,128]{2,1,0:T(8,128)(2,1)S(1)}, bf16[16,32,128]{2,1,0:T(8,128)(2,1)S(1)}, u32[]{:S(2)}, u32[]{:S(2)}) collective-permute-start(bf16[16,32,128]{2,1,0:T(8,128)(2,1)S(1)} %get-tuple-element.49.own_ref), channel_id=1, source_target_pairs={{2,4},{4,2},{3,5},{5,3},{6,8},{8,6},{7,9},{9,7},{10,12},{12,10},{1... | collective-permute-start | bytes 393224 | tf_op jit(solution)/shard_map/ppermute | solution.py:23
  83.2 9.3 %collective-permute-start.16 = (bf16[16,32,128]{2,1,0:T(8,128)(2,1)S(1)}, bf16[16,32,128]{2,1,0:T(8,128)(2,1)S(1)}, u32[]{:S(2)}, u32[]{:S(2)}) collective-permute-start(bf16[16,32,128]{2,1,0:T(8,128)(2,1)S(1)} %get-tuple-element.49.own_ref), channel_id=1, source_target_pairs={{0,2},{2,0},{1,3},{3,1},{4,6},{6,4},{5,7},{7,5},{8,10},{10,8},{9,1... | collective-permute-start | bytes 393224 | tf_op jit(solution)/shard_map/ppermute | solution.py:23
  94.0 6.0 %collective-permute-start.19 = (bf16[16,32,128]{2,1,0:T(8,128)(2,1)S(1)}, bf16[16,32,128]{2,1,0:T(8,128)(2,1)S(1)}, u32[]{:S(2)}, u32[]{:S(2)}) collective-permute-start(bf16[16,32,128]{2,1,0:T(8,128)(2,1)S(1)} %get-tuple-element.51.own_ref), channel_id=1, source_target_pairs={{2,4},{4,2},{3,5},{5,3},{6,8},{8,6},{7,9},{9,7},{10,12},{12,10},{1... | collective-permute-start | bytes 393224 | tf_op jit(solution)/shard_map/ppermute | solution.py:23
  94.7 8.8 %collective-permute-start.18 = (bf16[16,32,128]{2,1,0:T(8,128)(2,1)S(1)}, bf16[16,32,128]{2,1,0:T(8,128)(2,1)S(1)}, u32[]{:S(2)}, u32[]{:S(2)}) collective-permute-start(bf16[16,32,128]{2,1,0:T(8,128)(2,1)S(1)} %get-tuple-element.51.own_ref), channel_id=1, source_target_pairs={{0,2},{2,0},{1,3},{3,1},{4,6},{6,4},{5,7},{7,5},{8,10},{10,8},{9,1... | collective-permute-start | bytes 393224 | tf_op jit(solution)/shard_map/ppermute | solution.py:23
  105.0 6.2 %collective-permute-start.21 = (bf16[16,32,128]{2,1,0:T(8,128)(2,1)S(1)}, bf16[16,32,128]{2,1,0:T(8,128)(2,1)S(1)}, u32[]{:S(2)}, u32[]{:S(2)}) collective-permute-start(bf16[16,32,128]{2,1,0:T(8,128)(2,1)S(1)} %get-tuple-element.53.own_ref), channel_id=1, source_target_pairs={{2,4},{4,2},{3,5},{5,3},{6,8},{8,6},{7,9},{9,7},{10,12},{12,10},{1... | collective-permute-start | bytes 393224 | tf_op jit(solution)/shard_map/ppermute | solution.py:23
  105.6 9.2 %collective-permute-start.20 = (bf16[16,32,128]{2,1,0:T(8,128)(2,1)S(1)}, bf16[16,32,128]{2,1,0:T(8,128)(2,1)S(1)}, u32[]{:S(2)}, u32[]{:S(2)}) collective-permute-start(bf16[16,32,128]{2,1,0:T(8,128)(2,1)S(1)} %get-tuple-element.53.own_ref), channel_id=1, source_target_pairs={{0,2},{2,0},{1,3},{3,1},{4,6},{6,4},{5,7},{7,5},{8,10},{10,8},{9,1... | collective-permute-start | bytes 393224 | tf_op jit(solution)/shard_map/ppermute | solution.py:23
  116.4 7.3 %collective-permute-start.23 = (bf16[16,32,128]{2,1,0:T(8,128)(2,1)S(1)}, bf16[16,32,128]{2,1,0:T(8,128)(2,1)S(1)}, u32[]{:S(2)}, u32[]{:S(2)}) collective-permute-start(bf16[16,32,128]{2,1,0:T(8,128)(2,1)S(1)} %get-tuple-element.55.own_ref), channel_id=1, source_target_pairs={{2,4},{4,2},{3,5},{5,3},{6,8},{8,6},{7,9},{9,7},{10,12},{12,10},{1... | collective-permute-start | bytes 393224 | tf_op jit(solution)/shard_map/ppermute | solution.py:23
  117.0 9.0 %collective-permute-start.22 = (bf16[16,32,128]{2,1,0:T(8,128)(2,1)S(1)}, bf16[16,32,128]{2,1,0:T(8,128)(2,1)S(1)}, u32[]{:S(2)}, u32[]{:S(2)}) collective-permute-start(bf16[16,32,128]{2,1,0:T(8,128)(2,1)S(1)} %get-tuple-element.55.own_ref), channel_id=1, source_target_pairs={{0,2},{2,0},{1,3},{3,1},{4,6},{6,4},{5,7},{7,5},{8,10},{10,8},{9,1... | collective-permute-start | bytes 393224 | tf_op jit(solution)/shard_map/ppermute | solution.py:23
  128.2 6.7 %collective-permute-start.25 = (bf16[16,32,128]{2,1,0:T(8,128)(2,1)S(1)}, bf16[16,32,128]{2,1,0:T(8,128)(2,1)S(1)}, u32[]{:S(2)}, u32[]{:S(2)}) collective-permute-start(bf16[16,32,128]{2,1,0:T(8,128)(2,1)S(1)} %get-tuple-element.57.own_ref), channel_id=1, source_target_pairs={{2,4},{4,2},{3,5},{5,3},{6,8},{8,6},{7,9},{9,7},{10,12},{12,10},{1... | collective-permute-start | bytes 393224 | tf_op jit(solution)/shard_map/ppermute | solution.py:23
  128.9 8.4 %collective-permute-start.24 = (bf16[16,32,128]{2,1,0:T(8,128)(2,1)S(1)}, bf16[16,32,128]{2,1,0:T(8,128)(2,1)S(1)}, u32[]{:S(2)}, u32[]{:S(2)}) collective-permute-start(bf16[16,32,128]{2,1,0:T(8,128)(2,1)S(1)} %get-tuple-element.57.own_ref), channel_id=1, source_target_pairs={{0,2},{2,0},{1,3},{3,1},{4,6},{6,4},{5,7},{7,5},{8,10},{10,8},{9,1... | collective-permute-start | bytes 393224 | tf_op jit(solution)/shard_map/ppermute | solution.py:23
  139.5 18.4 %collective-permute-start.26 = (f32[8,32,128]{2,1,0:T(8,128)S(1)}, f32[8,32,128]{2,1,0:T(8,128)S(1)}, u32[]{:S(2)}, u32[]{:S(2)}) collective-permute-start(f32[8,32,128]{2,1,0:T(8,128)S(1)} %get-tuple-element.62), channel_id=1, source_target_pairs={{0,1},{1,0},{2,3},{3,2},{4,5},{5,4},{6,7},{7,6},{8,9},{9,8},{10,11... | collective-permute-start | bytes 393224 | tf_op jit(solution)/shard_map/ppermute | solution.py:28

commit v3 on v2

v3 whole, which is shorter than its diff:
```python
import functools

import jax
import jax.numpy as jnp
from jax import lax
from jax.experimental import pallas as pl
from jax.experimental.pallas import tpu as pltpu
from jax.sharding import PartitionSpec as P

DEG = 12
AXES = ("rx", "ry")
VMEM = pl.BlockSpec(memory_space=pltpu.VMEM)
SMEM = pl.BlockSpec(memory_space=pltpu.SMEM)
LIMIT = 16 * 2**20


def traded(value, first):
    count = lax.axis_size(AXES)
    route = []
    for low in range(2 * first, count - 2, 4):
        for core in (0, 1):
            route += [(low + core, low + core + 2), (low + core + 2, low + core)]
    return lax.ppermute(value, AXES, route)


def paired(value):
    groups = []
    for low in range(0, lax.axis_size("ry"), 4):
        groups += [[low, low + 2], [low + 1, low + 3]]
    return lax.all_gather(value, "ry", axis_index_groups=groups)


def of_both_cores(value):
    count = lax.axis_size("ry")
    groups = [[low, low + 1] for low in range(0, count, 2)]
    return lax.all_gather(value, "ry", axis_index_groups=groups)


def swapped(value):
    count = lax.axis_size(AXES)
    return lax.ppermute(value, AXES, [(source, source ^ 1) for source in range(count)])


def turn_kernel(near_ref, far_ref, out_ref):
    rows, slots = near_ref.shape[:2]
    for row in range(rows):
        for slot in range(slots):
            out_ref[row, slot] = near_ref[row, slot].T
            out_ref[rows + row, slot] = far_ref[row, slot].T


def turned(near, far):
    return pl.pallas_call(
        turn_kernel,
        in_specs=[VMEM, VMEM],
        out_specs=VMEM,
        out_shape=jax.ShapeDtypeStruct((2 * near.shape[0],) + near.shape[1:], near.dtype),
        compiler_params=pltpu.CompilerParams(vmem_limit_bytes=LIMIT),
        name="turn_tiles",
    )(near, far)


def apply_tiles(index_ref, tiles_ref, window, older_ref, latest_ref, rounded_ref):
    count, slots = tiles_ref.shape[:2]
    for row in range(count):
        total = None
        for slot in range(0, slots, 2):
            vectors = jnp.concatenate(
                [window[index_ref[row, slot]], window[index_ref[row, slot + 1]]], axis=1
            )
            tiles = jnp.concatenate([tiles_ref[row, slot], tiles_ref[row, slot + 1]], axis=0)
            part = jnp.dot(vectors, tiles, preferred_element_type=jnp.float32)
            total = part if total is None else total + part
        if older_ref is not None:
            total = 2.0 * total - older_ref[row]
        if latest_ref is not None:
            latest_ref[row] = total
        if rounded_ref is not None:
            rounded_ref[row] = total.astype(jnp.bfloat16)


def first_kernel(
    index_ref, even_chip_ref, even_ref, own_ref, odd_ref, tiles_ref, latest_ref, rounded_ref, window
):
    count = odd_ref.shape[0]
    is_even = even_chip_ref[0] == 1
    own, even = own_ref[...], even_ref[...]
    window[0:count] = odd_ref[...]
    window[count : 2 * count] = jnp.where(is_even, own, even)
    window[2 * count : 3 * count] = jnp.where(is_even, even, own)
    apply_tiles(index_ref, tiles_ref, window, None, latest_ref, rounded_ref)


def step_kernel(keep, index_ref, pair_ref, odd_ref, tiles_ref, older_ref, *rest):
    latest_ref = rest[0] if keep[0] else None
    rounded_ref = rest[-2] if keep[1] else None
    window = rest[-1]
    count = odd_ref.shape[0]
    window[0:count] = odd_ref[...]
    window[count : 2 * count] = pair_ref[0]
    window[2 * count : 3 * count] = pair_ref[1]
    apply_tiles(index_ref, tiles_ref, window, older_ref, latest_ref, rounded_ref)


def stepped(kernel, name, scalars, blocks, keep=(True, True)):
    tiles = next(block for block in blocks if block.ndim == 4 and block.shape[-2] == block.shape[-1])
    shape = (tiles.shape[0], blocks[0].shape[-2], tiles.shape[2])
    kinds = [kind for kind, kept in zip((jnp.float32, jnp.bfloat16), keep) if kept]
    return pl.pallas_call(
        kernel,
        in_specs=[SMEM] * len(scalars) + [VMEM] * len(blocks),
        out_specs=[VMEM] * len(kinds),
        out_shape=[jax.ShapeDtypeStruct(shape, kind) for kind in kinds],
        scratch_shapes=[pltpu.VMEM((3 * shape[0],) + shape[1:], jnp.bfloat16)],
        compiler_params=pltpu.CompilerParams(vmem_limit_bytes=LIMIT),
        cost_estimate=pl.CostEstimate(
            flops=2 * shape[1] * tiles.size, bytes_accessed=2 * tiles.size, transcendentals=0
        ),
        name=name,
    )(*scalars, *blocks)


def gram_kernel(scale, core_ref, mine_ref, both_ref, block_ref, part_ref, wide):
    tiles, half, width = mine_ref.shape
    core = core_ref[0]
    even = core == 0
    for tile in range(tiles):
        mine, theirs = mine_ref[tile], both_ref[1 - core, (tile + tiles // 2) % tiles]
        columns = pl.ds(tile * width, width)
        wide[0:half, columns] = jnp.where(even, mine, theirs)
        wide[half : 2 * half, columns] = jnp.where(even, theirs, mine)
    block_ref[...] = wide[:, : tiles // 2 * width]
    mine = jnp.concatenate([mine_ref[tile] for tile in range(tiles)], axis=1)
    part = scale * lax.dot_general(
        mine,
        wide[...],
        (((1,), (1,)), ((), ())),
        precision=lax.Precision.HIGHEST,
        preferred_element_type=jnp.float32,
    )
    part = jnp.concatenate([part[: half // 2], part[half // 2 :]], axis=1)
    part_ref[...] = jnp.broadcast_to(part[None], part_ref.shape)


def gram_rows(core, mine, both, scale, copies):
    tiles, half, width = mine.shape
    return pl.pallas_call(
        functools.partial(gram_kernel, scale),
        in_specs=[SMEM, VMEM, VMEM],
        out_specs=[VMEM, VMEM],
        out_shape=[
            jax.ShapeDtypeStruct((2 * half, tiles // 2 * width), jnp.float32),
            jax.ShapeDtypeStruct((copies, half // 2, 4 * half), jnp.float32),
        ],
        scratch_shapes=[pltpu.VMEM((2 * half, tiles * width), jnp.float32)],
        compiler_params=pltpu.CompilerParams(vmem_limit_bytes=LIMIT),
        name="gram",
    )(core, mine, both)


def sum_kernel(parts_ref, out_ref):
    parts = [parts_ref[at] for at in range(parts_ref.shape[0])]
    while len(parts) > 1:
        parts = [one + other for one, other in zip(parts[::2], parts[1::2])]
    out_ref[...] = jnp.broadcast_to(parts[0][None], out_ref.shape)


def summed(parts, copies):
    return pl.pallas_call(
        sum_kernel,
        in_specs=[VMEM],
        out_specs=VMEM,
        out_shape=jax.ShapeDtypeStruct((copies,) + parts.shape[1:], parts.dtype),
        compiler_params=pltpu.CompilerParams(vmem_limit_bytes=LIMIT),
        name="sum_parts",
    )(parts)


def finish_kernel(gram_ref, block_ref, basis_ref, factor_ref, rows):
    size = block_ref.shape[0]
    quarter = size // 4
    lane_of = lax.broadcasted_iota(jnp.int32, (8, 2 * size), 1)
    row_of = lax.broadcasted_iota(jnp.int32, (8, 2 * size), 0)
    groups = []
    for group in range(size // 8):
        core, row = divmod(8 * group, 2 * quarter)
        part, row = divmod(row, quarter)
        stored = gram_ref[core, row : row + 8, part * size : (part + 1) * size]
        unit = (lane_of == row_of + (8 * group + size)).astype(jnp.float32)
        groups.append(jnp.concatenate([stored, unit[:, size:]], axis=1))
    def spread(value):
        return jnp.broadcast_to(value, (8, 2 * size))

    for pivot in range(0, size, 2):
        at, inner = divmod(pivot, 8)
        own = groups[at]
        one, two = spread(own[inner : inner + 1, :]), spread(own[inner + 1 : inner + 2, :])
        firsts = [spread(group[:, pivot : pivot + 1]) for group in groups[at:]]
        seconds = [spread(group[:, pivot + 1 : pivot + 2]) for group in groups[at:]]
        corner, off = spread(firsts[0][inner : inner + 1, :]), spread(seconds[0][inner : inner + 1, :])
        other = spread(seconds[0][inner + 1 : inner + 2, :])
        inverse = 1.0 / (corner * other - off * off)
        left = (other * one - off * two) * inverse
        right = (corner * two - off * one) * inverse
        for group in range(at, size // 8):
            if group == at and inner == 6:
                continue
            first, second = firsts[group - at], seconds[group - at]
            if group == at:
                below = row_of > inner + 1
                first, second = jnp.where(below, first, 0.0), jnp.where(below, second, 0.0)
            groups[group] = groups[group] - (first * left + second * right)
        rows[pivot : pivot + 1, :] = (one * lax.rsqrt(corner))[0:1]
        ratio = off / corner
        rows[pivot + 1 : pivot + 2, :] = ((two - ratio * one) * lax.rsqrt(other - ratio * off))[0:1]
    upper = lax.broadcasted_iota(jnp.int32, (size, size), 0) <= lax.broadcasted_iota(
        jnp.int32, (size, size), 1
    )
    done = rows[...]
    factor_ref[...] = jnp.where(upper, done[:, :size], 0.0)
    basis_ref[...] = jnp.dot(
        done[:, size:],
        block_ref[...],
        precision=lax.Precision.HIGHEST,
        preferred_element_type=jnp.float32,
    )


def finish(gram, block):
    size = block.shape[0]
    return pl.pallas_call(
        finish_kernel,
        in_specs=[VMEM, VMEM],
        out_specs=[VMEM, VMEM],
        out_shape=[
            jax.ShapeDtypeStruct(block.shape, jnp.float32),
            jax.ShapeDtypeStruct((size, size), jnp.float32),
        ],
        scratch_shapes=[pltpu.VMEM((size, 2 * size), jnp.float32)],
        compiler_params=pltpu.CompilerParams(vmem_limit_bytes=LIMIT),
        name="factor_and_solve",
    )(gram, block)


def shards(start_block, operator_tiles, tile_pattern):
    vectors, node_count = start_block.shape
    rows_local, _, tile_size = operator_tiles.shape[:3]
    half = vectors // 2
    device_count = lax.axis_size(AXES)
    position = lax.axis_index(AXES)
    chip, core = position // 2, position % 2
    chip_rows = 2 * rows_local

    row_ids = jnp.arange(rows_local, dtype=jnp.int32)[:, None]
    away = tile_pattern - (position * rows_local + row_ids)
    start_tiles = start_block.reshape(vectors, rows_local, tile_size).transpose(1, 0, 2)
    low, high = start_tiles[:, :half], start_tiles[:, half:]
    slots = away.shape[1]
    packed = jnp.zeros((1, half, tile_size), jnp.bfloat16)
    packed = packed.at[0, :rows_local, :slots].set(away.astype(jnp.bfloat16))
    theirs = swapped(jnp.concatenate([jnp.where(core == 0, high, low), packed], axis=0))
    rounded = jnp.concatenate([jnp.where(core == 0, low, high), theirs[:rows_local]], axis=0)
    far_away = theirs[rows_local, :rows_local, :slots].astype(jnp.int32)

    tiles = turned(operator_tiles, swapped(operator_tiles))

    far_rows = (position ^ 1) * rows_local + row_ids
    columns = jnp.concatenate([tile_pattern, far_away + far_rows], axis=0)
    index = jnp.clip(columns - (chip - 1) * chip_rows, 0, 3 * chip_rows - 1)
    place, inner = index // chip_rows, (index % chip_rows) ^ (core * rows_local)
    index = jnp.where(chip % 2 == 1, (place + 1) % 3, place) * chip_rows + inner

    earlier = rounded.astype(jnp.float32)
    even_chip = (1 - chip % 2).reshape(1)
    latest, rounded = stepped(
        first_kernel,
        "first_step",
        (index, even_chip),
        (traded(rounded, 0), rounded, traded(rounded, 1), tiles),
    )
    for degree in range(2, DEG + 1):
        keep = (degree != DEG - 1, degree != DEG)
        made = stepped(
            functools.partial(step_kernel, keep),
            "step",
            (index,),
            (paired(rounded), traded(rounded, 1), tiles, earlier),
            keep,
        )
        earlier, latest, rounded = latest, made[0], made[-1]

    inner, outer = lax.axis_size("ry") // 2, lax.axis_size("rx")
    block, parts = gram_rows(
        core.reshape(1), latest, of_both_cores(latest), 1.0 / (node_count * device_count), inner
    )
    same_core = [list(range(low, 2 * inner, 2)) for low in (0, 1)]
    parts = lax.all_to_all(parts, "ry", 0, 0, axis_index_groups=same_core, tiled=True)
    parts = lax.all_to_all(summed(parts, outer), "rx", 0, 0, tiled=True)
    return tuple(finish(of_both_cores(summed(parts, 1)[0]), block))


def solution(mesh):
    return jax.shard_map(
        shards,
        mesh=mesh,
        in_specs=(P(None, AXES), P(AXES, None, None, None), P(AXES, None)),
        out_specs=(P(None, AXES), P()),
        check_vma=False,
    )
```

time: 234 us -> 222 us (0.949)
  blocking collectives: 67.5 us -> 167 us
  starting transfers between devices: 101 us -> 20.8 us
  waiting for transfers between devices: 32 us -> 2.52 us
    all_gather x0 -> x13, blocking collectives: none -> 101 us  [the longest x11 78.8 us: paired(): return lax.all_gather(value, 'ry', axis_index_groups=groups)]
    ppermute x24 -> x13, starting transfers between devices: 73 us -> 9.95 us  [traded(): return lax.ppermute(value, AXES, route)]
    ppermute x24 -> x13, waiting for transfers between devices: 29.8 us -> 1.33 us  [traded(): return lax.ppermute(value, AXES, route)]
    ppermute x3 -> x2, starting transfers between devices: 28.3 us -> 10.8 us  [swapped(): lax.ppermute(value, AXES, [(source, source ^ 1) for source in range(count)])]
    pallas_call x13 -> x15, Pallas kernels: 19.5 us -> 18.5 us  [the longest x12 17.9 us: stepped(): pl.pallas_call(kernel, in_specs=[SMEM] * len(scalars) + [VMEM] * len(bloc...]
    all_to_all x3 -> x2, blocking collectives: 67.5 us -> 66.7 us  [the longest x1 50.1 us: shards(): parts = lax.all_to_all(summed(parts, outer), 'rx', 0, 0, tiled=True)]
  transfers between devices with their start and end apart: 27 -> 15, of which waited for: 14 -> 2; matrix products, arithmetic and copies ran while one was open for 1% -> 1% of each run, Pallas kernels for 0% -> 1%
where the time goes in v3:
time: 222 us; the launch traced here: 220 us
  blocking collectives  167 us (75%)
  Pallas kernels  25.1 us (11%)
  starting transfers between devices  20.8 us (9%)
  waiting for transfers between devices  2.52 us (1%)
    all_gather x11, blocking collectives, paired(): return lax.all_gather(value, 'ry', axis_index_groups=groups)  78.8 us
    all_to_all x1, blocking collectives, shards(): parts = lax.all_to_all(summed(parts, outer), 'rx', 0, 0, tiled=True)  50.1 us
    all_gather x2, blocking collectives, of_both_cores(): return lax.all_gather(value, 'ry', axis_index_groups=groups)  22 us
    pallas_call x12, Pallas kernels, stepped(): pl.pallas_call(kernel, in_specs=[SMEM] * len(scalars) + [VMEM] * len(bloc...  17.9 us
    all_to_all x1, blocking collectives, shards(): lax.all_to_all(parts, 'ry', 0, 0, axis_index_groups=same_core, tiled=True)  16.5 us
    ppermute x2, starting transfers between devices, swapped(): lax.ppermute(value, AXES, [(source, source ^ 1) for source in range(count)])  10.8 us
    ppermute x13, starting transfers between devices, traded(): return lax.ppermute(value, AXES, route)  9.95 us
    pallas_call x1, Pallas kernels, finish(): pl.pallas_call(finish_kernel, in_specs=[VMEM, VMEM], out_specs=[VMEM, VME...  5.42 us
  transfers between devices with their start and end apart: 15, of which 2 were waited for; matrix products, arithmetic and copies ran while one was open for 1% of the time, Pallas kernels for 1%

profile of v3, /device:TPU:1, one launch (start us, length us, event | category | flops | bytes accessed | tf_op | source)
XLA Modules:
  0.0 220.0 jit_solution(13712543481794056531)
XLA Ops:
  0.6 0.0 copy-start
  0.6 8.9 %collective-permute-start.3 = (bf16[8,8,128,128]{3,2,1,0:T(8,128)(2,1)}, bf16[8,8,128,128]{3,2,1,0:T(8,128)(2,1)S(1)}, u32[]{:S(2)}, u32[]{:S(2)}) collective-permute-start(bf16[8,8,128,128]{3,2,1,0:T(8,128)(2,1)} %near_ref.1), channel_id=1, source_target_pairs={{0,1},{1,0},{2,3},{3,2},{4,5},{5,4},{6,7},{7,6},{8,9},{9,8},{10,11... | collective-permute-start | bytes 6291464 | tf_op jit(solution)/shard_map/ppermute | solution.py:41
  9.6 0.8 fusion.12
  10.4 1.9 collective-permute-start
  12.4 1.2 collective-permute-done
  13.6 0.7 collective-permute-start.2
  14.3 1.9 collective-permute-start.1
  16.2 0.1 convert_add_fusion
  16.3 0.7 fusion.4.index_ref
  17.0 0.0 collective-permute-done.3.far_ref
  17.0 0.0 copy-start.1
  17.0 1.6 copy-done.1
  18.6 1.1 turn_tiles.1.tiles_ref
  19.8 0.0 collective-permute-done.2.odd_ref
  19.8 1.3 collective-permute-done.1.even_ref
  21.1 1.5 first_step.1
  22.6 0.7 collective-permute-start.4
  23.3 5.5 %all-gather = bf16[32,32,128]{2,1,0:T(8,128)(2,1)S(1)} all-gather(bf16[16,32,128]{2,1,0:T(8,128)(2,1)S(1)} %get-tuple-element.36), channel_id=2, replica_groups={{0,2},{1,3},{4,6},{5,7},{8,10},{9,11},{12,14},{13,15},{16,18},{17,19},{..., dimensions={0}, use_global_device_ids=true | all-gather | bytes 393216 | tf_op jit(solution)/shard_map/all_gather | solution.py:30
  28.8 0.0 collective-permute-done.4.odd_ref
  28.8 1.5 step.11
  30.3 0.7 collective-permute-start.5
  31.0 6.4 %all-gather.1 = bf16[32,32,128]{2,1,0:T(8,128)(2,1)S(1)} all-gather(bf16[16,32,128]{2,1,0:T(8,128)(2,1)S(1)} %get-tuple-element.37), channel_id=3, replica_groups={{0,2},{1,3},{4,6},{5,7},{8,10},{9,11},{12,14},{13,15},{16,18},{17,19},{..., dimensions={0}, use_global_device_ids=true | all-gather | bytes 393216 | tf_op jit(solution)/shard_map/all_gather | solution.py:30
  37.4 0.0 collective-permute-done.5.odd_ref
  37.4 1.5 step.12
  38.9 0.7 collective-permute-start.6
  39.6 7.3 %all-gather.2 = bf16[32,32,128]{2,1,0:T(8,128)(2,1)S(1)} all-gather(bf16[16,32,128]{2,1,0:T(8,128)(2,1)S(1)} %get-tuple-element.39), channel_id=4, replica_groups={{0,2},{1,3},{4,6},{5,7},{8,10},{9,11},{12,14},{13,15},{16,18},{17,19},{..., dimensions={0}, use_global_device_ids=true | all-gather | bytes 393216 | tf_op jit(solution)/shard_map/all_gather | solution.py:30
  46.9 0.0 collective-permute-done.6.odd_ref
  46.9 1.5 step.13
  48.4 0.7 collective-permute-start.7
  49.1 5.9 %all-gather.3 = bf16[32,32,128]{2,1,0:T(8,128)(2,1)S(1)} all-gather(bf16[16,32,128]{2,1,0:T(8,128)(2,1)S(1)} %get-tuple-element.41), channel_id=5, replica_groups={{0,2},{1,3},{4,6},{5,7},{8,10},{9,11},{12,14},{13,15},{16,18},{17,19},{..., dimensions={0}, use_global_device_ids=true | all-gather | bytes 393216 | tf_op jit(solution)/shard_map/all_gather | solution.py:30
  55.0 0.0 collective-permute-done.7.odd_ref
  55.0 1.5 step.14
  56.5 0.7 collective-permute-start.8
  57.2 8.2 %all-gather.4 = bf16[32,32,128]{2,1,0:T(8,128)(2,1)S(1)} all-gather(bf16[16,32,128]{2,1,0:T(8,128)(2,1)S(1)} %get-tuple-element.43), channel_id=6, replica_groups={{0,2},{1,3},{4,6},{5,7},{8,10},{9,11},{12,14},{13,15},{16,18},{17,19},{..., dimensions={0}, use_global_device_ids=true | all-gather | bytes 393216 | tf_op jit(solution)/shard_map/all_gather | solution.py:30
  65.4 0.0 collective-permute-done.8.odd_ref
  65.4 1.5 step.15
  66.9 0.7 collective-permute-start.9
  67.5 6.2 %all-gather.5 = bf16[32,32,128]{2,1,0:T(8,128)(2,1)S(1)} all-gather(bf16[16,32,128]{2,1,0:T(8,128)(2,1)S(1)} %get-tuple-element.45), channel_id=7, replica_groups={{0,2},{1,3},{4,6},{5,7},{8,10},{9,11},{12,14},{13,15},{16,18},{17,19},{..., dimensions={0}, use_global_device_ids=true | all-gather | bytes 393216 | tf_op jit(solution)/shard_map/all_gather | solution.py:30
  73.8 0.0 collective-permute-done.9.odd_ref
  73.8 1.5 step.16
  75.3 0.7 collective-permute-start.10
  76.0 7.9 %all-gather.6 = bf16[32,32,128]{2,1,0:T(8,128)(2,1)S(1)} all-gather(bf16[16,32,128]{2,1,0:T(8,128)(2,1)S(1)} %get-tuple-element.47), channel_id=8, replica_groups={{0,2},{1,3},{4,6},{5,7},{8,10},{9,11},{12,14},{13,15},{16,18},{17,19},{..., dimensions={0}, use_global_device_ids=true | all-gather | bytes 393216 | tf_op jit(solution)/shard_map/all_gather | solution.py:30
  83.9 0.0 collective-permute-done.10.odd_ref
  83.9 1.5 step.17
  85.3 0.7 collective-permute-start.11
  86.0 8.8 %all-gather.7 = bf16[32,32,128]{2,1,0:T(8,128)(2,1)S(1)} all-gather(bf16[16,32,128]{2,1,0:T(8,128)(2,1)S(1)} %get-tuple-element.49), channel_id=9, replica_groups={{0,2},{1,3},{4,6},{5,7},{8,10},{9,11},{12,14},{13,15},{16,18},{17,19},{..., dimensions={0}, use_global_device_ids=true | all-gather | bytes 393216 | tf_op jit(solution)/shard_map/all_gather | solution.py:30
  94.8 0.0 collective-permute-done.11.odd_ref
  94.8 1.5 step.18
  96.3 0.7 collective-permute-start.12
  97.0 6.3 %all-gather.8 = bf16[32,32,128]{2,1,0:T(8,128)(2,1)S(1)} all-gather(bf16[16,32,128]{2,1,0:T(8,128)(2,1)S(1)} %get-tuple-element.51), channel_id=10, replica_groups={{0,2},{1,3},{4,6},{5,7},{8,10},{9,11},{12,14},{13,15},{16,18},{17,19},{..., dimensions={0}, use_global_device_ids=true | all-gather | bytes 393216 | tf_op jit(solution)/shard_map/all_gather | solution.py:30
  103.3 1.5 step.19
  104.8 0.7 collective-permute-start.13
  105.4 7.8 %all-gather.9 = bf16[32,32,128]{2,1,0:T(8,128)(2,1)S(1)} all-gather(bf16[16,32,128]{2,1,0:T(8,128)(2,1)S(1)} %get-tuple-element.53), channel_id=11, replica_groups={{0,2},{1,3},{4,6},{5,7},{8,10},{9,11},{12,14},{13,15},{16,18},{17,19},{..., dimensions={0}, use_global_device_ids=true | all-gather | bytes 393216 | tf_op jit(solution)/shard_map/all_gather | solution.py:30
  113.3 0.0 collective-permute-done.13.odd_ref
  113.3 1.5 step.20
  114.7 0.7 collective-permute-start.14
  115.4 8.4 %all-gather.10 = bf16[32,32,128]{2,1,0:T(8,128)(2,1)S(1)} all-gather(bf16[16,32,128]{2,1,0:T(8,128)(2,1)S(1)} %step.20), channel_id=12, replica_groups={{0,2},{1,3},{4,6},{5,7},{8,10},{9,11},{12,14},{13,15},{16,18},{17,19},{..., dimensions={0}, use_global_device_ids=true | all-gather | bytes 393216 | tf_op jit(solution)/shard_map/all_gather | solution.py:30
  123.8 1.5 step.21.mine_ref
  125.3 16.7 %all-gather.11 = f32[32,32,128]{2,1,0:T(8,128)S(1)} all-gather(f32[16,32,128]{2,1,0:T(8,128)S(1)} %step.21.mine_ref), channel_id=13, replica_groups={{0,1},{2,3},{4,5},{6,7},{8,9},{10,11},{12,13},{14,15},{16,17},{18,19},{..., dimensions={0}, use_global_device_ids=true | all-gather | bytes 786432 | tf_op jit(solution)/shard_map/all_gather | solution.py:36
  142.0 0.6 gram.1
  142.6 16.5 %all_to_all.10.parts_ref = f32[8,16,128]{2,1,0:T(8,128)S(1)} all-to-all(f32[8,16,128]{2,1,0:T(8,128)S(1)} %get-tuple-element.56), channel_id=1, replica_groups={{0,2,4,6,8,10,12,14},{1,3,5,7,9,11,13,15},{16,18,20,22,24,26,28,30},{17..., dimensions={0} | all-to-all | bytes 131072 | tf_op jit(solution)/shard_map/all_to_all | solution.py:297
  159.2 50.1 %all_to_all.11.parts_ref = f32[32,16,128]{2,1,0:T(8,128)S(1)} all-to-all(f32[32,16,128]{2,1,0:T(8,128)S(1)} %sum_parts.2), channel_id=1, replica_groups=mesh['rx'=32,'ry'=16] {'rx'}, dimensions={0} | all-to-all | bytes 524288 | tf_op jit(solution)/shard_map/all_to_all | solution.py:298
  209.3 5.3 %all_gather.99.gram_ref = f32[2,16,128]{2,1,0:T(8,128)S(1)} all-gather(f32[1,16,128]{2,1,0:T(8,128)S(1)} %sum_parts.3), channel_id=1, replica_groups={{0,1},{2,3},{4,5},{6,7},{8,9},{10,11},{12,13},{14,15},{16,17},{18,19},{..., dimensions={0}, use_global_device_ids=true | all-gather | bytes 24576 | tf_op jit(solution)/shard_map/all_gather | solution.py:36
  214.6 5.4 %factor_and_solve.1 = (f32[64,1024]{1,0:T(8,128)}, f32[64,64]{1,0:T(8,128)}) custom-call(f32[2,16,128]{2,1,0:T(8,128)S(1)} %all_gather.99.gram_ref, f32[64,1024]{1,0:T(8,128)S(1)} %get-tuple-element.57.block_ref), custom_call_target="tpu_custom_call" | custom-call | tf_op jit(solution)/shard_map/factor_and_solve/pallas_call | solution.py:231
  (12 shorter events, 0.1 us)
Async XLA Ops:
  0.6 9.7 %copy-start = (bf16[64,1024]{1,0:T(8,128)(2,1)S(1)}, bf16[64,1024]{1,0:T(8,128)(2,1)}, u32[]{:S(2)}) copy-start(bf16[64,1024]{1,0:T(8,128)(2,1)} %param.5) | copy-start | bytes 393220
  0.6 16.4 %collective-permute-start.3 = (bf16[8,8,128,128]{3,2,1,0:T(8,128)(2,1)}, bf16[8,8,128,128]{3,2,1,0:T(8,128)(2,1)S(1)}, u32[]{:S(2)}, u32[]{:S(2)}) collective-permute-start(bf16[8,8,128,128]{3,2,1,0:T(8,128)(2,1)} %near_ref.1), channel_id=1, source_target_pairs={{0,1},{1,0},{2,3},{3,2},{4,5},{5,4},{6,7},{7,6},{8,9},{9,8},{10,11... | collective-permute-start | bytes 6291464 | tf_op jit(solution)/shard_map/ppermute | solution.py:41
  10.4 3.2 %collective-permute-start = (bf16[9,32,128]{2,1,0:T(8,128)(2,1)S(1)}, bf16[9,32,128]{2,1,0:T(8,128)(2,1)S(1)}, u32[]{:S(2)}, u32[]{:S(2)}) collective-permute-start(bf16[9,32,128]{2,1,0:T(8,128)(2,1)S(1)} %fusion.1), channel_id=1, source_target_pairs={{0,1},{1,0},{2,3},{3,2},{4,5},{5,4},{6,7},{7,6},{8,9},{9,8},{10,11... | collective-permute-start | bytes 221192 | tf_op jit(solution)/shard_map/ppermute | solution.py:41
  13.6 6.1 %collective-permute-start.2 = (bf16[16,32,128]{2,1,0:T(8,128)(2,1)S(1)}, bf16[16,32,128]{2,1,0:T(8,128)(2,1)S(1)}, u32[]{:S(2)}, u32[]{:S(2)}) collective-permute-start(bf16[16,32,128]{2,1,0:T(8,128)(2,1)S(1)} %get-tuple-element.59.own_ref), channel_id=1, source_target_pairs={{2,4},{4,2},{3,5},{5,3},{6,8},{8,6},{7,9},{9,7},{10,12},{12,10},{1... | collective-permute-start | bytes 393224 | tf_op jit(solution)/shard_map/ppermute | solution.py:23
  14.3 6.8 %collective-permute-start.1 = (bf16[16,32,128]{2,1,0:T(8,128)(2,1)S(1)}, bf16[16,32,128]{2,1,0:T(8,128)(2,1)S(1)}, u32[]{:S(2)}, u32[]{:S(2)}) collective-permute-start(bf16[16,32,128]{2,1,0:T(8,128)(2,1)S(1)} %get-tuple-element.59.own_ref), channel_id=1, source_target_pairs={{0,2},{2,0},{1,3},{3,1},{4,6},{6,4},{5,7},{7,5},{8,10},{10,8},{9,1... | collective-permute-start | bytes 393224 | tf_op jit(solution)/shard_map/ppermute | solution.py:23
  17.0 1.6 copy-start.1
  22.6 6.2 %collective-permute-start.4 = (bf16[16,32,128]{2,1,0:T(8,128)(2,1)S(1)}, bf16[16,32,128]{2,1,0:T(8,128)(2,1)S(1)}, u32[]{:S(2)}, u32[]{:S(2)}) collective-permute-start(bf16[16,32,128]{2,1,0:T(8,128)(2,1)S(1)} %get-tuple-element.36), channel_id=1, source_target_pairs={{2,4},{4,2},{3,5},{5,3},{6,8},{8,6},{7,9},{9,7},{10,12},{12,10},{1... | collective-permute-start | bytes 393224 | tf_op jit(solution)/shard_map/ppermute | solution.py:23
  30.3 7.1 %collective-permute-start.5 = (bf16[16,32,128]{2,1,0:T(8,128)(2,1)S(1)}, bf16[16,32,128]{2,1,0:T(8,128)(2,1)S(1)}, u32[]{:S(2)}, u32[]{:S(2)}) collective-permute-start(bf16[16,32,128]{2,1,0:T(8,128)(2,1)S(1)} %get-tuple-element.37), channel_id=1, source_target_pairs={{2,4},{4,2},{3,5},{5,3},{6,8},{8,6},{7,9},{9,7},{10,12},{12,10},{1... | collective-permute-start | bytes 393224 | tf_op jit(solution)/shard_map/ppermute | solution.py:23
  38.9 8.0 %collective-permute-start.6 = (bf16[16,32,128]{2,1,0:T(8,128)(2,1)S(1)}, bf16[16,32,128]{2,1,0:T(8,128)(2,1)S(1)}, u32[]{:S(2)}, u32[]{:S(2)}) collective-permute-start(bf16[16,32,128]{2,1,0:T(8,128)(2,1)S(1)} %get-tuple-element.39), channel_id=1, source_target_pairs={{2,4},{4,2},{3,5},{5,3},{6,8},{8,6},{7,9},{9,7},{10,12},{12,10},{1... | collective-permute-start | bytes 393224 | tf_op jit(solution)/shard_map/ppermute | solution.py:23
  48.4 6.6 %collective-permute-start.7 = (bf16[16,32,128]{2,1,0:T(8,128)(2,1)S(1)}, bf16[16,32,128]{2,1,0:T(8,128)(2,1)S(1)}, u32[]{:S(2)}, u32[]{:S(2)}) collective-permute-start(bf16[16,32,128]{2,1,0:T(8,128)(2,1)S(1)} %get-tuple-element.41), channel_id=1, source_target_pairs={{2,4},{4,2},{3,5},{5,3},{6,8},{8,6},{7,9},{9,7},{10,12},{12,10},{1... | collective-permute-start | bytes 393224 | tf_op jit(solution)/shard_map/ppermute | solution.py:23
  56.5 8.9 %collective-permute-start.8 = (bf16[16,32,128]{2,1,0:T(8,128)(2,1)S(1)}, bf16[16,32,128]{2,1,0:T(8,128)(2,1)S(1)}, u32[]{:S(2)}, u32[]{:S(2)}) collective-permute-start(bf16[16,32,128]{2,1,0:T(8,128)(2,1)S(1)} %get-tuple-element.43), channel_id=1, source_target_pairs={{2,4},{4,2},{3,5},{5,3},{6,8},{8,6},{7,9},{9,7},{10,12},{12,10},{1... | collective-permute-start | bytes 393224 | tf_op jit(solution)/shard_map/ppermute | solution.py:23
  66.9 6.9 %collective-permute-start.9 = (bf16[16,32,128]{2,1,0:T(8,128)(2,1)S(1)}, bf16[16,32,128]{2,1,0:T(8,128)(2,1)S(1)}, u32[]{:S(2)}, u32[]{:S(2)}) collective-permute-start(bf16[16,32,128]{2,1,0:T(8,128)(2,1)S(1)} %get-tuple-element.45), channel_id=1, source_target_pairs={{2,4},{4,2},{3,5},{5,3},{6,8},{8,6},{7,9},{9,7},{10,12},{12,10},{1... | collective-permute-start | bytes 393224 | tf_op jit(solution)/shard_map/ppermute | solution.py:23
  75.3 8.6 %collective-permute-start.10 = (bf16[16,32,128]{2,1,0:T(8,128)(2,1)S(1)}, bf16[16,32,128]{2,1,0:T(8,128)(2,1)S(1)}, u32[]{:S(2)}, u32[]{:S(2)}) collective-permute-start(bf16[16,32,128]{2,1,0:T(8,128)(2,1)S(1)} %get-tuple-element.47), channel_id=1, source_target_pairs={{2,4},{4,2},{3,5},{5,3},{6,8},{8,6},{7,9},{9,7},{10,12},{12,10},{1... | collective-permute-start | bytes 393224 | tf_op jit(solution)/shard_map/ppermute | solution.py:23
  85.3 9.4 %collective-permute-start.11 = (bf16[16,32,128]{2,1,0:T(8,128)(2,1)S(1)}, bf16[16,32,128]{2,1,0:T(8,128)(2,1)S(1)}, u32[]{:S(2)}, u32[]{:S(2)}) collective-permute-start(bf16[16,32,128]{2,1,0:T(8,128)(2,1)S(1)} %get-tuple-element.49), channel_id=1, source_target_pairs={{2,4},{4,2},{3,5},{5,3},{6,8},{8,6},{7,9},{9,7},{10,12},{12,10},{1... | collective-permute-start | bytes 393224 | tf_op jit(solution)/shard_map/ppermute | solution.py:23
  96.3 7.0 %collective-permute-start.12 = (bf16[16,32,128]{2,1,0:T(8,128)(2,1)S(1)}, bf16[16,32,128]{2,1,0:T(8,128)(2,1)S(1)}, u32[]{:S(2)}, u32[]{:S(2)}) collective-permute-start(bf16[16,32,128]{2,1,0:T(8,128)(2,1)S(1)} %get-tuple-element.51), channel_id=1, source_target_pairs={{2,4},{4,2},{3,5},{5,3},{6,8},{8,6},{7,9},{9,7},{10,12},{12,10},{1... | collective-permute-start | bytes 393224 | tf_op jit(solution)/shard_map/ppermute | solution.py:23
  104.8 8.5 %collective-permute-start.13 = (bf16[16,32,128]{2,1,0:T(8,128)(2,1)S(1)}, bf16[16,32,128]{2,1,0:T(8,128)(2,1)S(1)}, u32[]{:S(2)}, u32[]{:S(2)}) collective-permute-start(bf16[16,32,128]{2,1,0:T(8,128)(2,1)S(1)} %get-tuple-element.53), channel_id=1, source_target_pairs={{2,4},{4,2},{3,5},{5,3},{6,8},{8,6},{7,9},{9,7},{10,12},{12,10},{1... | collective-permute-start | bytes 393224 | tf_op jit(solution)/shard_map/ppermute | solution.py:23
  114.7 9.1 %collective-permute-start.14 = (bf16[16,32,128]{2,1,0:T(8,128)(2,1)S(1)}, bf16[16,32,128]{2,1,0:T(8,128)(2,1)S(1)}, u32[]{:S(2)}, u32[]{:S(2)}) collective-permute-start(bf16[16,32,128]{2,1,0:T(8,128)(2,1)S(1)} %step.20), channel_id=1, source_target_pairs={{2,4},{4,2},{3,5},{5,3},{6,8},{8,6},{7,9},{9,7},{10,12},{12,10},{1... | collective-permute-start | bytes 393224 | tf_op jit(solution)/shard_map/ppermute | solution.py:23

commit v4 on v3

--- a/solution.py
+++ b/solution.py
@@ -10,7 +10,6 @@
 DEG = 12
 AXES = ("rx", "ry")
 VMEM = pl.BlockSpec(memory_space=pltpu.VMEM)
-SMEM = pl.BlockSpec(memory_space=pltpu.SMEM)
 LIMIT = 16 * 2**20
 
 
@@ -83,7 +82,7 @@
     index_ref, even_chip_ref, even_ref, own_ref, odd_ref, tiles_ref, latest_ref, rounded_ref, window
 ):
     count = odd_ref.shape[0]
-    is_even = even_chip_ref[0] == 1
+    is_even = even_chip_ref[0, 0] == 1
     own, even = own_ref[...], even_ref[...]
     window[0:count] = odd_ref[...]
     window[count : 2 * count] = jnp.where(is_even, own, even)
@@ -108,7 +107,7 @@
     kinds = [kind for kind, kept in zip((jnp.float32, jnp.bfloat16), keep) if kept]
     return pl.pallas_call(
         kernel,
-        in_specs=[SMEM] * len(scalars) + [VMEM] * len(blocks),
+        in_specs=[VMEM] * (len(scalars) + len(blocks)),
         out_specs=[VMEM] * len(kinds),
         out_shape=[jax.ShapeDtypeStruct(shape, kind) for kind in kinds],
         scratch_shapes=[pltpu.VMEM((3 * shape[0],) + shape[1:], jnp.bfloat16)],
@@ -122,7 +121,7 @@
 
 def gram_kernel(scale, core_ref, mine_ref, both_ref, block_ref, part_ref, wide):
     tiles, half, width = mine_ref.shape
-    core = core_ref[0]
+    core = core_ref[0, 0]
     even = core == 0
     for tile in range(tiles):
         mine, theirs = mine_ref[tile], both_ref[1 - core, (tile + tiles // 2) % tiles]
@@ -146,7 +145,7 @@
     tiles, half, width = mine.shape
     return pl.pallas_call(
         functools.partial(gram_kernel, scale),
-        in_specs=[SMEM, VMEM, VMEM],
+        in_specs=[VMEM, VMEM, VMEM],
         out_specs=[VMEM, VMEM],
         out_shape=[
             jax.ShapeDtypeStruct((2 * half, tiles // 2 * width), jnp.float32),
@@ -271,7 +270,7 @@
     index = jnp.where(chip % 2 == 1, (place + 1) % 3, place) * chip_rows + inner
 
     earlier = rounded.astype(jnp.float32)
-    even_chip = (1 - chip % 2).reshape(1)
+    even_chip = (1 - chip % 2).reshape(1, 1)
     latest, rounded = stepped(
         first_kernel,
         "first_step",
@@ -291,7 +290,7 @@
 
     inner, outer = lax.axis_size("ry") // 2, lax.axis_size("rx")
     block, parts = gram_rows(
-        core.reshape(1), latest, of_both_cores(latest), 1.0 / (node_count * device_count), inner
+        core.reshape(1, 1), latest, of_both_cores(latest), 1.0 / (node_count * device_count), inner
     )
     same_core = [list(range(low, 2 * inner, 2)) for low in (0, 1)]
     parts = lax.all_to_all(parts, "ry", 0, 0, axis_index_groups=same_core, tiled=True)

time: 222 us -> 214 us (0.964)
  Pallas kernels: 25.1 us -> 17.9 us
    pallas_call x13, Pallas kernels: 18.5 us -> 11.3 us  [the longest x12 10.7 us: stepped(): pl.pallas_call(kernel, in_specs=[VMEM] * (len(scalars) + len(blocks)), ou...]
where the time goes in v4:
time: 214 us; the launch traced here: 213 us
  blocking collectives  168 us (79%)
  starting transfers between devices  20.8 us (10%)
  Pallas kernels  17.9 us (8%)
  waiting for transfers between devices  2.52 us (1%)
    all_gather x11, blocking collectives, paired(): return lax.all_gather(value, 'ry', axis_index_groups=groups)  79.5 us
    all_to_all x1, blocking collectives, shards(): parts = lax.all_to_all(summed(parts, outer), 'rx', 0, 0, tiled=True)  50.6 us
    all_gather x2, blocking collectives, of_both_cores(): return lax.all_gather(value, 'ry', axis_index_groups=groups)  21.2 us
    all_to_all x1, blocking collectives, shards(): lax.all_to_all(parts, 'ry', 0, 0, axis_index_groups=same_core, tiled=True)  16.7 us
    ppermute x2, starting transfers between devices, swapped(): lax.ppermute(value, AXES, [(source, source ^ 1) for source in range(count)])  10.8 us
    pallas_call x12, Pallas kernels, stepped(): pl.pallas_call(kernel, in_specs=[VMEM] * (len(scalars) + len(blocks)), ou...  10.7 us
    ppermute x13, starting transfers between devices, traded(): return lax.ppermute(value, AXES, route)  9.95 us
    pallas_call x1, Pallas kernels, finish(): pl.pallas_call(finish_kernel, in_specs=[VMEM, VMEM], out_specs=[VMEM, VME...  5.43 us
  transfers between devices with their start and end apart: 15, of which 2 were waited for; matrix products, arithmetic and copies ran while one was open for 1% of the time, Pallas kernels for 1%

profile of v4, /device:TPU:1, one launch (start us, length us, event | category | flops | bytes accessed | tf_op | source)
XLA Modules:
  0.0 213.4 jit_solution(13013431452002971404)
XLA Ops:
  0.6 0.0 copy-start
  0.6 8.9 %collective-permute-start.3 = (bf16[8,8,128,128]{3,2,1,0:T(8,128)(2,1)}, bf16[8,8,128,128]{3,2,1,0:T(8,128)(2,1)S(1)}, u32[]{:S(2)}, u32[]{:S(2)}) collective-permute-start(bf16[8,8,128,128]{3,2,1,0:T(8,128)(2,1)} %near_ref.1), channel_id=1, source_target_pairs={{0,1},{1,0},{2,3},{3,2},{4,5},{5,4},{6,7},{7,6},{8,9},{9,8},{10,11... | collective-permute-start | bytes 6291464 | tf_op jit(solution)/shard_map/ppermute | solution.py:40
  9.6 0.8 fusion.12
  10.4 1.9 collective-permute-start
  12.4 1.2 collective-permute-done
  13.6 0.7 collective-permute-start.2
  14.3 1.9 collective-permute-start.1
  16.2 0.1 convert_add_fusion
  16.3 0.7 fusion.4.index_ref
  17.0 0.0 collective-permute-done.3.far_ref
  17.0 0.0 copy-start.1
  17.0 1.6 copy-done.1
  18.6 1.1 turn_tiles.1.tiles_ref
  19.8 0.0 collective-permute-done.2.odd_ref
  19.8 1.3 collective-permute-done.1.even_ref
  21.1 0.9 first_step.1
  22.0 0.7 collective-permute-start.4
  22.7 5.5 %all-gather = bf16[32,32,128]{2,1,0:T(8,128)(2,1)S(1)} all-gather(bf16[16,32,128]{2,1,0:T(8,128)(2,1)S(1)} %get-tuple-element.36), channel_id=2, replica_groups={{0,2},{1,3},{4,6},{5,7},{8,10},{9,11},{12,14},{13,15},{16,18},{17,19},{..., dimensions={0}, use_global_device_ids=true | all-gather | bytes 393216 | tf_op jit(solution)/shard_map/all_gather | solution.py:29
  28.2 0.0 collective-permute-done.4.odd_ref
  28.2 0.9 step.11
  29.1 0.7 collective-permute-start.5
  29.8 6.4 %all-gather.1 = bf16[32,32,128]{2,1,0:T(8,128)(2,1)S(1)} all-gather(bf16[16,32,128]{2,1,0:T(8,128)(2,1)S(1)} %get-tuple-element.37), channel_id=3, replica_groups={{0,2},{1,3},{4,6},{5,7},{8,10},{9,11},{12,14},{13,15},{16,18},{17,19},{..., dimensions={0}, use_global_device_ids=true | all-gather | bytes 393216 | tf_op jit(solution)/shard_map/all_gather | solution.py:29
  36.2 0.0 collective-permute-done.5.odd_ref
  36.2 0.9 step.12
  37.1 0.7 collective-permute-start.6
  37.8 7.3 %all-gather.2 = bf16[32,32,128]{2,1,0:T(8,128)(2,1)S(1)} all-gather(bf16[16,32,128]{2,1,0:T(8,128)(2,1)S(1)} %get-tuple-element.39), channel_id=4, replica_groups={{0,2},{1,3},{4,6},{5,7},{8,10},{9,11},{12,14},{13,15},{16,18},{17,19},{..., dimensions={0}, use_global_device_ids=true | all-gather | bytes 393216 | tf_op jit(solution)/shard_map/all_gather | solution.py:29
  45.1 0.0 collective-permute-done.6.odd_ref
  45.1 0.9 step.13
  46.0 0.7 collective-permute-start.7
  46.7 5.9 %all-gather.3 = bf16[32,32,128]{2,1,0:T(8,128)(2,1)S(1)} all-gather(bf16[16,32,128]{2,1,0:T(8,128)(2,1)S(1)} %get-tuple-element.41), channel_id=5, replica_groups={{0,2},{1,3},{4,6},{5,7},{8,10},{9,11},{12,14},{13,15},{16,18},{17,19},{..., dimensions={0}, use_global_device_ids=true | all-gather | bytes 393216 | tf_op jit(solution)/shard_map/all_gather | solution.py:29
  52.6 0.0 collective-permute-done.7.odd_ref
  52.6 0.9 step.14
  53.5 0.7 collective-permute-start.8
  54.2 8.2 %all-gather.4 = bf16[32,32,128]{2,1,0:T(8,128)(2,1)S(1)} all-gather(bf16[16,32,128]{2,1,0:T(8,128)(2,1)S(1)} %get-tuple-element.43), channel_id=6, replica_groups={{0,2},{1,3},{4,6},{5,7},{8,10},{9,11},{12,14},{13,15},{16,18},{17,19},{..., dimensions={0}, use_global_device_ids=true | all-gather | bytes 393216 | tf_op jit(solution)/shard_map/all_gather | solution.py:29
  62.4 0.0 collective-permute-done.8.odd_ref
  62.4 0.9 step.15
  63.3 0.7 collective-permute-start.9
  64.0 6.7 %all-gather.5 = bf16[32,32,128]{2,1,0:T(8,128)(2,1)S(1)} all-gather(bf16[16,32,128]{2,1,0:T(8,128)(2,1)S(1)} %get-tuple-element.45), channel_id=7, replica_groups={{0,2},{1,3},{4,6},{5,7},{8,10},{9,11},{12,14},{13,15},{16,18},{17,19},{..., dimensions={0}, use_global_device_ids=true | all-gather | bytes 393216 | tf_op jit(solution)/shard_map/all_gather | solution.py:29
  70.6 0.9 step.16
  71.5 0.7 collective-permute-start.10
  72.2 7.7 %all-gather.6 = bf16[32,32,128]{2,1,0:T(8,128)(2,1)S(1)} all-gather(bf16[16,32,128]{2,1,0:T(8,128)(2,1)S(1)} %get-tuple-element.47), channel_id=8, replica_groups={{0,2},{1,3},{4,6},{5,7},{8,10},{9,11},{12,14},{13,15},{16,18},{17,19},{..., dimensions={0}, use_global_device_ids=true | all-gather | bytes 393216 | tf_op jit(solution)/shard_map/all_gather | solution.py:29
  79.9 0.0 collective-permute-done.10.odd_ref
  79.9 0.9 step.17
  80.8 0.7 collective-permute-start.11
  81.4 8.8 %all-gather.7 = bf16[32,32,128]{2,1,0:T(8,128)(2,1)S(1)} all-gather(bf16[16,32,128]{2,1,0:T(8,128)(2,1)S(1)} %get-tuple-element.49), channel_id=9, replica_groups={{0,2},{1,3},{4,6},{5,7},{8,10},{9,11},{12,14},{13,15},{16,18},{17,19},{..., dimensions={0}, use_global_device_ids=true | all-gather | bytes 393216 | tf_op jit(solution)/shard_map/all_gather | solution.py:29
  90.2 0.0 collective-permute-done.11.odd_ref
  90.2 0.9 step.18
  91.1 0.7 collective-permute-start.12
  91.8 7.4 %all-gather.8 = bf16[32,32,128]{2,1,0:T(8,128)(2,1)S(1)} all-gather(bf16[16,32,128]{2,1,0:T(8,128)(2,1)S(1)} %get-tuple-element.51), channel_id=10, replica_groups={{0,2},{1,3},{4,6},{5,7},{8,10},{9,11},{12,14},{13,15},{16,18},{17,19},{..., dimensions={0}, use_global_device_ids=true | all-gather | bytes 393216 | tf_op jit(solution)/shard_map/all_gather | solution.py:29
  99.2 0.9 step.19
  100.1 0.7 collective-permute-start.13
  100.8 6.6 %all-gather.9 = bf16[32,32,128]{2,1,0:T(8,128)(2,1)S(1)} all-gather(bf16[16,32,128]{2,1,0:T(8,128)(2,1)S(1)} %get-tuple-element.53), channel_id=11, replica_groups={{0,2},{1,3},{4,6},{5,7},{8,10},{9,11},{12,14},{13,15},{16,18},{17,19},{..., dimensions={0}, use_global_device_ids=true | all-gather | bytes 393216 | tf_op jit(solution)/shard_map/all_gather | solution.py:29
  107.4 0.0 collective-permute-done.13.odd_ref
  107.4 0.9 step.20
  108.3 0.7 collective-permute-start.14
  108.9 8.9 %all-gather.10 = bf16[32,32,128]{2,1,0:T(8,128)(2,1)S(1)} all-gather(bf16[16,32,128]{2,1,0:T(8,128)(2,1)S(1)} %step.20), channel_id=12, replica_groups={{0,2},{1,3},{4,6},{5,7},{8,10},{9,11},{12,14},{13,15},{16,18},{17,19},{..., dimensions={0}, use_global_device_ids=true | all-gather | bytes 393216 | tf_op jit(solution)/shard_map/all_gather | solution.py:29
  117.9 0.0 collective-permute-done.14.odd_ref
  117.9 0.9 step.21.mine_ref
  118.8 16.0 %all-gather.11 = f32[32,32,128]{2,1,0:T(8,128)S(1)} all-gather(f32[16,32,128]{2,1,0:T(8,128)S(1)} %step.21.mine_ref), channel_id=13, replica_groups={{0,1},{2,3},{4,5},{6,7},{8,9},{10,11},{12,13},{14,15},{16,17},{18,19},{..., dimensions={0}, use_global_device_ids=true | all-gather | bytes 786432 | tf_op jit(solution)/shard_map/all_gather | solution.py:35
  134.8 0.7 gram.1
  135.4 16.7 %all_to_all.10.parts_ref = f32[8,16,128]{2,1,0:T(8,128)S(1)} all-to-all(f32[8,16,128]{2,1,0:T(8,128)S(1)} %get-tuple-element.56), channel_id=1, replica_groups={{0,2,4,6,8,10,12,14},{1,3,5,7,9,11,13,15},{16,18,20,22,24,26,28,30},{17..., dimensions={0} | all-to-all | bytes 131072 | tf_op jit(solution)/shard_map/all_to_all | solution.py:296
  152.2 50.6 %all_to_all.11.parts_ref = f32[32,16,128]{2,1,0:T(8,128)S(1)} all-to-all(f32[32,16,128]{2,1,0:T(8,128)S(1)} %sum_parts.2), channel_id=1, replica_groups=mesh['rx'=32,'ry'=16] {'rx'}, dimensions={0} | all-to-all | bytes 524288 | tf_op jit(solution)/shard_map/all_to_all | solution.py:297
  202.8 5.3 %all_gather.99.gram_ref = f32[2,16,128]{2,1,0:T(8,128)S(1)} all-gather(f32[1,16,128]{2,1,0:T(8,128)S(1)} %sum_parts.3), channel_id=1, replica_groups={{0,1},{2,3},{4,5},{6,7},{8,9},{10,11},{12,13},{14,15},{16,17},{18,19},{..., dimensions={0}, use_global_device_ids=true | all-gather | bytes 24576 | tf_op jit(solution)/shard_map/all_gather | solution.py:35
  208.0 5.4 %factor_and_solve.1 = (f32[64,1024]{1,0:T(8,128)}, f32[64,64]{1,0:T(8,128)}) custom-call(f32[2,16,128]{2,1,0:T(8,128)S(1)} %all_gather.99.gram_ref, f32[64,1024]{1,0:T(8,128)S(1)} %get-tuple-element.57.block_ref), custom_call_target="tpu_custom_call" | custom-call | tf_op jit(solution)/shard_map/factor_and_solve/pallas_call | solution.py:230
  (12 shorter events, 0.1 us)
Async XLA Ops:
  0.6 9.7 %copy-start = (bf16[64,1024]{1,0:T(8,128)(2,1)S(1)}, bf16[64,1024]{1,0:T(8,128)(2,1)}, u32[]{:S(2)}) copy-start(bf16[64,1024]{1,0:T(8,128)(2,1)} %param.5) | copy-start | bytes 393220
  0.6 16.4 %collective-permute-start.3 = (bf16[8,8,128,128]{3,2,1,0:T(8,128)(2,1)}, bf16[8,8,128,128]{3,2,1,0:T(8,128)(2,1)S(1)}, u32[]{:S(2)}, u32[]{:S(2)}) collective-permute-start(bf16[8,8,128,128]{3,2,1,0:T(8,128)(2,1)} %near_ref.1), channel_id=1, source_target_pairs={{0,1},{1,0},{2,3},{3,2},{4,5},{5,4},{6,7},{7,6},{8,9},{9,8},{10,11... | collective-permute-start | bytes 6291464 | tf_op jit(solution)/shard_map/ppermute | solution.py:40
  10.4 3.2 %collective-permute-start = (bf16[9,32,128]{2,1,0:T(8,128)(2,1)S(1)}, bf16[9,32,128]{2,1,0:T(8,128)(2,1)S(1)}, u32[]{:S(2)}, u32[]{:S(2)}) collective-permute-start(bf16[9,32,128]{2,1,0:T(8,128)(2,1)S(1)} %fusion.1), channel_id=1, source_target_pairs={{0,1},{1,0},{2,3},{3,2},{4,5},{5,4},{6,7},{7,6},{8,9},{9,8},{10,11... | collective-permute-start | bytes 221192 | tf_op jit(solution)/shard_map/ppermute | solution.py:40
  13.6 6.1 %collective-permute-start.2 = (bf16[16,32,128]{2,1,0:T(8,128)(2,1)S(1)}, bf16[16,32,128]{2,1,0:T(8,128)(2,1)S(1)}, u32[]{:S(2)}, u32[]{:S(2)}) collective-permute-start(bf16[16,32,128]{2,1,0:T(8,128)(2,1)S(1)} %get-tuple-element.59.own_ref), channel_id=1, source_target_pairs={{2,4},{4,2},{3,5},{5,3},{6,8},{8,6},{7,9},{9,7},{10,12},{12,10},{1... | collective-permute-start | bytes 393224 | tf_op jit(solution)/shard_map/ppermute | solution.py:22
  14.3 6.8 %collective-permute-start.1 = (bf16[16,32,128]{2,1,0:T(8,128)(2,1)S(1)}, bf16[16,32,128]{2,1,0:T(8,128)(2,1)S(1)}, u32[]{:S(2)}, u32[]{:S(2)}) collective-permute-start(bf16[16,32,128]{2,1,0:T(8,128)(2,1)S(1)} %get-tuple-element.59.own_ref), channel_id=1, source_target_pairs={{0,2},{2,0},{1,3},{3,1},{4,6},{6,4},{5,7},{7,5},{8,10},{10,8},{9,1... | collective-permute-start | bytes 393224 | tf_op jit(solution)/shard_map/ppermute | solution.py:22
  17.0 1.6 copy-start.1
  22.0 6.2 %collective-permute-start.4 = (bf16[16,32,128]{2,1,0:T(8,128)(2,1)S(1)}, bf16[16,32,128]{2,1,0:T(8,128)(2,1)S(1)}, u32[]{:S(2)}, u32[]{:S(2)}) collective-permute-start(bf16[16,32,128]{2,1,0:T(8,128)(2,1)S(1)} %get-tuple-element.36), channel_id=1, source_target_pairs={{2,4},{4,2},{3,5},{5,3},{6,8},{8,6},{7,9},{9,7},{10,12},{12,10},{1... | collective-permute-start | bytes 393224 | tf_op jit(solution)/shard_map/ppermute | solution.py:22
  29.1 7.1 %collective-permute-start.5 = (bf16[16,32,128]{2,1,0:T(8,128)(2,1)S(1)}, bf16[16,32,128]{2,1,0:T(8,128)(2,1)S(1)}, u32[]{:S(2)}, u32[]{:S(2)}) collective-permute-start(bf16[16,32,128]{2,1,0:T(8,128)(2,1)S(1)} %get-tuple-element.37), channel_id=1, source_target_pairs={{2,4},{4,2},{3,5},{5,3},{6,8},{8,6},{7,9},{9,7},{10,12},{12,10},{1... | collective-permute-start | bytes 393224 | tf_op jit(solution)/shard_map/ppermute | solution.py:22
  37.1 8.0 %collective-permute-start.6 = (bf16[16,32,128]{2,1,0:T(8,128)(2,1)S(1)}, bf16[16,32,128]{2,1,0:T(8,128)(2,1)S(1)}, u32[]{:S(2)}, u32[]{:S(2)}) collective-permute-start(bf16[16,32,128]{2,1,0:T(8,128)(2,1)S(1)} %get-tuple-element.39), channel_id=1, source_target_pairs={{2,4},{4,2},{3,5},{5,3},{6,8},{8,6},{7,9},{9,7},{10,12},{12,10},{1... | collective-permute-start | bytes 393224 | tf_op jit(solution)/shard_map/ppermute | solution.py:22
  46.0 6.6 %collective-permute-start.7 = (bf16[16,32,128]{2,1,0:T(8,128)(2,1)S(1)}, bf16[16,32,128]{2,1,0:T(8,128)(2,1)S(1)}, u32[]{:S(2)}, u32[]{:S(2)}) collective-permute-start(bf16[16,32,128]{2,1,0:T(8,128)(2,1)S(1)} %get-tuple-element.41), channel_id=1, source_target_pairs={{2,4},{4,2},{3,5},{5,3},{6,8},{8,6},{7,9},{9,7},{10,12},{12,10},{1... | collective-permute-start | bytes 393224 | tf_op jit(solution)/shard_map/ppermute | solution.py:22
  53.5 8.9 %collective-permute-start.8 = (bf16[16,32,128]{2,1,0:T(8,128)(2,1)S(1)}, bf16[16,32,128]{2,1,0:T(8,128)(2,1)S(1)}, u32[]{:S(2)}, u32[]{:S(2)}) collective-permute-start(bf16[16,32,128]{2,1,0:T(8,128)(2,1)S(1)} %get-tuple-element.43), channel_id=1, source_target_pairs={{2,4},{4,2},{3,5},{5,3},{6,8},{8,6},{7,9},{9,7},{10,12},{12,10},{1... | collective-permute-start | bytes 393224 | tf_op jit(solution)/shard_map/ppermute | solution.py:22
  63.3 7.4 %collective-permute-start.9 = (bf16[16,32,128]{2,1,0:T(8,128)(2,1)S(1)}, bf16[16,32,128]{2,1,0:T(8,128)(2,1)S(1)}, u32[]{:S(2)}, u32[]{:S(2)}) collective-permute-start(bf16[16,32,128]{2,1,0:T(8,128)(2,1)S(1)} %get-tuple-element.45), channel_id=1, source_target_pairs={{2,4},{4,2},{3,5},{5,3},{6,8},{8,6},{7,9},{9,7},{10,12},{12,10},{1... | collective-permute-start | bytes 393224 | tf_op jit(solution)/shard_map/ppermute | solution.py:22
  71.5 8.3 %collective-permute-start.10 = (bf16[16,32,128]{2,1,0:T(8,128)(2,1)S(1)}, bf16[16,32,128]{2,1,0:T(8,128)(2,1)S(1)}, u32[]{:S(2)}, u32[]{:S(2)}) collective-permute-start(bf16[16,32,128]{2,1,0:T(8,128)(2,1)S(1)} %get-tuple-element.47), channel_id=1, source_target_pairs={{2,4},{4,2},{3,5},{5,3},{6,8},{8,6},{7,9},{9,7},{10,12},{12,10},{1... | collective-permute-start | bytes 393224 | tf_op jit(solution)/shard_map/ppermute | solution.py:22
  80.8 9.4 %collective-permute-start.11 = (bf16[16,32,128]{2,1,0:T(8,128)(2,1)S(1)}, bf16[16,32,128]{2,1,0:T(8,128)(2,1)S(1)}, u32[]{:S(2)}, u32[]{:S(2)}) collective-permute-start(bf16[16,32,128]{2,1,0:T(8,128)(2,1)S(1)} %get-tuple-element.49), channel_id=1, source_target_pairs={{2,4},{4,2},{3,5},{5,3},{6,8},{8,6},{7,9},{9,7},{10,12},{12,10},{1... | collective-permute-start | bytes 393224 | tf_op jit(solution)/shard_map/ppermute | solution.py:22
  91.1 8.1 %collective-permute-start.12 = (bf16[16,32,128]{2,1,0:T(8,128)(2,1)S(1)}, bf16[16,32,128]{2,1,0:T(8,128)(2,1)S(1)}, u32[]{:S(2)}, u32[]{:S(2)}) collective-permute-start(bf16[16,32,128]{2,1,0:T(8,128)(2,1)S(1)} %get-tuple-element.51), channel_id=1, source_target_pairs={{2,4},{4,2},{3,5},{5,3},{6,8},{8,6},{7,9},{9,7},{10,12},{12,10},{1... | collective-permute-start | bytes 393224 | tf_op jit(solution)/shard_map/ppermute | solution.py:22
  100.1 7.3 %collective-permute-start.13 = (bf16[16,32,128]{2,1,0:T(8,128)(2,1)S(1)}, bf16[16,32,128]{2,1,0:T(8,128)(2,1)S(1)}, u32[]{:S(2)}, u32[]{:S(2)}) collective-permute-start(bf16[16,32,128]{2,1,0:T(8,128)(2,1)S(1)} %get-tuple-element.53), channel_id=1, source_target_pairs={{2,4},{4,2},{3,5},{5,3},{6,8},{8,6},{7,9},{9,7},{10,12},{12,10},{1... | collective-permute-start | bytes 393224 | tf_op jit(solution)/shard_map/ppermute | solution.py:22
  108.3 9.6 %collective-permute-start.14 = (bf16[16,32,128]{2,1,0:T(8,128)(2,1)S(1)}, bf16[16,32,128]{2,1,0:T(8,128)(2,1)S(1)}, u32[]{:S(2)}, u32[]{:S(2)}) collective-permute-start(bf16[16,32,128]{2,1,0:T(8,128)(2,1)S(1)} %step.20), channel_id=1, source_target_pairs={{2,4},{4,2},{3,5},{5,3},{6,8},{8,6},{7,9},{9,7},{10,12},{12,10},{1... | collective-permute-start | bytes 393224 | tf_op jit(solution)/shard_map/ppermute | solution.py:22

commit v5 on v4

--- a/solution.py
+++ b/solution.py
@@ -190,28 +190,43 @@
     def spread(value):
         return jnp.broadcast_to(value, (8, 2 * size))
 
-    for pivot in range(0, size, 2):
+    for pivot in range(0, size, 4):
         at, inner = divmod(pivot, 8)
-        own = groups[at]
-        one, two = spread(own[inner : inner + 1, :]), spread(own[inner + 1 : inner + 2, :])
-        firsts = [spread(group[:, pivot : pivot + 1]) for group in groups[at:]]
-        seconds = [spread(group[:, pivot + 1 : pivot + 2]) for group in groups[at:]]
-        corner, off = spread(firsts[0][inner : inner + 1, :]), spread(seconds[0][inner : inner + 1, :])
-        other = spread(seconds[0][inner + 1 : inner + 2, :])
-        inverse = 1.0 / (corner * other - off * off)
-        left = (other * one - off * two) * inverse
-        right = (corner * two - off * one) * inverse
+        columns = [
+            [spread(group[:, pivot + i : pivot + i + 1]) for i in range(4)] for group in groups[at:]
+        ]
+        lines = [spread(groups[at][inner + i : inner + i + 1, :]) for i in range(4)]
+        block = [
+            [spread(columns[0][j][inner + i : inner + i + 1, :]) for j in range(i + 1)] for i in range(4)
+        ]
+        inverses, scales = [], []
+        lower = [[None] * 4 for _ in range(4)]
+        for j in range(4):
+            inverse = 1.0 / block[j][j]
+            inverses.append(inverse)
+            scales.append(lax.rsqrt(block[j][j]))
+            for i in range(j + 1, 4):
+                lower[i][j] = block[i][j] * inverse
+            for i in range(j + 1, 4):
+                for k in range(j + 1, i + 1):
+                    block[i][k] = block[i][k] - lower[i][j] * block[k][j]
+        for j in range(4):
+            for i in range(j + 1, 4):
+                lines[i] = lines[i] - lower[i][j] * lines[j]
+            rows[pivot + j : pivot + j + 1, :] = (lines[j] * scales[j])[0:1]
         for group in range(at, size // 8):
-            if group == at and inner == 6:
+            if group == at and inner == 4:
                 continue
-            first, second = firsts[group - at], seconds[group - at]
+            own = columns[group - at]
+            change = None
+            for j in range(4):
+                for i in range(j + 1, 4):
+                    own[i] = own[i] - lower[i][j] * own[j]
+                part = own[j] * inverses[j] * lines[j]
+                change = part if change is None else change + part
             if group == at:
-                below = row_of > inner + 1
-                first, second = jnp.where(below, first, 0.0), jnp.where(below, second, 0.0)
-            groups[group] = groups[group] - (first * left + second * right)
-        rows[pivot : pivot + 1, :] = (one * lax.rsqrt(corner))[0:1]
-        ratio = off / corner
-        rows[pivot + 1 : pivot + 2, :] = ((two - ratio * one) * lax.rsqrt(other - ratio * off))[0:1]
+                change = jnp.where(row_of > inner + 3, change, 0.0)
+            groups[group] = groups[group] - change
     upper = lax.broadcasted_iota(jnp.int32, (size, size), 0) <= lax.broadcasted_iota(
         jnp.int32, (size, size), 1
     )
@@ -257,7 +272,8 @@
     slots = away.shape[1]
     packed = jnp.zeros((1, half, tile_size), jnp.bfloat16)
     packed = packed.at[0, :rows_local, :slots].set(away.astype(jnp.bfloat16))
-    theirs = swapped(jnp.concatenate([jnp.where(core == 0, high, low), packed], axis=0))
+    sent = of_both_cores(jnp.concatenate([jnp.where(core == 0, high, low), packed], axis=0))
+    theirs = jnp.where(core == 0, sent[1], sent[0])
     rounded = jnp.concatenate([jnp.where(core == 0, low, high), theirs[:rows_local]], axis=0)
     far_away = theirs[rows_local, :rows_local, :slots].astype(jnp.int32)
 

time: 214 us -> 213 us (level)
  blocking collectives: 168 us -> 171 us
    all_gather x2 -> x3, blocking collectives: 21.2 us -> 24.6 us  [of_both_cores(): return lax.all_gather(value, 'ry', axis_index_groups=groups)]
    ppermute x2 -> x1, starting transfers between devices: 10.8 us -> 8.92 us  [swapped(): lax.ppermute(value, AXES, [(source, source ^ 1) for source in range(count)])]
  transfers between devices with their start and end apart: 15 -> 14, of which waited for: 2 -> 1; matrix products, arithmetic and copies ran while one was open for 1% -> 1% of each run, Pallas kernels for 1% -> 1%
where the time goes in v5:
time: 213 us; the launch traced here: 212 us
  blocking collectives  171 us (80%)
  starting transfers between devices  18.9 us (9%)
  Pallas kernels  18 us (8%)
    all_gather x11, blocking collectives, paired(): return lax.all_gather(value, 'ry', axis_index_groups=groups)  79.3 us
    all_to_all x1, blocking collectives, shards(): parts = lax.all_to_all(summed(parts, outer), 'rx', 0, 0, tiled=True)  50.8 us
    all_gather x3, blocking collectives, of_both_cores(): return lax.all_gather(value, 'ry', axis_index_groups=groups)  24.6 us
    all_to_all x1, blocking collectives, shards(): lax.all_to_all(parts, 'ry', 0, 0, axis_index_groups=same_core, tiled=True)  16.6 us
    pallas_call x12, Pallas kernels, stepped(): pl.pallas_call(kernel, in_specs=[VMEM] * (len(scalars) + len(blocks)), ou...  10.7 us
    ppermute x13, starting transfers between devices, traded(): return lax.ppermute(value, AXES, route)  9.95 us
    ppermute x1, starting transfers between devices, swapped(): lax.ppermute(value, AXES, [(source, source ^ 1) for source in range(count)])  8.92 us
  transfers between devices with their start and end apart: 14, of which 1 were waited for; matrix products, arithmetic and copies ran while one was open for 1% of the time, Pallas kernels for 1%

profile of v5, /device:TPU:1, one launch (start us, length us, event | category | flops | bytes accessed | tf_op | source)
XLA Modules:
  0.0 211.9 jit_solution(3917564368859864329)
XLA Ops:
  0.6 0.0 copy-start
  0.7 8.9 %collective-permute-start.2 = (bf16[8,8,128,128]{3,2,1,0:T(8,128)(2,1)}, bf16[8,8,128,128]{3,2,1,0:T(8,128)(2,1)}, u32[]{:S(2)}, u32[]{:S(2)}) collective-permute-start(bf16[8,8,128,128]{3,2,1,0:T(8,128)(2,1)} %near_ref.1), channel_id=1, source_target_pairs={{0,1},{1,0},{2,3},{3,2},{4,5},{5,4},{6,7},{7,6},{8,9},{9,8},{10,11... | collective-permute-start | bytes 6291464 | tf_op jit(solution)/shard_map/ppermute | solution.py:40
  9.6 0.8 fusion.12
  10.4 3.0 %all-gather = bf16[18,32,128]{2,1,0:T(8,128)(2,1)S(1)} all-gather(bf16[9,32,128]{2,1,0:T(8,128)(2,1)S(1)} %fusion.1), channel_id=2, replica_groups={{0,1},{2,3},{4,5},{6,7},{8,9},{10,11},{12,13},{14,15},{16,17},{18,19},{..., dimensions={0}, use_global_device_ids=true | all-gather | bytes 221184 | tf_op jit(solution)/shard_map/all_gather | solution.py:35
  13.5 0.7 collective-permute-start.1
  14.2 1.9 collective-permute-start
  16.2 0.1 convert_add_fusion
  16.2 0.7 fusion.4.index_ref
  16.9 0.0 collective-permute-done.2.far_ref
  17.0 0.0 copy-done.1
  17.0 2.7 %turn_tiles.1.tiles_ref = bf16[16,8,128,128]{3,2,1,0:T(8,128)(2,1)S(1)} custom-call(bf16[8,8,128,128]{3,2,1,0:T(8,128)(2,1)S(1)} %copy-done.1, bf16[8,8,128,128]{3,2,1,0:T(8,128)(2,1)} %collective-permute-done.2.far_ref), custom_call_target="tpu_custom_call" | custom-call | tf_op jit(solution)/shard_map/turn_tiles/pallas_call | solution.py:52
  19.7 0.0 collective-permute-done.1.odd_ref
  19.7 1.1 collective-permute-done.even_ref
  20.8 0.9 first_step.1
  21.7 0.7 collective-permute-start.3
  22.4 5.4 %all-gather.1 = bf16[32,32,128]{2,1,0:T(8,128)(2,1)S(1)} all-gather(bf16[16,32,128]{2,1,0:T(8,128)(2,1)S(1)} %get-tuple-element.36), channel_id=3, replica_groups={{0,2},{1,3},{4,6},{5,7},{8,10},{9,11},{12,14},{13,15},{16,18},{17,19},{..., dimensions={0}, use_global_device_ids=true | all-gather | bytes 393216 | tf_op jit(solution)/shard_map/all_gather | solution.py:29
  27.8 0.0 collective-permute-done.3.odd_ref
  27.8 0.9 step.11
  28.7 0.7 collective-permute-start.4
  29.4 6.7 %all-gather.2 = bf16[32,32,128]{2,1,0:T(8,128)(2,1)S(1)} all-gather(bf16[16,32,128]{2,1,0:T(8,128)(2,1)S(1)} %get-tuple-element.37), channel_id=4, replica_groups={{0,2},{1,3},{4,6},{5,7},{8,10},{9,11},{12,14},{13,15},{16,18},{17,19},{..., dimensions={0}, use_global_device_ids=true | all-gather | bytes 393216 | tf_op jit(solution)/shard_map/all_gather | solution.py:29
  36.1 0.0 collective-permute-done.4.odd_ref
  36.1 0.9 step.12
  37.0 0.7 collective-permute-start.5
  37.7 7.3 %all-gather.3 = bf16[32,32,128]{2,1,0:T(8,128)(2,1)S(1)} all-gather(bf16[16,32,128]{2,1,0:T(8,128)(2,1)S(1)} %get-tuple-element.39), channel_id=5, replica_groups={{0,2},{1,3},{4,6},{5,7},{8,10},{9,11},{12,14},{13,15},{16,18},{17,19},{..., dimensions={0}, use_global_device_ids=true | all-gather | bytes 393216 | tf_op jit(solution)/shard_map/all_gather | solution.py:29
  45.0 0.0 collective-permute-done.5.odd_ref
  45.0 0.9 step.13
  45.9 0.7 collective-permute-start.6
  46.6 5.9 %all-gather.4 = bf16[32,32,128]{2,1,0:T(8,128)(2,1)S(1)} all-gather(bf16[16,32,128]{2,1,0:T(8,128)(2,1)S(1)} %get-tuple-element.41), channel_id=6, replica_groups={{0,2},{1,3},{4,6},{5,7},{8,10},{9,11},{12,14},{13,15},{16,18},{17,19},{..., dimensions={0}, use_global_device_ids=true | all-gather | bytes 393216 | tf_op jit(solution)/shard_map/all_gather | solution.py:29
  52.5 0.0 collective-permute-done.6.odd_ref
  52.5 0.9 step.14
  53.4 0.7 collective-permute-start.7
  54.1 8.2 %all-gather.5 = bf16[32,32,128]{2,1,0:T(8,128)(2,1)S(1)} all-gather(bf16[16,32,128]{2,1,0:T(8,128)(2,1)S(1)} %get-tuple-element.43), channel_id=7, replica_groups={{0,2},{1,3},{4,6},{5,7},{8,10},{9,11},{12,14},{13,15},{16,18},{17,19},{..., dimensions={0}, use_global_device_ids=true | all-gather | bytes 393216 | tf_op jit(solution)/shard_map/all_gather | solution.py:29
  62.3 0.0 collective-permute-done.7.odd_ref
  62.3 0.9 step.15
  63.2 0.7 collective-permute-start.8
  63.9 6.7 %all-gather.6 = bf16[32,32,128]{2,1,0:T(8,128)(2,1)S(1)} all-gather(bf16[16,32,128]{2,1,0:T(8,128)(2,1)S(1)} %get-tuple-element.45), channel_id=8, replica_groups={{0,2},{1,3},{4,6},{5,7},{8,10},{9,11},{12,14},{13,15},{16,18},{17,19},{..., dimensions={0}, use_global_device_ids=true | all-gather | bytes 393216 | tf_op jit(solution)/shard_map/all_gather | solution.py:29
  70.5 0.0 collective-permute-done.8.odd_ref
  70.5 0.9 step.16
  71.4 0.7 collective-permute-start.9
  72.1 7.6 %all-gather.7 = bf16[32,32,128]{2,1,0:T(8,128)(2,1)S(1)} all-gather(bf16[16,32,128]{2,1,0:T(8,128)(2,1)S(1)} %get-tuple-element.47), channel_id=9, replica_groups={{0,2},{1,3},{4,6},{5,7},{8,10},{9,11},{12,14},{13,15},{16,18},{17,19},{..., dimensions={0}, use_global_device_ids=true | all-gather | bytes 393216 | tf_op jit(solution)/shard_map/all_gather | solution.py:29
  79.7 0.0 collective-permute-done.9.odd_ref
  79.7 0.9 step.17
  80.6 0.7 collective-permute-start.10
  81.3 8.2 %all-gather.8 = bf16[32,32,128]{2,1,0:T(8,128)(2,1)S(1)} all-gather(bf16[16,32,128]{2,1,0:T(8,128)(2,1)S(1)} %get-tuple-element.49), channel_id=10, replica_groups={{0,2},{1,3},{4,6},{5,7},{8,10},{9,11},{12,14},{13,15},{16,18},{17,19},{..., dimensions={0}, use_global_device_ids=true | all-gather | bytes 393216 | tf_op jit(solution)/shard_map/all_gather | solution.py:29
  89.5 0.0 collective-permute-done.10.odd_ref
  89.5 0.9 step.18
  90.4 0.7 collective-permute-start.11
  91.1 8.0 %all-gather.9 = bf16[32,32,128]{2,1,0:T(8,128)(2,1)S(1)} all-gather(bf16[16,32,128]{2,1,0:T(8,128)(2,1)S(1)} %get-tuple-element.51), channel_id=11, replica_groups={{0,2},{1,3},{4,6},{5,7},{8,10},{9,11},{12,14},{13,15},{16,18},{17,19},{..., dimensions={0}, use_global_device_ids=true | all-gather | bytes 393216 | tf_op jit(solution)/shard_map/all_gather | solution.py:29
  99.1 0.0 collective-permute-done.11.odd_ref
  99.1 0.9 step.19
  100.0 0.7 collective-permute-start.12
  100.6 6.5 %all-gather.10 = bf16[32,32,128]{2,1,0:T(8,128)(2,1)S(1)} all-gather(bf16[16,32,128]{2,1,0:T(8,128)(2,1)S(1)} %get-tuple-element.53), channel_id=12, replica_groups={{0,2},{1,3},{4,6},{5,7},{8,10},{9,11},{12,14},{13,15},{16,18},{17,19},{..., dimensions={0}, use_global_device_ids=true | all-gather | bytes 393216 | tf_op jit(solution)/shard_map/all_gather | solution.py:29
  107.2 0.0 collective-permute-done.12.odd_ref
  107.2 0.9 step.20
  108.1 0.7 collective-permute-start.13
  108.7 8.7 %all-gather.11 = bf16[32,32,128]{2,1,0:T(8,128)(2,1)S(1)} all-gather(bf16[16,32,128]{2,1,0:T(8,128)(2,1)S(1)} %step.20), channel_id=13, replica_groups={{0,2},{1,3},{4,6},{5,7},{8,10},{9,11},{12,14},{13,15},{16,18},{17,19},{..., dimensions={0}, use_global_device_ids=true | all-gather | bytes 393216 | tf_op jit(solution)/shard_map/all_gather | solution.py:29
  117.5 0.0 collective-permute-done.13.odd_ref
  117.5 0.9 step.21.mine_ref
  118.4 16.3 %all-gather.12 = f32[32,32,128]{2,1,0:T(8,128)S(1)} all-gather(f32[16,32,128]{2,1,0:T(8,128)S(1)} %step.21.mine_ref), channel_id=14, replica_groups={{0,1},{2,3},{4,5},{6,7},{8,9},{10,11},{12,13},{14,15},{16,17},{18,19},{..., dimensions={0}, use_global_device_ids=true | all-gather | bytes 786432 | tf_op jit(solution)/shard_map/all_gather | solution.py:35
  134.7 0.7 gram.1
  135.4 16.6 %all_to_all.10.parts_ref = f32[8,16,128]{2,1,0:T(8,128)S(1)} all-to-all(f32[8,16,128]{2,1,0:T(8,128)S(1)} %get-tuple-element.56), channel_id=1, replica_groups={{0,2,4,6,8,10,12,14},{1,3,5,7,9,11,13,15},{16,18,20,22,24,26,28,30},{17..., dimensions={0} | all-to-all | bytes 131072 | tf_op jit(solution)/shard_map/all_to_all | solution.py:312
  152.0 50.8 %all_to_all.11.parts_ref = f32[32,16,128]{2,1,0:T(8,128)S(1)} all-to-all(f32[32,16,128]{2,1,0:T(8,128)S(1)} %sum_parts.2), channel_id=1, replica_groups=mesh['rx'=32,'ry'=16] {'rx'}, dimensions={0} | all-to-all | bytes 524288 | tf_op jit(solution)/shard_map/all_to_all | solution.py:313
  202.8 5.2 %all_gather.107.gram_ref = f32[2,16,128]{2,1,0:T(8,128)S(1)} all-gather(f32[1,16,128]{2,1,0:T(8,128)S(1)} %sum_parts.3), channel_id=1, replica_groups={{0,1},{2,3},{4,5},{6,7},{8,9},{10,11},{12,13},{14,15},{16,17},{18,19},{..., dimensions={0}, use_global_device_ids=true | all-gather | bytes 24576 | tf_op jit(solution)/shard_map/all_gather | solution.py:35
  208.0 3.9 %factor_and_solve.1 = (f32[64,1024]{1,0:T(8,128)}, f32[64,64]{1,0:T(8,128)}) custom-call(f32[2,16,128]{2,1,0:T(8,128)S(1)} %all_gather.107.gram_ref, f32[64,1024]{1,0:T(8,128)S(1)} %get-tuple-element.57.block_ref), custom_call_target="tpu_custom_call" | custom-call | tf_op jit(solution)/shard_map/factor_and_solve/pallas_call | solution.py:245
  (13 shorter events, 0.2 us)
Async XLA Ops:
  0.6 9.7 %copy-start = (bf16[64,1024]{1,0:T(8,128)(2,1)S(1)}, bf16[64,1024]{1,0:T(8,128)(2,1)}, u32[]{:S(2)}) copy-start(bf16[64,1024]{1,0:T(8,128)(2,1)} %param.5) | copy-start | bytes 393220
  0.6 16.3 %copy-start.1 = (bf16[8,8,128,128]{3,2,1,0:T(8,128)(2,1)S(1)}, bf16[8,8,128,128]{3,2,1,0:T(8,128)(2,1)}, u32[]{:S(2)}) copy-start(bf16[8,8,128,128]{3,2,1,0:T(8,128)(2,1)} %near_ref.1) | copy-start | bytes 6291460
  0.7 16.3 %collective-permute-start.2 = (bf16[8,8,128,128]{3,2,1,0:T(8,128)(2,1)}, bf16[8,8,128,128]{3,2,1,0:T(8,128)(2,1)}, u32[]{:S(2)}, u32[]{:S(2)}) collective-permute-start(bf16[8,8,128,128]{3,2,1,0:T(8,128)(2,1)} %near_ref.1), channel_id=1, source_target_pairs={{0,1},{1,0},{2,3},{3,2},{4,5},{5,4},{6,7},{7,6},{8,9},{9,8},{10,11... | collective-permute-start | bytes 6291464 | tf_op jit(solution)/shard_map/ppermute | solution.py:40
  13.5 6.2 %collective-permute-start.1 = (bf16[16,32,128]{2,1,0:T(8,128)(2,1)S(1)}, bf16[16,32,128]{2,1,0:T(8,128)(2,1)S(1)}, u32[]{:S(2)}, u32[]{:S(2)}) collective-permute-start(bf16[16,32,128]{2,1,0:T(8,128)(2,1)S(1)} %get-tuple-element.59.own_ref), channel_id=1, source_target_pairs={{2,4},{4,2},{3,5},{5,3},{6,8},{8,6},{7,9},{9,7},{10,12},{12,10},{1... | collective-permute-start | bytes 393224 | tf_op jit(solution)/shard_map/ppermute | solution.py:22
  14.2 6.6 %collective-permute-start = (bf16[16,32,128]{2,1,0:T(8,128)(2,1)S(1)}, bf16[16,32,128]{2,1,0:T(8,128)(2,1)S(1)}, u32[]{:S(2)}, u32[]{:S(2)}) collective-permute-start(bf16[16,32,128]{2,1,0:T(8,128)(2,1)S(1)} %get-tuple-element.59.own_ref), channel_id=1, source_target_pairs={{0,2},{2,0},{1,3},{3,1},{4,6},{6,4},{5,7},{7,5},{8,10},{10,8},{9,1... | collective-permute-start | bytes 393224 | tf_op jit(solution)/shard_map/ppermute | solution.py:22
  21.7 6.1 %collective-permute-start.3 = (bf16[16,32,128]{2,1,0:T(8,128)(2,1)S(1)}, bf16[16,32,128]{2,1,0:T(8,128)(2,1)S(1)}, u32[]{:S(2)}, u32[]{:S(2)}) collective-permute-start(bf16[16,32,128]{2,1,0:T(8,128)(2,1)S(1)} %get-tuple-element.36), channel_id=1, source_target_pairs={{2,4},{4,2},{3,5},{5,3},{6,8},{8,6},{7,9},{9,7},{10,12},{12,10},{1... | collective-permute-start | bytes 393224 | tf_op jit(solution)/shard_map/ppermute | solution.py:22
  28.7 7.4 %collective-permute-start.4 = (bf16[16,32,128]{2,1,0:T(8,128)(2,1)S(1)}, bf16[16,32,128]{2,1,0:T(8,128)(2,1)S(1)}, u32[]{:S(2)}, u32[]{:S(2)}) collective-permute-start(bf16[16,32,128]{2,1,0:T(8,128)(2,1)S(1)} %get-tuple-element.37), channel_id=1, source_target_pairs={{2,4},{4,2},{3,5},{5,3},{6,8},{8,6},{7,9},{9,7},{10,12},{12,10},{1... | collective-permute-start | bytes 393224 | tf_op jit(solution)/shard_map/ppermute | solution.py:22
  37.0 8.0 %collective-permute-start.5 = (bf16[16,32,128]{2,1,0:T(8,128)(2,1)S(1)}, bf16[16,32,128]{2,1,0:T(8,128)(2,1)S(1)}, u32[]{:S(2)}, u32[]{:S(2)}) collective-permute-start(bf16[16,32,128]{2,1,0:T(8,128)(2,1)S(1)} %get-tuple-element.39), channel_id=1, source_target_pairs={{2,4},{4,2},{3,5},{5,3},{6,8},{8,6},{7,9},{9,7},{10,12},{12,10},{1... | collective-permute-start | bytes 393224 | tf_op jit(solution)/shard_map/ppermute | solution.py:22
  45.9 6.6 %collective-permute-start.6 = (bf16[16,32,128]{2,1,0:T(8,128)(2,1)S(1)}, bf16[16,32,128]{2,1,0:T(8,128)(2,1)S(1)}, u32[]{:S(2)}, u32[]{:S(2)}) collective-permute-start(bf16[16,32,128]{2,1,0:T(8,128)(2,1)S(1)} %get-tuple-element.41), channel_id=1, source_target_pairs={{2,4},{4,2},{3,5},{5,3},{6,8},{8,6},{7,9},{9,7},{10,12},{12,10},{1... | collective-permute-start | bytes 393224 | tf_op jit(solution)/shard_map/ppermute | solution.py:22
  53.4 8.9 %collective-permute-start.7 = (bf16[16,32,128]{2,1,0:T(8,128)(2,1)S(1)}, bf16[16,32,128]{2,1,0:T(8,128)(2,1)S(1)}, u32[]{:S(2)}, u32[]{:S(2)}) collective-permute-start(bf16[16,32,128]{2,1,0:T(8,128)(2,1)S(1)} %get-tuple-element.43), channel_id=1, source_target_pairs={{2,4},{4,2},{3,5},{5,3},{6,8},{8,6},{7,9},{9,7},{10,12},{12,10},{1... | collective-permute-start | bytes 393224 | tf_op jit(solution)/shard_map/ppermute | solution.py:22
  63.2 7.3 %collective-permute-start.8 = (bf16[16,32,128]{2,1,0:T(8,128)(2,1)S(1)}, bf16[16,32,128]{2,1,0:T(8,128)(2,1)S(1)}, u32[]{:S(2)}, u32[]{:S(2)}) collective-permute-start(bf16[16,32,128]{2,1,0:T(8,128)(2,1)S(1)} %get-tuple-element.45), channel_id=1, source_target_pairs={{2,4},{4,2},{3,5},{5,3},{6,8},{8,6},{7,9},{9,7},{10,12},{12,10},{1... | collective-permute-start | bytes 393224 | tf_op jit(solution)/shard_map/ppermute | solution.py:22
  71.4 8.3 %collective-permute-start.9 = (bf16[16,32,128]{2,1,0:T(8,128)(2,1)S(1)}, bf16[16,32,128]{2,1,0:T(8,128)(2,1)S(1)}, u32[]{:S(2)}, u32[]{:S(2)}) collective-permute-start(bf16[16,32,128]{2,1,0:T(8,128)(2,1)S(1)} %get-tuple-element.47), channel_id=1, source_target_pairs={{2,4},{4,2},{3,5},{5,3},{6,8},{8,6},{7,9},{9,7},{10,12},{12,10},{1... | collective-permute-start | bytes 393224 | tf_op jit(solution)/shard_map/ppermute | solution.py:22
  80.6 8.8 %collective-permute-start.10 = (bf16[16,32,128]{2,1,0:T(8,128)(2,1)S(1)}, bf16[16,32,128]{2,1,0:T(8,128)(2,1)S(1)}, u32[]{:S(2)}, u32[]{:S(2)}) collective-permute-start(bf16[16,32,128]{2,1,0:T(8,128)(2,1)S(1)} %get-tuple-element.49), channel_id=1, source_target_pairs={{2,4},{4,2},{3,5},{5,3},{6,8},{8,6},{7,9},{9,7},{10,12},{12,10},{1... | collective-permute-start | bytes 393224 | tf_op jit(solution)/shard_map/ppermute | solution.py:22
  90.4 8.7 %collective-permute-start.11 = (bf16[16,32,128]{2,1,0:T(8,128)(2,1)S(1)}, bf16[16,32,128]{2,1,0:T(8,128)(2,1)S(1)}, u32[]{:S(2)}, u32[]{:S(2)}) collective-permute-start(bf16[16,32,128]{2,1,0:T(8,128)(2,1)S(1)} %get-tuple-element.51), channel_id=1, source_target_pairs={{2,4},{4,2},{3,5},{5,3},{6,8},{8,6},{7,9},{9,7},{10,12},{12,10},{1... | collective-permute-start | bytes 393224 | tf_op jit(solution)/shard_map/ppermute | solution.py:22
  100.0 7.2 %collective-permute-start.12 = (bf16[16,32,128]{2,1,0:T(8,128)(2,1)S(1)}, bf16[16,32,128]{2,1,0:T(8,128)(2,1)S(1)}, u32[]{:S(2)}, u32[]{:S(2)}) collective-permute-start(bf16[16,32,128]{2,1,0:T(8,128)(2,1)S(1)} %get-tuple-element.53), channel_id=1, source_target_pairs={{2,4},{4,2},{3,5},{5,3},{6,8},{8,6},{7,9},{9,7},{10,12},{12,10},{1... | collective-permute-start | bytes 393224 | tf_op jit(solution)/shard_map/ppermute | solution.py:22
  108.1 9.4 %collective-permute-start.13 = (bf16[16,32,128]{2,1,0:T(8,128)(2,1)S(1)}, bf16[16,32,128]{2,1,0:T(8,128)(2,1)S(1)}, u32[]{:S(2)}, u32[]{:S(2)}) collective-permute-start(bf16[16,32,128]{2,1,0:T(8,128)(2,1)S(1)} %step.20), channel_id=1, source_target_pairs={{2,4},{4,2},{3,5},{5,3},{6,8},{8,6},{7,9},{9,7},{10,12},{12,10},{1... | collective-permute-start | bytes 393224 | tf_op jit(solution)/shard_map/ppermute | solution.py:22

commit v6 on v5

--- a/solution.py
+++ b/solution.py
@@ -79,7 +79,7 @@
 
 
 def first_kernel(
-    index_ref, even_chip_ref, even_ref, own_ref, odd_ref, tiles_ref, latest_ref, rounded_ref, window
+    index_ref, even_chip_ref, odd_ref, own_ref, even_ref, tiles_ref, latest_ref, rounded_ref, window
 ):
     count = odd_ref.shape[0]
     is_even = even_chip_ref[0, 0] == 1
@@ -277,6 +277,7 @@
     rounded = jnp.concatenate([jnp.where(core == 0, low, high), theirs[:rows_local]], axis=0)
     far_away = theirs[rows_local, :rows_local, :slots].astype(jnp.int32)
 
+    operator_tiles, rounded = lax.optimization_barrier((operator_tiles, rounded))
     tiles = turned(operator_tiles, swapped(operator_tiles))
 
     far_rows = (position ^ 1) * rows_local + row_ids
@@ -291,7 +292,7 @@
         first_kernel,
         "first_step",
         (index, even_chip),
-        (traded(rounded, 0), rounded, traded(rounded, 1), tiles),
+        (traded(rounded, 1), rounded, traded(rounded, 0), tiles),
     )
     for degree in range(2, DEG + 1):
         keep = (degree != DEG - 1, degree != DEG)

time: 213 us -> 212 us (level)
  starting transfers between devices: 18.9 us -> 12.2 us
  blocking collectives: 171 us -> 176 us
  local copies, waits for them, and re-layouts: 0.04 us -> 2.51 us
    ppermute x1, starting transfers between devices: 8.92 us -> 2.26 us  [swapped(): lax.ppermute(value, AXES, [(source, source ^ 1) for source in range(count)])]
    all_gather x3, blocking collectives: 24.6 us -> 29.6 us  [of_both_cores(): return lax.all_gather(value, 'ry', axis_index_groups=groups)]
    unnamed x4, local copies, waits for them, and re-layouts: 0.01 us -> 2.48 us
  transfers between devices with their start and end apart: 14 -> 14, of which waited for: 1 -> 2; matrix products, arithmetic and copies ran while one was open for 1% -> 0% of each run, Pallas kernels for 1% -> 1%
where the time goes in v6:
time: 212 us; the launch traced here: 211 us
  blocking collectives  176 us (83%)
  Pallas kernels  16.4 us (8%)
  starting transfers between devices  12.2 us (6%)
  local copies, waits for them, and re-layouts  2.51 us (1%)
    all_gather x11, blocking collectives, paired(): return lax.all_gather(value, 'ry', axis_index_groups=groups)  79.5 us
    all_to_all x1, blocking collectives, shards(): parts = lax.all_to_all(summed(parts, outer), 'rx', 0, 0, tiled=True)  50.4 us
    all_gather x3, blocking collectives, of_both_cores(): return lax.all_gather(value, 'ry', axis_index_groups=groups)  29.6 us
    all_to_all x1, blocking collectives, shards(): lax.all_to_all(parts, 'ry', 0, 0, axis_index_groups=same_core, tiled=True)  16.7 us
    pallas_call x12, Pallas kernels, stepped(): pl.pallas_call(kernel, in_specs=[VMEM] * (len(scalars) + len(blocks)), ou...  10.7 us
    ppermute x13, starting transfers between devices, traded(): return lax.ppermute(value, AXES, route)  9.95 us
  transfers between devices with their start and end apart: 14, of which 2 were waited for; matrix products, arithmetic and copies ran while one was open for 0% of the time, Pallas kernels for 1%

profile of v6, /device:TPU:1, one launch (start us, length us, event | category | flops | bytes accessed | tf_op | source)
XLA Modules:
  0.0 211.4 jit_solution(12587380118566023626)
XLA Ops:
  0.6 0.0 copy-start
  0.7 0.9 copy-done
  1.6 0.8 fusion.12
  2.4 8.4 %all-gather = bf16[18,32,128]{2,1,0:T(8,128)(2,1)S(1)} all-gather(bf16[9,32,128]{2,1,0:T(8,128)(2,1)S(1)} %fusion.1), channel_id=2, replica_groups={{0,1},{2,3},{4,5},{6,7},{8,9},{10,11},{12,13},{14,15},{16,17},{18,19},{..., dimensions={0}, use_global_device_ids=true | all-gather | bytes 221184 | tf_op jit(solution)/shard_map/all_gather | solution.py:35
  10.9 2.3 %collective-permute-start.2 = (bf16[8,8,128,128]{3,2,1,0:T(8,128)(2,1)}, bf16[8,8,128,128]{3,2,1,0:T(8,128)(2,1)S(1)}, u32[]{:S(2)}, u32[]{:S(2)}) collective-permute-start(bf16[8,8,128,128]{3,2,1,0:T(8,128)(2,1)} %near_ref), channel_id=1, source_target_pairs={{0,1},{1,0},{2,3},{3,2},{4,5},{5,4},{6,7},{7,6},{8,9},{9,8},{10,11... | collective-permute-start | bytes 6291464 | tf_op jit(solution)/shard_map/ppermute | solution.py:40
  13.1 0.7 collective-permute-start
  13.8 1.9 collective-permute-start.1
  15.8 0.1 convert_add_fusion
  15.8 0.7 fusion.4.index_ref
  16.6 0.6 collective-permute-done.2.far_ref
  17.1 1.6 copy-done.1
  18.7 1.1 turn_tiles.1.tiles_ref
  19.9 0.0 collective-permute-done.odd_ref
  19.9 0.8 collective-permute-done.1.even_ref
  20.7 0.9 first_step.1
  21.6 0.7 collective-permute-start.3
  22.3 5.5 %all-gather.1 = bf16[32,32,128]{2,1,0:T(8,128)(2,1)S(1)} all-gather(bf16[16,32,128]{2,1,0:T(8,128)(2,1)S(1)} %get-tuple-element.40), channel_id=3, replica_groups={{0,2},{1,3},{4,6},{5,7},{8,10},{9,11},{12,14},{13,15},{16,18},{17,19},{..., dimensions={0}, use_global_device_ids=true | all-gather | bytes 393216 | tf_op jit(solution)/shard_map/all_gather | solution.py:29
  27.8 0.0 collective-permute-done.3.odd_ref
  27.8 0.9 step.11
  28.7 0.7 collective-permute-start.4
  29.4 6.4 %all-gather.2 = bf16[32,32,128]{2,1,0:T(8,128)(2,1)S(1)} all-gather(bf16[16,32,128]{2,1,0:T(8,128)(2,1)S(1)} %get-tuple-element.41), channel_id=4, replica_groups={{0,2},{1,3},{4,6},{5,7},{8,10},{9,11},{12,14},{13,15},{16,18},{17,19},{..., dimensions={0}, use_global_device_ids=true | all-gather | bytes 393216 | tf_op jit(solution)/shard_map/all_gather | solution.py:29
  35.7 0.0 collective-permute-done.4.odd_ref
  35.7 0.9 step.12
  36.6 0.7 collective-permute-start.5
  37.3 7.3 %all-gather.3 = bf16[32,32,128]{2,1,0:T(8,128)(2,1)S(1)} all-gather(bf16[16,32,128]{2,1,0:T(8,128)(2,1)S(1)} %get-tuple-element.43), channel_id=5, replica_groups={{0,2},{1,3},{4,6},{5,7},{8,10},{9,11},{12,14},{13,15},{16,18},{17,19},{..., dimensions={0}, use_global_device_ids=true | all-gather | bytes 393216 | tf_op jit(solution)/shard_map/all_gather | solution.py:29
  44.6 0.0 collective-permute-done.5.odd_ref
  44.6 0.9 step.13
  45.5 0.7 collective-permute-start.6
  46.2 6.0 %all-gather.4 = bf16[32,32,128]{2,1,0:T(8,128)(2,1)S(1)} all-gather(bf16[16,32,128]{2,1,0:T(8,128)(2,1)S(1)} %get-tuple-element.45), channel_id=6, replica_groups={{0,2},{1,3},{4,6},{5,7},{8,10},{9,11},{12,14},{13,15},{16,18},{17,19},{..., dimensions={0}, use_global_device_ids=true | all-gather | bytes 393216 | tf_op jit(solution)/shard_map/all_gather | solution.py:29
  52.1 0.0 collective-permute-done.6.odd_ref
  52.1 0.9 step.14
  53.0 0.7 collective-permute-start.7
  53.7 8.2 %all-gather.5 = bf16[32,32,128]{2,1,0:T(8,128)(2,1)S(1)} all-gather(bf16[16,32,128]{2,1,0:T(8,128)(2,1)S(1)} %get-tuple-element.47), channel_id=7, replica_groups={{0,2},{1,3},{4,6},{5,7},{8,10},{9,11},{12,14},{13,15},{16,18},{17,19},{..., dimensions={0}, use_global_device_ids=true | all-gather | bytes 393216 | tf_op jit(solution)/shard_map/all_gather | solution.py:29
  61.9 0.0 collective-permute-done.7.odd_ref
  61.9 0.9 step.15
  62.8 0.7 collective-permute-start.8
  63.5 6.7 %all-gather.6 = bf16[32,32,128]{2,1,0:T(8,128)(2,1)S(1)} all-gather(bf16[16,32,128]{2,1,0:T(8,128)(2,1)S(1)} %get-tuple-element.49), channel_id=8, replica_groups={{0,2},{1,3},{4,6},{5,7},{8,10},{9,11},{12,14},{13,15},{16,18},{17,19},{..., dimensions={0}, use_global_device_ids=true | all-gather | bytes 393216 | tf_op jit(solution)/shard_map/all_gather | solution.py:29
  70.2 0.0 collective-permute-done.8.odd_ref
  70.2 0.9 step.16
  71.1 0.7 collective-permute-start.9
  71.7 7.7 %all-gather.7 = bf16[32,32,128]{2,1,0:T(8,128)(2,1)S(1)} all-gather(bf16[16,32,128]{2,1,0:T(8,128)(2,1)S(1)} %get-tuple-element.51), channel_id=9, replica_groups={{0,2},{1,3},{4,6},{5,7},{8,10},{9,11},{12,14},{13,15},{16,18},{17,19},{..., dimensions={0}, use_global_device_ids=true | all-gather | bytes 393216 | tf_op jit(solution)/shard_map/all_gather | solution.py:29
  79.4 0.0 collective-permute-done.9.odd_ref
  79.4 0.9 step.17
  80.3 0.7 collective-permute-start.10
  81.0 9.0 %all-gather.8 = bf16[32,32,128]{2,1,0:T(8,128)(2,1)S(1)} all-gather(bf16[16,32,128]{2,1,0:T(8,128)(2,1)S(1)} %get-tuple-element.53), channel_id=10, replica_groups={{0,2},{1,3},{4,6},{5,7},{8,10},{9,11},{12,14},{13,15},{16,18},{17,19},{..., dimensions={0}, use_global_device_ids=true | all-gather | bytes 393216 | tf_op jit(solution)/shard_map/all_gather | solution.py:29
  90.0 0.0 collective-permute-done.10.odd_ref
  90.0 0.9 step.18
  90.9 0.7 collective-permute-start.11
  91.6 7.2 %all-gather.9 = bf16[32,32,128]{2,1,0:T(8,128)(2,1)S(1)} all-gather(bf16[16,32,128]{2,1,0:T(8,128)(2,1)S(1)} %get-tuple-element.55), channel_id=11, replica_groups={{0,2},{1,3},{4,6},{5,7},{8,10},{9,11},{12,14},{13,15},{16,18},{17,19},{..., dimensions={0}, use_global_device_ids=true | all-gather | bytes 393216 | tf_op jit(solution)/shard_map/all_gather | solution.py:29
  98.8 0.9 step.19
  99.7 0.7 collective-permute-start.12
  100.4 6.6 %all-gather.10 = bf16[32,32,128]{2,1,0:T(8,128)(2,1)S(1)} all-gather(bf16[16,32,128]{2,1,0:T(8,128)(2,1)S(1)} %get-tuple-element.57), channel_id=12, replica_groups={{0,2},{1,3},{4,6},{5,7},{8,10},{9,11},{12,14},{13,15},{16,18},{17,19},{..., dimensions={0}, use_global_device_ids=true | all-gather | bytes 393216 | tf_op jit(solution)/shard_map/all_gather | solution.py:29
  107.0 0.0 collective-permute-done.12.odd_ref
  107.0 0.9 step.20
  107.9 0.7 collective-permute-start.13
  108.6 9.0 %all-gather.11 = bf16[32,32,128]{2,1,0:T(8,128)(2,1)S(1)} all-gather(bf16[16,32,128]{2,1,0:T(8,128)(2,1)S(1)} %step.20), channel_id=13, replica_groups={{0,2},{1,3},{4,6},{5,7},{8,10},{9,11},{12,14},{13,15},{16,18},{17,19},{..., dimensions={0}, use_global_device_ids=true | all-gather | bytes 393216 | tf_op jit(solution)/shard_map/all_gather | solution.py:29
  117.6 0.0 collective-permute-done.13.odd_ref
  117.6 0.9 step.21.mine_ref
  118.5 15.9 %all-gather.12 = f32[32,32,128]{2,1,0:T(8,128)S(1)} all-gather(f32[16,32,128]{2,1,0:T(8,128)S(1)} %step.21.mine_ref), channel_id=14, replica_groups={{0,1},{2,3},{4,5},{6,7},{8,9},{10,11},{12,13},{14,15},{16,17},{18,19},{..., dimensions={0}, use_global_device_ids=true | all-gather | bytes 786432 | tf_op jit(solution)/shard_map/all_gather | solution.py:35
  134.4 0.7 gram.1
  135.1 16.7 %all_to_all.10.parts_ref = f32[8,16,128]{2,1,0:T(8,128)S(1)} all-to-all(f32[8,16,128]{2,1,0:T(8,128)S(1)} %get-tuple-element.60), channel_id=1, replica_groups={{0,2,4,6,8,10,12,14},{1,3,5,7,9,11,13,15},{16,18,20,22,24,26,28,30},{17..., dimensions={0} | all-to-all | bytes 131072 | tf_op jit(solution)/shard_map/all_to_all | solution.py:313
  151.8 50.4 %all_to_all.11.parts_ref = f32[32,16,128]{2,1,0:T(8,128)S(1)} all-to-all(f32[32,16,128]{2,1,0:T(8,128)S(1)} %sum_parts.2), channel_id=1, replica_groups=mesh['rx'=32,'ry'=16] {'rx'}, dimensions={0} | all-to-all | bytes 524288 | tf_op jit(solution)/shard_map/all_to_all | solution.py:314
  202.2 5.2 %all_gather.107.gram_ref = f32[2,16,128]{2,1,0:T(8,128)S(1)} all-gather(f32[1,16,128]{2,1,0:T(8,128)S(1)} %sum_parts.3), channel_id=1, replica_groups={{0,1},{2,3},{4,5},{6,7},{8,9},{10,11},{12,13},{14,15},{16,17},{18,19},{..., dimensions={0}, use_global_device_ids=true | all-gather | bytes 24576 | tf_op jit(solution)/shard_map/all_gather | solution.py:35
  207.5 3.9 %factor_and_solve.1 = (f32[64,1024]{1,0:T(8,128)}, f32[64,64]{1,0:T(8,128)}) custom-call(f32[2,16,128]{2,1,0:T(8,128)S(1)} %all_gather.107.gram_ref, f32[64,1024]{1,0:T(8,128)S(1)} %get-tuple-element.61.block_ref), custom_call_target="tpu_custom_call" | custom-call | tf_op jit(solution)/shard_map/factor_and_solve/pallas_call | solution.py:245
  (14 shorter events, 0.2 us)
Async XLA Ops:
  0.6 0.9 copy-start
  10.9 6.3 %collective-permute-start.2 = (bf16[8,8,128,128]{3,2,1,0:T(8,128)(2,1)}, bf16[8,8,128,128]{3,2,1,0:T(8,128)(2,1)S(1)}, u32[]{:S(2)}, u32[]{:S(2)}) collective-permute-start(bf16[8,8,128,128]{3,2,1,0:T(8,128)(2,1)} %near_ref), channel_id=1, source_target_pairs={{0,1},{1,0},{2,3},{3,2},{4,5},{5,4},{6,7},{7,6},{8,9},{9,8},{10,11... | collective-permute-start | bytes 6291464 | tf_op jit(solution)/shard_map/ppermute | solution.py:40
  13.1 6.7 %collective-permute-start = (bf16[16,32,128]{2,1,0:T(8,128)(2,1)S(1)}, bf16[16,32,128]{2,1,0:T(8,128)(2,1)S(1)}, u32[]{:S(2)}, u32[]{:S(2)}) collective-permute-start(bf16[16,32,128]{2,1,0:T(8,128)(2,1)S(1)} %pad_maximum_fusion.own_ref), channel_id=1, source_target_pairs={{2,4},{4,2},{3,5},{5,3},{6,8},{8,6},{7,9},{9,7},{10,12},{12,10},{1... | collective-permute-start | bytes 393224 | tf_op jit(solution)/shard_map/ppermute | solution.py:22
  13.8 6.8 %collective-permute-start.1 = (bf16[16,32,128]{2,1,0:T(8,128)(2,1)S(1)}, bf16[16,32,128]{2,1,0:T(8,128)(2,1)S(1)}, u32[]{:S(2)}, u32[]{:S(2)}) collective-permute-start(bf16[16,32,128]{2,1,0:T(8,128)(2,1)S(1)} %pad_maximum_fusion.own_ref), channel_id=1, source_target_pairs={{0,2},{2,0},{1,3},{3,1},{4,6},{6,4},{5,7},{7,5},{8,10},{10,8},{9,1... | collective-permute-start | bytes 393224 | tf_op jit(solution)/shard_map/ppermute | solution.py:22
  17.1 1.6 copy-start.1
  21.6 6.2 %collective-permute-start.3 = (bf16[16,32,128]{2,1,0:T(8,128)(2,1)S(1)}, bf16[16,32,128]{2,1,0:T(8,128)(2,1)S(1)}, u32[]{:S(2)}, u32[]{:S(2)}) collective-permute-start(bf16[16,32,128]{2,1,0:T(8,128)(2,1)S(1)} %get-tuple-element.40), channel_id=1, source_target_pairs={{2,4},{4,2},{3,5},{5,3},{6,8},{8,6},{7,9},{9,7},{10,12},{12,10},{1... | collective-permute-start | bytes 393224 | tf_op jit(solution)/shard_map/ppermute | solution.py:22
  28.7 7.0 %collective-permute-start.4 = (bf16[16,32,128]{2,1,0:T(8,128)(2,1)S(1)}, bf16[16,32,128]{2,1,0:T(8,128)(2,1)S(1)}, u32[]{:S(2)}, u32[]{:S(2)}) collective-permute-start(bf16[16,32,128]{2,1,0:T(8,128)(2,1)S(1)} %get-tuple-element.41), channel_id=1, source_target_pairs={{2,4},{4,2},{3,5},{5,3},{6,8},{8,6},{7,9},{9,7},{10,12},{12,10},{1... | collective-permute-start | bytes 393224 | tf_op jit(solution)/shard_map/ppermute | solution.py:22
  36.6 8.0 %collective-permute-start.5 = (bf16[16,32,128]{2,1,0:T(8,128)(2,1)S(1)}, bf16[16,32,128]{2,1,0:T(8,128)(2,1)S(1)}, u32[]{:S(2)}, u32[]{:S(2)}) collective-permute-start(bf16[16,32,128]{2,1,0:T(8,128)(2,1)S(1)} %get-tuple-element.43), channel_id=1, source_target_pairs={{2,4},{4,2},{3,5},{5,3},{6,8},{8,6},{7,9},{9,7},{10,12},{12,10},{1... | collective-permute-start | bytes 393224 | tf_op jit(solution)/shard_map/ppermute | solution.py:22
  45.5 6.6 %collective-permute-start.6 = (bf16[16,32,128]{2,1,0:T(8,128)(2,1)S(1)}, bf16[16,32,128]{2,1,0:T(8,128)(2,1)S(1)}, u32[]{:S(2)}, u32[]{:S(2)}) collective-permute-start(bf16[16,32,128]{2,1,0:T(8,128)(2,1)S(1)} %get-tuple-element.45), channel_id=1, source_target_pairs={{2,4},{4,2},{3,5},{5,3},{6,8},{8,6},{7,9},{9,7},{10,12},{12,10},{1... | collective-permute-start | bytes 393224 | tf_op jit(solution)/shard_map/ppermute | solution.py:22
  53.0 8.9 %collective-permute-start.7 = (bf16[16,32,128]{2,1,0:T(8,128)(2,1)S(1)}, bf16[16,32,128]{2,1,0:T(8,128)(2,1)S(1)}, u32[]{:S(2)}, u32[]{:S(2)}) collective-permute-start(bf16[16,32,128]{2,1,0:T(8,128)(2,1)S(1)} %get-tuple-element.47), channel_id=1, source_target_pairs={{2,4},{4,2},{3,5},{5,3},{6,8},{8,6},{7,9},{9,7},{10,12},{12,10},{1... | collective-permute-start | bytes 393224 | tf_op jit(solution)/shard_map/ppermute | solution.py:22
  62.8 7.4 %collective-permute-start.8 = (bf16[16,32,128]{2,1,0:T(8,128)(2,1)S(1)}, bf16[16,32,128]{2,1,0:T(8,128)(2,1)S(1)}, u32[]{:S(2)}, u32[]{:S(2)}) collective-permute-start(bf16[16,32,128]{2,1,0:T(8,128)(2,1)S(1)} %get-tuple-element.49), channel_id=1, source_target_pairs={{2,4},{4,2},{3,5},{5,3},{6,8},{8,6},{7,9},{9,7},{10,12},{12,10},{1... | collective-permute-start | bytes 393224 | tf_op jit(solution)/shard_map/ppermute | solution.py:22
  71.1 8.3 %collective-permute-start.9 = (bf16[16,32,128]{2,1,0:T(8,128)(2,1)S(1)}, bf16[16,32,128]{2,1,0:T(8,128)(2,1)S(1)}, u32[]{:S(2)}, u32[]{:S(2)}) collective-permute-start(bf16[16,32,128]{2,1,0:T(8,128)(2,1)S(1)} %get-tuple-element.51), channel_id=1, source_target_pairs={{2,4},{4,2},{3,5},{5,3},{6,8},{8,6},{7,9},{9,7},{10,12},{12,10},{1... | collective-permute-start | bytes 393224 | tf_op jit(solution)/shard_map/ppermute | solution.py:22
  80.3 9.7 %collective-permute-start.10 = (bf16[16,32,128]{2,1,0:T(8,128)(2,1)S(1)}, bf16[16,32,128]{2,1,0:T(8,128)(2,1)S(1)}, u32[]{:S(2)}, u32[]{:S(2)}) collective-permute-start(bf16[16,32,128]{2,1,0:T(8,128)(2,1)S(1)} %get-tuple-element.53), channel_id=1, source_target_pairs={{2,4},{4,2},{3,5},{5,3},{6,8},{8,6},{7,9},{9,7},{10,12},{12,10},{1... | collective-permute-start | bytes 393224 | tf_op jit(solution)/shard_map/ppermute | solution.py:22
  90.9 7.9 %collective-permute-start.11 = (bf16[16,32,128]{2,1,0:T(8,128)(2,1)S(1)}, bf16[16,32,128]{2,1,0:T(8,128)(2,1)S(1)}, u32[]{:S(2)}, u32[]{:S(2)}) collective-permute-start(bf16[16,32,128]{2,1,0:T(8,128)(2,1)S(1)} %get-tuple-element.55), channel_id=1, source_target_pairs={{2,4},{4,2},{3,5},{5,3},{6,8},{8,6},{7,9},{9,7},{10,12},{12,10},{1... | collective-permute-start | bytes 393224 | tf_op jit(solution)/shard_map/ppermute | solution.py:22
  99.7 7.3 %collective-permute-start.12 = (bf16[16,32,128]{2,1,0:T(8,128)(2,1)S(1)}, bf16[16,32,128]{2,1,0:T(8,128)(2,1)S(1)}, u32[]{:S(2)}, u32[]{:S(2)}) collective-permute-start(bf16[16,32,128]{2,1,0:T(8,128)(2,1)S(1)} %get-tuple-element.57), channel_id=1, source_target_pairs={{2,4},{4,2},{3,5},{5,3},{6,8},{8,6},{7,9},{9,7},{10,12},{12,10},{1... | collective-permute-start | bytes 393224 | tf_op jit(solution)/shard_map/ppermute | solution.py:22
  107.9 9.6 %collective-permute-start.13 = (bf16[16,32,128]{2,1,0:T(8,128)(2,1)S(1)}, bf16[16,32,128]{2,1,0:T(8,128)(2,1)S(1)}, u32[]{:S(2)}, u32[]{:S(2)}) collective-permute-start(bf16[16,32,128]{2,1,0:T(8,128)(2,1)S(1)} %step.20), channel_id=1, source_target_pairs={{2,4},{4,2},{3,5},{5,3},{6,8},{8,6},{7,9},{9,7},{10,12},{12,10},{1... | collective-permute-start | bytes 393224 | tf_op jit(solution)/shard_map/ppermute | solution.py:22

commit v7 on v6

--- a/solution.py
+++ b/solution.py
@@ -232,12 +232,14 @@
     )
     done = rows[...]
     factor_ref[...] = jnp.where(upper, done[:, :size], 0.0)
-    basis_ref[...] = jnp.dot(
-        done[:, size:],
-        block_ref[...],
-        precision=lax.Precision.HIGHEST,
-        preferred_element_type=jnp.float32,
-    )
+    inverse, middle = done[:, size:], size // 2
+    for first, last in ((0, middle), (middle, size)):
+        basis_ref[first:last, :] = jnp.dot(
+            inverse[first:last, :last],
+            block_ref[:last, :],
+            precision=lax.Precision.HIGHEST,
+            preferred_element_type=jnp.float32,
+        )
 
 
 def finish(gram, block):

time: 212 us -> 212 us (level)
  no operation moved by 1% of the time
where the time goes in v7:
time: 212 us; the launch traced here: 211 us
  blocking collectives  176 us (83%)
  Pallas kernels  16.3 us (8%)
  starting transfers between devices  12.2 us (6%)
  local copies, waits for them, and re-layouts  2.51 us (1%)
    all_gather x11, blocking collectives, paired(): return lax.all_gather(value, 'ry', axis_index_groups=groups)  79.5 us
    all_to_all x1, blocking collectives, shards(): parts = lax.all_to_all(summed(parts, outer), 'rx', 0, 0, tiled=True)  50.4 us
    all_gather x3, blocking collectives, of_both_cores(): return lax.all_gather(value, 'ry', axis_index_groups=groups)  29.6 us
    all_to_all x1, blocking collectives, shards(): lax.all_to_all(parts, 'ry', 0, 0, axis_index_groups=same_core, tiled=True)  16.7 us
    pallas_call x12, Pallas kernels, stepped(): pl.pallas_call(kernel, in_specs=[VMEM] * (len(scalars) + len(blocks)), ou...  10.7 us
    ppermute x13, starting transfers between devices, traded(): return lax.ppermute(value, AXES, route)  9.95 us
  transfers between devices with their start and end apart: 14, of which 2 were waited for; matrix products, arithmetic and copies ran while one was open for 0% of the time, Pallas kernels for 1%

profile of v7, /device:TPU:1, one launch (start us, length us, event | category | flops | bytes accessed | tf_op | source)
XLA Modules:
  0.0 211.3 jit_solution(17000180472456069299)
XLA Ops:
  0.6 0.0 copy-start
  0.7 0.9 copy-done
  1.6 0.8 fusion.12
  2.4 8.4 %all-gather = bf16[18,32,128]{2,1,0:T(8,128)(2,1)S(1)} all-gather(bf16[9,32,128]{2,1,0:T(8,128)(2,1)S(1)} %fusion.1), channel_id=2, replica_groups={{0,1},{2,3},{4,5},{6,7},{8,9},{10,11},{12,13},{14,15},{16,17},{18,19},{..., dimensions={0}, use_global_device_ids=true | all-gather | bytes 221184 | tf_op jit(solution)/shard_map/all_gather | solution.py:35
  10.9 2.3 %collective-permute-start.2 = (bf16[8,8,128,128]{3,2,1,0:T(8,128)(2,1)}, bf16[8,8,128,128]{3,2,1,0:T(8,128)(2,1)S(1)}, u32[]{:S(2)}, u32[]{:S(2)}) collective-permute-start(bf16[8,8,128,128]{3,2,1,0:T(8,128)(2,1)} %near_ref), channel_id=1, source_target_pairs={{0,1},{1,0},{2,3},{3,2},{4,5},{5,4},{6,7},{7,6},{8,9},{9,8},{10,11... | collective-permute-start | bytes 6291464 | tf_op jit(solution)/shard_map/ppermute | solution.py:40
  13.1 0.7 collective-permute-start
  13.8 1.9 collective-permute-start.1
  15.8 0.1 convert_add_fusion
  15.8 0.7 fusion.4.index_ref
  16.6 0.6 collective-permute-done.2.far_ref
  17.1 1.6 copy-done.1
  18.7 1.1 turn_tiles.1.tiles_ref
  19.9 0.0 collective-permute-done.odd_ref
  19.9 0.8 collective-permute-done.1.even_ref
  20.7 0.9 first_step.1
  21.6 0.7 collective-permute-start.3
  22.3 5.5 %all-gather.1 = bf16[32,32,128]{2,1,0:T(8,128)(2,1)S(1)} all-gather(bf16[16,32,128]{2,1,0:T(8,128)(2,1)S(1)} %get-tuple-element.40), channel_id=3, replica_groups={{0,2},{1,3},{4,6},{5,7},{8,10},{9,11},{12,14},{13,15},{16,18},{17,19},{..., dimensions={0}, use_global_device_ids=true | all-gather | bytes 393216 | tf_op jit(solution)/shard_map/all_gather | solution.py:29
  27.8 0.0 collective-permute-done.3.odd_ref
  27.8 0.9 step.11
  28.7 0.7 collective-permute-start.4
  29.4 6.4 %all-gather.2 = bf16[32,32,128]{2,1,0:T(8,128)(2,1)S(1)} all-gather(bf16[16,32,128]{2,1,0:T(8,128)(2,1)S(1)} %get-tuple-element.41), channel_id=4, replica_groups={{0,2},{1,3},{4,6},{5,7},{8,10},{9,11},{12,14},{13,15},{16,18},{17,19},{..., dimensions={0}, use_global_device_ids=true | all-gather | bytes 393216 | tf_op jit(solution)/shard_map/all_gather | solution.py:29
  35.7 0.0 collective-permute-done.4.odd_ref
  35.7 0.9 step.12
  36.6 0.7 collective-permute-start.5
  37.3 7.3 %all-gather.3 = bf16[32,32,128]{2,1,0:T(8,128)(2,1)S(1)} all-gather(bf16[16,32,128]{2,1,0:T(8,128)(2,1)S(1)} %get-tuple-element.43), channel_id=5, replica_groups={{0,2},{1,3},{4,6},{5,7},{8,10},{9,11},{12,14},{13,15},{16,18},{17,19},{..., dimensions={0}, use_global_device_ids=true | all-gather | bytes 393216 | tf_op jit(solution)/shard_map/all_gather | solution.py:29
  44.6 0.0 collective-permute-done.5.odd_ref
  44.6 0.9 step.13
  45.5 0.7 collective-permute-start.6
  46.2 6.0 %all-gather.4 = bf16[32,32,128]{2,1,0:T(8,128)(2,1)S(1)} all-gather(bf16[16,32,128]{2,1,0:T(8,128)(2,1)S(1)} %get-tuple-element.45), channel_id=6, replica_groups={{0,2},{1,3},{4,6},{5,7},{8,10},{9,11},{12,14},{13,15},{16,18},{17,19},{..., dimensions={0}, use_global_device_ids=true | all-gather | bytes 393216 | tf_op jit(solution)/shard_map/all_gather | solution.py:29
  52.1 0.0 collective-permute-done.6.odd_ref
  52.1 0.9 step.14
  53.0 0.7 collective-permute-start.7
  53.7 8.2 %all-gather.5 = bf16[32,32,128]{2,1,0:T(8,128)(2,1)S(1)} all-gather(bf16[16,32,128]{2,1,0:T(8,128)(2,1)S(1)} %get-tuple-element.47), channel_id=7, replica_groups={{0,2},{1,3},{4,6},{5,7},{8,10},{9,11},{12,14},{13,15},{16,18},{17,19},{..., dimensions={0}, use_global_device_ids=true | all-gather | bytes 393216 | tf_op jit(solution)/shard_map/all_gather | solution.py:29
  61.9 0.0 collective-permute-done.7.odd_ref
  61.9 0.9 step.15
  62.8 0.7 collective-permute-start.8
  63.5 6.7 %all-gather.6 = bf16[32,32,128]{2,1,0:T(8,128)(2,1)S(1)} all-gather(bf16[16,32,128]{2,1,0:T(8,128)(2,1)S(1)} %get-tuple-element.49), channel_id=8, replica_groups={{0,2},{1,3},{4,6},{5,7},{8,10},{9,11},{12,14},{13,15},{16,18},{17,19},{..., dimensions={0}, use_global_device_ids=true | all-gather | bytes 393216 | tf_op jit(solution)/shard_map/all_gather | solution.py:29
  70.2 0.0 collective-permute-done.8.odd_ref
  70.2 0.9 step.16
  71.1 0.7 collective-permute-start.9
  71.7 7.7 %all-gather.7 = bf16[32,32,128]{2,1,0:T(8,128)(2,1)S(1)} all-gather(bf16[16,32,128]{2,1,0:T(8,128)(2,1)S(1)} %get-tuple-element.51), channel_id=9, replica_groups={{0,2},{1,3},{4,6},{5,7},{8,10},{9,11},{12,14},{13,15},{16,18},{17,19},{..., dimensions={0}, use_global_device_ids=true | all-gather | bytes 393216 | tf_op jit(solution)/shard_map/all_gather | solution.py:29
  79.4 0.0 collective-permute-done.9.odd_ref
  79.4 0.9 step.17
  80.3 0.7 collective-permute-start.10
  81.0 9.1 %all-gather.8 = bf16[32,32,128]{2,1,0:T(8,128)(2,1)S(1)} all-gather(bf16[16,32,128]{2,1,0:T(8,128)(2,1)S(1)} %get-tuple-element.53), channel_id=10, replica_groups={{0,2},{1,3},{4,6},{5,7},{8,10},{9,11},{12,14},{13,15},{16,18},{17,19},{..., dimensions={0}, use_global_device_ids=true | all-gather | bytes 393216 | tf_op jit(solution)/shard_map/all_gather | solution.py:29
  90.0 0.0 collective-permute-done.10.odd_ref
  90.1 0.9 step.18
  91.0 0.7 collective-permute-start.11
  91.6 7.1 %all-gather.9 = bf16[32,32,128]{2,1,0:T(8,128)(2,1)S(1)} all-gather(bf16[16,32,128]{2,1,0:T(8,128)(2,1)S(1)} %get-tuple-element.55), channel_id=11, replica_groups={{0,2},{1,3},{4,6},{5,7},{8,10},{9,11},{12,14},{13,15},{16,18},{17,19},{..., dimensions={0}, use_global_device_ids=true | all-gather | bytes 393216 | tf_op jit(solution)/shard_map/all_gather | solution.py:29
  98.7 0.0 collective-permute-done.11.odd_ref
  98.7 0.9 step.19
  99.6 0.7 collective-permute-start.12
  100.3 6.7 %all-gather.10 = bf16[32,32,128]{2,1,0:T(8,128)(2,1)S(1)} all-gather(bf16[16,32,128]{2,1,0:T(8,128)(2,1)S(1)} %get-tuple-element.57), channel_id=12, replica_groups={{0,2},{1,3},{4,6},{5,7},{8,10},{9,11},{12,14},{13,15},{16,18},{17,19},{..., dimensions={0}, use_global_device_ids=true | all-gather | bytes 393216 | tf_op jit(solution)/shard_map/all_gather | solution.py:29
  107.1 0.0 collective-permute-done.12.odd_ref
  107.1 0.9 step.20
  108.0 0.7 collective-permute-start.13
  108.6 8.9 %all-gather.11 = bf16[32,32,128]{2,1,0:T(8,128)(2,1)S(1)} all-gather(bf16[16,32,128]{2,1,0:T(8,128)(2,1)S(1)} %step.20), channel_id=13, replica_groups={{0,2},{1,3},{4,6},{5,7},{8,10},{9,11},{12,14},{13,15},{16,18},{17,19},{..., dimensions={0}, use_global_device_ids=true | all-gather | bytes 393216 | tf_op jit(solution)/shard_map/all_gather | solution.py:29
  117.6 0.9 step.21.mine_ref
  118.5 15.9 %all-gather.12 = f32[32,32,128]{2,1,0:T(8,128)S(1)} all-gather(f32[16,32,128]{2,1,0:T(8,128)S(1)} %step.21.mine_ref), channel_id=14, replica_groups={{0,1},{2,3},{4,5},{6,7},{8,9},{10,11},{12,13},{14,15},{16,17},{18,19},{..., dimensions={0}, use_global_device_ids=true | all-gather | bytes 786432 | tf_op jit(solution)/shard_map/all_gather | solution.py:35
  134.4 0.7 gram.1
  135.1 16.7 %all_to_all.10.parts_ref = f32[8,16,128]{2,1,0:T(8,128)S(1)} all-to-all(f32[8,16,128]{2,1,0:T(8,128)S(1)} %get-tuple-element.60), channel_id=1, replica_groups={{0,2,4,6,8,10,12,14},{1,3,5,7,9,11,13,15},{16,18,20,22,24,26,28,30},{17..., dimensions={0} | all-to-all | bytes 131072 | tf_op jit(solution)/shard_map/all_to_all | solution.py:315
  151.8 50.4 %all_to_all.11.parts_ref = f32[32,16,128]{2,1,0:T(8,128)S(1)} all-to-all(f32[32,16,128]{2,1,0:T(8,128)S(1)} %sum_parts.2), channel_id=1, replica_groups=mesh['rx'=32,'ry'=16] {'rx'}, dimensions={0} | all-to-all | bytes 524288 | tf_op jit(solution)/shard_map/all_to_all | solution.py:316
  202.3 5.2 %all_gather.107.gram_ref = f32[2,16,128]{2,1,0:T(8,128)S(1)} all-gather(f32[1,16,128]{2,1,0:T(8,128)S(1)} %sum_parts.3), channel_id=1, replica_groups={{0,1},{2,3},{4,5},{6,7},{8,9},{10,11},{12,13},{14,15},{16,17},{18,19},{..., dimensions={0}, use_global_device_ids=true | all-gather | bytes 24576 | tf_op jit(solution)/shard_map/all_gather | solution.py:35
  207.5 3.8 %factor_and_solve.1 = (f32[64,1024]{1,0:T(8,128)}, f32[64,64]{1,0:T(8,128)}) custom-call(f32[2,16,128]{2,1,0:T(8,128)S(1)} %all_gather.107.gram_ref, f32[64,1024]{1,0:T(8,128)S(1)} %get-tuple-element.61.block_ref), custom_call_target="tpu_custom_call" | custom-call | tf_op jit(solution)/shard_map/factor_and_solve/pallas_call | solution.py:247
  (14 shorter events, 0.2 us)
Async XLA Ops:
  0.6 0.9 copy-start
  10.9 6.3 %collective-permute-start.2 = (bf16[8,8,128,128]{3,2,1,0:T(8,128)(2,1)}, bf16[8,8,128,128]{3,2,1,0:T(8,128)(2,1)S(1)}, u32[]{:S(2)}, u32[]{:S(2)}) collective-permute-start(bf16[8,8,128,128]{3,2,1,0:T(8,128)(2,1)} %near_ref), channel_id=1, source_target_pairs={{0,1},{1,0},{2,3},{3,2},{4,5},{5,4},{6,7},{7,6},{8,9},{9,8},{10,11... | collective-permute-start | bytes 6291464 | tf_op jit(solution)/shard_map/ppermute | solution.py:40
  13.1 6.7 %collective-permute-start = (bf16[16,32,128]{2,1,0:T(8,128)(2,1)S(1)}, bf16[16,32,128]{2,1,0:T(8,128)(2,1)S(1)}, u32[]{:S(2)}, u32[]{:S(2)}) collective-permute-start(bf16[16,32,128]{2,1,0:T(8,128)(2,1)S(1)} %pad_maximum_fusion.own_ref), channel_id=1, source_target_pairs={{2,4},{4,2},{3,5},{5,3},{6,8},{8,6},{7,9},{9,7},{10,12},{12,10},{1... | collective-permute-start | bytes 393224 | tf_op jit(solution)/shard_map/ppermute | solution.py:22
  13.8 6.8 %collective-permute-start.1 = (bf16[16,32,128]{2,1,0:T(8,128)(2,1)S(1)}, bf16[16,32,128]{2,1,0:T(8,128)(2,1)S(1)}, u32[]{:S(2)}, u32[]{:S(2)}) collective-permute-start(bf16[16,32,128]{2,1,0:T(8,128)(2,1)S(1)} %pad_maximum_fusion.own_ref), channel_id=1, source_target_pairs={{0,2},{2,0},{1,3},{3,1},{4,6},{6,4},{5,7},{7,5},{8,10},{10,8},{9,1... | collective-permute-start | bytes 393224 | tf_op jit(solution)/shard_map/ppermute | solution.py:22
  17.1 1.6 copy-start.1
  21.6 6.2 %collective-permute-start.3 = (bf16[16,32,128]{2,1,0:T(8,128)(2,1)S(1)}, bf16[16,32,128]{2,1,0:T(8,128)(2,1)S(1)}, u32[]{:S(2)}, u32[]{:S(2)}) collective-permute-start(bf16[16,32,128]{2,1,0:T(8,128)(2,1)S(1)} %get-tuple-element.40), channel_id=1, source_target_pairs={{2,4},{4,2},{3,5},{5,3},{6,8},{8,6},{7,9},{9,7},{10,12},{12,10},{1... | collective-permute-start | bytes 393224 | tf_op jit(solution)/shard_map/ppermute | solution.py:22
  28.7 7.0 %collective-permute-start.4 = (bf16[16,32,128]{2,1,0:T(8,128)(2,1)S(1)}, bf16[16,32,128]{2,1,0:T(8,128)(2,1)S(1)}, u32[]{:S(2)}, u32[]{:S(2)}) collective-permute-start(bf16[16,32,128]{2,1,0:T(8,128)(2,1)S(1)} %get-tuple-element.41), channel_id=1, source_target_pairs={{2,4},{4,2},{3,5},{5,3},{6,8},{8,6},{7,9},{9,7},{10,12},{12,10},{1... | collective-permute-start | bytes 393224 | tf_op jit(solution)/shard_map/ppermute | solution.py:22
  36.6 8.0 %collective-permute-start.5 = (bf16[16,32,128]{2,1,0:T(8,128)(2,1)S(1)}, bf16[16,32,128]{2,1,0:T(8,128)(2,1)S(1)}, u32[]{:S(2)}, u32[]{:S(2)}) collective-permute-start(bf16[16,32,128]{2,1,0:T(8,128)(2,1)S(1)} %get-tuple-element.43), channel_id=1, source_target_pairs={{2,4},{4,2},{3,5},{5,3},{6,8},{8,6},{7,9},{9,7},{10,12},{12,10},{1... | collective-permute-start | bytes 393224 | tf_op jit(solution)/shard_map/ppermute | solution.py:22
  45.5 6.6 %collective-permute-start.6 = (bf16[16,32,128]{2,1,0:T(8,128)(2,1)S(1)}, bf16[16,32,128]{2,1,0:T(8,128)(2,1)S(1)}, u32[]{:S(2)}, u32[]{:S(2)}) collective-permute-start(bf16[16,32,128]{2,1,0:T(8,128)(2,1)S(1)} %get-tuple-element.45), channel_id=1, source_target_pairs={{2,4},{4,2},{3,5},{5,3},{6,8},{8,6},{7,9},{9,7},{10,12},{12,10},{1... | collective-permute-start | bytes 393224 | tf_op jit(solution)/shard_map/ppermute | solution.py:22
  53.0 8.9 %collective-permute-start.7 = (bf16[16,32,128]{2,1,0:T(8,128)(2,1)S(1)}, bf16[16,32,128]{2,1,0:T(8,128)(2,1)S(1)}, u32[]{:S(2)}, u32[]{:S(2)}) collective-permute-start(bf16[16,32,128]{2,1,0:T(8,128)(2,1)S(1)} %get-tuple-element.47), channel_id=1, source_target_pairs={{2,4},{4,2},{3,5},{5,3},{6,8},{8,6},{7,9},{9,7},{10,12},{12,10},{1... | collective-permute-start | bytes 393224 | tf_op jit(solution)/shard_map/ppermute | solution.py:22
  62.8 7.4 %collective-permute-start.8 = (bf16[16,32,128]{2,1,0:T(8,128)(2,1)S(1)}, bf16[16,32,128]{2,1,0:T(8,128)(2,1)S(1)}, u32[]{:S(2)}, u32[]{:S(2)}) collective-permute-start(bf16[16,32,128]{2,1,0:T(8,128)(2,1)S(1)} %get-tuple-element.49), channel_id=1, source_target_pairs={{2,4},{4,2},{3,5},{5,3},{6,8},{8,6},{7,9},{9,7},{10,12},{12,10},{1... | collective-permute-start | bytes 393224 | tf_op jit(solution)/shard_map/ppermute | solution.py:22
  71.1 8.3 %collective-permute-start.9 = (bf16[16,32,128]{2,1,0:T(8,128)(2,1)S(1)}, bf16[16,32,128]{2,1,0:T(8,128)(2,1)S(1)}, u32[]{:S(2)}, u32[]{:S(2)}) collective-permute-start(bf16[16,32,128]{2,1,0:T(8,128)(2,1)S(1)} %get-tuple-element.51), channel_id=1, source_target_pairs={{2,4},{4,2},{3,5},{5,3},{6,8},{8,6},{7,9},{9,7},{10,12},{12,10},{1... | collective-permute-start | bytes 393224 | tf_op jit(solution)/shard_map/ppermute | solution.py:22
  80.3 9.8 %collective-permute-start.10 = (bf16[16,32,128]{2,1,0:T(8,128)(2,1)S(1)}, bf16[16,32,128]{2,1,0:T(8,128)(2,1)S(1)}, u32[]{:S(2)}, u32[]{:S(2)}) collective-permute-start(bf16[16,32,128]{2,1,0:T(8,128)(2,1)S(1)} %get-tuple-element.53), channel_id=1, source_target_pairs={{2,4},{4,2},{3,5},{5,3},{6,8},{8,6},{7,9},{9,7},{10,12},{12,10},{1... | collective-permute-start | bytes 393224 | tf_op jit(solution)/shard_map/ppermute | solution.py:22
  91.0 7.8 %collective-permute-start.11 = (bf16[16,32,128]{2,1,0:T(8,128)(2,1)S(1)}, bf16[16,32,128]{2,1,0:T(8,128)(2,1)S(1)}, u32[]{:S(2)}, u32[]{:S(2)}) collective-permute-start(bf16[16,32,128]{2,1,0:T(8,128)(2,1)S(1)} %get-tuple-element.55), channel_id=1, source_target_pairs={{2,4},{4,2},{3,5},{5,3},{6,8},{8,6},{7,9},{9,7},{10,12},{12,10},{1... | collective-permute-start | bytes 393224 | tf_op jit(solution)/shard_map/ppermute | solution.py:22
  99.6 7.4 %collective-permute-start.12 = (bf16[16,32,128]{2,1,0:T(8,128)(2,1)S(1)}, bf16[16,32,128]{2,1,0:T(8,128)(2,1)S(1)}, u32[]{:S(2)}, u32[]{:S(2)}) collective-permute-start(bf16[16,32,128]{2,1,0:T(8,128)(2,1)S(1)} %get-tuple-element.57), channel_id=1, source_target_pairs={{2,4},{4,2},{3,5},{5,3},{6,8},{8,6},{7,9},{9,7},{10,12},{12,10},{1... | collective-permute-start | bytes 393224 | tf_op jit(solution)/shard_map/ppermute | solution.py:22
  108.0 9.6 %collective-permute-start.13 = (bf16[16,32,128]{2,1,0:T(8,128)(2,1)S(1)}, bf16[16,32,128]{2,1,0:T(8,128)(2,1)S(1)}, u32[]{:S(2)}, u32[]{:S(2)}) collective-permute-start(bf16[16,32,128]{2,1,0:T(8,128)(2,1)S(1)} %step.20), channel_id=1, source_target_pairs={{2,4},{4,2},{3,5},{5,3},{6,8},{8,6},{7,9},{9,7},{10,12},{12,10},{1... | collective-permute-start | bytes 393224 | tf_op jit(solution)/shard_map/ppermute | solution.py:22

commit v8 on v7

--- a/solution.py
+++ b/solution.py
@@ -38,6 +38,38 @@
 def swapped(value):
     count = lax.axis_size(AXES)
     return lax.ppermute(value, AXES, [(source, source ^ 1) for source in range(count)])
+
+
+def split_kernel(position_ref, start_ref, pattern_ref, mine_ref, sent_ref):
+    tiles, half, width = mine_ref.shape
+    position = position_ref[0, 0]
+    even = position % 2 == 0
+    for tile in range(tiles):
+        columns = slice(tile * width, (tile + 1) * width)
+        low, high = start_ref[0:half, columns], start_ref[half : 2 * half, columns]
+        mine_ref[tile] = jnp.where(even, low, high)
+        sent_ref[tile] = jnp.where(even, high, low)
+    rows, slots = pattern_ref.shape
+    row_ids = lax.broadcasted_iota(jnp.int32, (rows, slots), 0) + position * rows
+    away = (pattern_ref[...] - row_ids).astype(jnp.float32)
+    away = jnp.concatenate([away, jnp.zeros((rows, width - slots), jnp.float32)], axis=1)
+    away = jnp.concatenate([away, jnp.zeros((half - rows, width), jnp.float32)], axis=0)
+    sent_ref[tiles] = away.astype(jnp.bfloat16)
+
+
+def split(position, start_block, pattern, width):
+    half, tiles = start_block.shape[0] // 2, start_block.shape[1] // width
+    return pl.pallas_call(
+        split_kernel,
+        in_specs=[VMEM, VMEM, VMEM],
+        out_specs=[VMEM, VMEM],
+        out_shape=[
+            jax.ShapeDtypeStruct((tiles, half, width), jnp.bfloat16),
+            jax.ShapeDtypeStruct((tiles + 1, half, width), jnp.bfloat16),
+        ],
+        compiler_params=pltpu.CompilerParams(vmem_limit_bytes=LIMIT),
+        name="split_start",
+    )(position, start_block, pattern)
 
 
 def turn_kernel(near_ref, far_ref, out_ref):
@@ -268,15 +300,11 @@
     chip_rows = 2 * rows_local
 
     row_ids = jnp.arange(rows_local, dtype=jnp.int32)[:, None]
-    away = tile_pattern - (position * rows_local + row_ids)
-    start_tiles = start_block.reshape(vectors, rows_local, tile_size).transpose(1, 0, 2)
-    low, high = start_tiles[:, :half], start_tiles[:, half:]
-    slots = away.shape[1]
-    packed = jnp.zeros((1, half, tile_size), jnp.bfloat16)
-    packed = packed.at[0, :rows_local, :slots].set(away.astype(jnp.bfloat16))
-    sent = of_both_cores(jnp.concatenate([jnp.where(core == 0, high, low), packed], axis=0))
+    slots = tile_pattern.shape[1]
+    mine, sent = split(position.reshape(1, 1), start_block, tile_pattern, tile_size)
+    sent = of_both_cores(sent)
     theirs = jnp.where(core == 0, sent[1], sent[0])
-    rounded = jnp.concatenate([jnp.where(core == 0, low, high), theirs[:rows_local]], axis=0)
+    rounded = jnp.concatenate([mine, theirs[:rows_local]], axis=0)
     far_away = theirs[rows_local, :rows_local, :slots].astype(jnp.int32)
 
     operator_tiles, rounded = lax.optimization_barrier((operator_tiles, rounded))

time: 212 us -> 212 us (level)
  no operation moved by 1% of the time
where the time goes in v8:
time: 212 us; the launch traced here: 211 us
  blocking collectives  176 us (83%)
  Pallas kernels  16.4 us (8%)
  starting transfers between devices  12.2 us (6%)
  local copies, waits for them, and re-layouts  3.18 us (2%)
    all_gather x11, blocking collectives, paired(): return lax.all_gather(value, 'ry', axis_index_groups=groups)  79.5 us
    all_to_all x1, blocking collectives, shards(): parts = lax.all_to_all(summed(parts, outer), 'rx', 0, 0, tiled=True)  50.4 us
    all_gather x3, blocking collectives, of_both_cores(): return lax.all_gather(value, 'ry', axis_index_groups=groups)  29.6 us
    all_to_all x1, blocking collectives, shards(): lax.all_to_all(parts, 'ry', 0, 0, axis_index_groups=same_core, tiled=True)  16.7 us
    pallas_call x12, Pallas kernels, stepped(): pl.pallas_call(kernel, in_specs=[VMEM] * (len(scalars) + len(blocks)), ou...  10.7 us
    ppermute x13, starting transfers between devices, traded(): return lax.ppermute(value, AXES, route)  9.95 us
  transfers between devices with their start and end apart: 14, of which 2 were waited for; matrix products, arithmetic and copies ran while one was open for 0% of the time, Pallas kernels for 1%

profile of v8, /device:TPU:1, one launch (start us, length us, event | category | flops | bytes accessed | tf_op | source)
XLA Modules:
  0.0 211.2 jit_solution(2651424361721463734)
XLA Ops:
  0.7 0.9 copy-done.1
  1.6 0.7 copy-done.2
  2.2 0.1 split_start.1
  2.3 8.4 %all-gather = bf16[18,32,128]{2,1,0:T(8,128)(2,1)S(1)} all-gather(bf16[9,32,128]{2,1,0:T(8,128)(2,1)S(1)} %get-tuple-element.28), channel_id=2, replica_groups={{0,1},{2,3},{4,5},{6,7},{8,9},{10,11},{12,13},{14,15},{16,17},{18,19},{..., dimensions={0}, use_global_device_ids=true | all-gather | bytes 221184 | tf_op jit(solution)/shard_map/all_gather | solution.py:35
  10.8 2.3 %collective-permute-start.2 = (bf16[8,8,128,128]{3,2,1,0:T(8,128)(2,1)}, bf16[8,8,128,128]{3,2,1,0:T(8,128)(2,1)S(1)}, u32[]{:S(2)}, u32[]{:S(2)}) collective-permute-start(bf16[8,8,128,128]{3,2,1,0:T(8,128)(2,1)} %near_ref), channel_id=1, source_target_pairs={{0,1},{1,0},{2,3},{3,2},{4,5},{5,4},{6,7},{7,6},{8,9},{9,8},{10,11... | collective-permute-start | bytes 6291464 | tf_op jit(solution)/shard_map/ppermute | solution.py:40
  13.1 0.7 collective-permute-start
  13.7 1.9 collective-permute-start.1
  15.7 0.1 convert_add_fusion
  15.8 0.7 fusion.2.index_ref
  16.5 0.6 collective-permute-done.2.far_ref
  17.1 1.6 copy-done
  18.7 1.1 turn_tiles.1.tiles_ref
  19.8 0.0 collective-permute-done.odd_ref
  19.8 0.8 collective-permute-done.1.even_ref
  20.6 0.9 first_step.1
  21.5 0.7 collective-permute-start.3
  22.2 5.5 %all-gather.1 = bf16[32,32,128]{2,1,0:T(8,128)(2,1)S(1)} all-gather(bf16[16,32,128]{2,1,0:T(8,128)(2,1)S(1)} %get-tuple-element.32), channel_id=3, replica_groups={{0,2},{1,3},{4,6},{5,7},{8,10},{9,11},{12,14},{13,15},{16,18},{17,19},{..., dimensions={0}, use_global_device_ids=true | all-gather | bytes 393216 | tf_op jit(solution)/shard_map/all_gather | solution.py:29
  27.7 0.0 collective-permute-done.3.odd_ref
  27.7 0.9 step.11
  28.6 0.7 collective-permute-start.4
  29.3 6.3 %all-gather.2 = bf16[32,32,128]{2,1,0:T(8,128)(2,1)S(1)} all-gather(bf16[16,32,128]{2,1,0:T(8,128)(2,1)S(1)} %get-tuple-element.33), channel_id=4, replica_groups={{0,2},{1,3},{4,6},{5,7},{8,10},{9,11},{12,14},{13,15},{16,18},{17,19},{..., dimensions={0}, use_global_device_ids=true | all-gather | bytes 393216 | tf_op jit(solution)/shard_map/all_gather | solution.py:29
  35.7 0.0 collective-permute-done.4.odd_ref
  35.7 0.9 step.12
  36.6 0.7 collective-permute-start.5
  37.2 7.3 %all-gather.3 = bf16[32,32,128]{2,1,0:T(8,128)(2,1)S(1)} all-gather(bf16[16,32,128]{2,1,0:T(8,128)(2,1)S(1)} %get-tuple-element.35), channel_id=5, replica_groups={{0,2},{1,3},{4,6},{5,7},{8,10},{9,11},{12,14},{13,15},{16,18},{17,19},{..., dimensions={0}, use_global_device_ids=true | all-gather | bytes 393216 | tf_op jit(solution)/shard_map/all_gather | solution.py:29
  44.5 0.0 collective-permute-done.5.odd_ref
  44.5 0.9 step.13
  45.4 0.7 collective-permute-start.6
  46.1 6.0 %all-gather.4 = bf16[32,32,128]{2,1,0:T(8,128)(2,1)S(1)} all-gather(bf16[16,32,128]{2,1,0:T(8,128)(2,1)S(1)} %get-tuple-element.37), channel_id=6, replica_groups={{0,2},{1,3},{4,6},{5,7},{8,10},{9,11},{12,14},{13,15},{16,18},{17,19},{..., dimensions={0}, use_global_device_ids=true | all-gather | bytes 393216 | tf_op jit(solution)/shard_map/all_gather | solution.py:29
  52.1 0.0 collective-permute-done.6.odd_ref
  52.1 0.9 step.14
  53.0 0.7 collective-permute-start.7
  53.6 8.2 %all-gather.5 = bf16[32,32,128]{2,1,0:T(8,128)(2,1)S(1)} all-gather(bf16[16,32,128]{2,1,0:T(8,128)(2,1)S(1)} %get-tuple-element.39), channel_id=7, replica_groups={{0,2},{1,3},{4,6},{5,7},{8,10},{9,11},{12,14},{13,15},{16,18},{17,19},{..., dimensions={0}, use_global_device_ids=true | all-gather | bytes 393216 | tf_op jit(solution)/shard_map/all_gather | solution.py:29
  61.8 0.0 collective-permute-done.7.odd_ref
  61.8 0.9 step.15
  62.7 0.7 collective-permute-start.8
  63.4 6.7 %all-gather.6 = bf16[32,32,128]{2,1,0:T(8,128)(2,1)S(1)} all-gather(bf16[16,32,128]{2,1,0:T(8,128)(2,1)S(1)} %get-tuple-element.41), channel_id=8, replica_groups={{0,2},{1,3},{4,6},{5,7},{8,10},{9,11},{12,14},{13,15},{16,18},{17,19},{..., dimensions={0}, use_global_device_ids=true | all-gather | bytes 393216 | tf_op jit(solution)/shard_map/all_gather | solution.py:29
  70.1 0.0 collective-permute-done.8.odd_ref
  70.1 0.9 step.16
  71.0 0.7 collective-permute-start.9
  71.7 7.7 %all-gather.7 = bf16[32,32,128]{2,1,0:T(8,128)(2,1)S(1)} all-gather(bf16[16,32,128]{2,1,0:T(8,128)(2,1)S(1)} %get-tuple-element.43), channel_id=9, replica_groups={{0,2},{1,3},{4,6},{5,7},{8,10},{9,11},{12,14},{13,15},{16,18},{17,19},{..., dimensions={0}, use_global_device_ids=true | all-gather | bytes 393216 | tf_op jit(solution)/shard_map/all_gather | solution.py:29
  79.3 0.0 collective-permute-done.9.odd_ref
  79.3 0.9 step.17
  80.2 0.7 collective-permute-start.10
  80.9 9.0 %all-gather.8 = bf16[32,32,128]{2,1,0:T(8,128)(2,1)S(1)} all-gather(bf16[16,32,128]{2,1,0:T(8,128)(2,1)S(1)} %get-tuple-element.45), channel_id=10, replica_groups={{0,2},{1,3},{4,6},{5,7},{8,10},{9,11},{12,14},{13,15},{16,18},{17,19},{..., dimensions={0}, use_global_device_ids=true | all-gather | bytes 393216 | tf_op jit(solution)/shard_map/all_gather | solution.py:29
  89.9 0.0 collective-permute-done.10.odd_ref
  89.9 0.9 step.18
  90.8 0.7 collective-permute-start.11
  91.5 7.2 %all-gather.9 = bf16[32,32,128]{2,1,0:T(8,128)(2,1)S(1)} all-gather(bf16[16,32,128]{2,1,0:T(8,128)(2,1)S(1)} %get-tuple-element.47), channel_id=11, replica_groups={{0,2},{1,3},{4,6},{5,7},{8,10},{9,11},{12,14},{13,15},{16,18},{17,19},{..., dimensions={0}, use_global_device_ids=true | all-gather | bytes 393216 | tf_op jit(solution)/shard_map/all_gather | solution.py:29
  98.7 0.0 collective-permute-done.11.odd_ref
  98.7 0.9 step.19
  99.6 0.7 collective-permute-start.12
  100.3 6.7 %all-gather.10 = bf16[32,32,128]{2,1,0:T(8,128)(2,1)S(1)} all-gather(bf16[16,32,128]{2,1,0:T(8,128)(2,1)S(1)} %get-tuple-element.49), channel_id=12, replica_groups={{0,2},{1,3},{4,6},{5,7},{8,10},{9,11},{12,14},{13,15},{16,18},{17,19},{..., dimensions={0}, use_global_device_ids=true | all-gather | bytes 393216 | tf_op jit(solution)/shard_map/all_gather | solution.py:29
  106.9 0.9 step.20
  107.8 0.7 collective-permute-start.13
  108.5 9.0 %all-gather.11 = bf16[32,32,128]{2,1,0:T(8,128)(2,1)S(1)} all-gather(bf16[16,32,128]{2,1,0:T(8,128)(2,1)S(1)} %step.20), channel_id=13, replica_groups={{0,2},{1,3},{4,6},{5,7},{8,10},{9,11},{12,14},{13,15},{16,18},{17,19},{..., dimensions={0}, use_global_device_ids=true | all-gather | bytes 393216 | tf_op jit(solution)/shard_map/all_gather | solution.py:29
  117.5 0.0 collective-permute-done.13.odd_ref
  117.5 0.9 step.21.mine_ref
  118.4 15.9 %all-gather.12 = f32[32,32,128]{2,1,0:T(8,128)S(1)} all-gather(f32[16,32,128]{2,1,0:T(8,128)S(1)} %step.21.mine_ref), channel_id=14, replica_groups={{0,1},{2,3},{4,5},{6,7},{8,9},{10,11},{12,13},{14,15},{16,17},{18,19},{..., dimensions={0}, use_global_device_ids=true | all-gather | bytes 786432 | tf_op jit(solution)/shard_map/all_gather | solution.py:35
  134.3 0.7 gram.1
  135.0 16.7 %all_to_all.10.parts_ref = f32[8,16,128]{2,1,0:T(8,128)S(1)} all-to-all(f32[8,16,128]{2,1,0:T(8,128)S(1)} %get-tuple-element.52), channel_id=1, replica_groups={{0,2,4,6,8,10,12,14},{1,3,5,7,9,11,13,15},{16,18,20,22,24,26,28,30},{17..., dimensions={0} | all-to-all | bytes 131072 | tf_op jit(solution)/shard_map/all_to_all | solution.py:343
  151.7 50.4 %all_to_all.11.parts_ref = f32[32,16,128]{2,1,0:T(8,128)S(1)} all-to-all(f32[32,16,128]{2,1,0:T(8,128)S(1)} %sum_parts.2), channel_id=1, replica_groups=mesh['rx'=32,'ry'=16] {'rx'}, dimensions={0} | all-to-all | bytes 524288 | tf_op jit(solution)/shard_map/all_to_all | solution.py:344
  202.2 5.2 %all_gather.107.gram_ref = f32[2,16,128]{2,1,0:T(8,128)S(1)} all-gather(f32[1,16,128]{2,1,0:T(8,128)S(1)} %sum_parts.3), channel_id=1, replica_groups={{0,1},{2,3},{4,5},{6,7},{8,9},{10,11},{12,13},{14,15},{16,17},{18,19},{..., dimensions={0}, use_global_device_ids=true | all-gather | bytes 24576 | tf_op jit(solution)/shard_map/all_gather | solution.py:35
  207.4 3.8 %factor_and_solve.1 = (f32[64,1024]{1,0:T(8,128)}, f32[64,64]{1,0:T(8,128)}) custom-call(f32[2,16,128]{2,1,0:T(8,128)S(1)} %all_gather.107.gram_ref, f32[64,1024]{1,0:T(8,128)S(1)} %get-tuple-element.53.block_ref), custom_call_target="tpu_custom_call" | custom-call | tf_op jit(solution)/shard_map/factor_and_solve/pallas_call | solution.py:279
  (12 shorter events, 0.1 us)
Async XLA Ops:
  0.6 0.9 copy-start.1
  1.6 0.7 copy-start.2
  10.8 6.3 %collective-permute-start.2 = (bf16[8,8,128,128]{3,2,1,0:T(8,128)(2,1)}, bf16[8,8,128,128]{3,2,1,0:T(8,128)(2,1)S(1)}, u32[]{:S(2)}, u32[]{:S(2)}) collective-permute-start(bf16[8,8,128,128]{3,2,1,0:T(8,128)(2,1)} %near_ref), channel_id=1, source_target_pairs={{0,1},{1,0},{2,3},{3,2},{4,5},{5,4},{6,7},{7,6},{8,9},{9,8},{10,11... | collective-permute-start | bytes 6291464 | tf_op jit(solution)/shard_map/ppermute | solution.py:40
  13.1 6.7 %collective-permute-start = (bf16[16,32,128]{2,1,0:T(8,128)(2,1)S(1)}, bf16[16,32,128]{2,1,0:T(8,128)(2,1)S(1)}, u32[]{:S(2)}, u32[]{:S(2)}) collective-permute-start(bf16[16,32,128]{2,1,0:T(8,128)(2,1)S(1)} %pad_maximum_fusion.own_ref), channel_id=1, source_target_pairs={{2,4},{4,2},{3,5},{5,3},{6,8},{8,6},{7,9},{9,7},{10,12},{12,10},{1... | collective-permute-start | bytes 393224 | tf_op jit(solution)/shard_map/ppermute | solution.py:22
  13.7 6.8 %collective-permute-start.1 = (bf16[16,32,128]{2,1,0:T(8,128)(2,1)S(1)}, bf16[16,32,128]{2,1,0:T(8,128)(2,1)S(1)}, u32[]{:S(2)}, u32[]{:S(2)}) collective-permute-start(bf16[16,32,128]{2,1,0:T(8,128)(2,1)S(1)} %pad_maximum_fusion.own_ref), channel_id=1, source_target_pairs={{0,2},{2,0},{1,3},{3,1},{4,6},{6,4},{5,7},{7,5},{8,10},{10,8},{9,1... | collective-permute-start | bytes 393224 | tf_op jit(solution)/shard_map/ppermute | solution.py:22
  17.1 1.6 copy-start
  21.5 6.2 %collective-permute-start.3 = (bf16[16,32,128]{2,1,0:T(8,128)(2,1)S(1)}, bf16[16,32,128]{2,1,0:T(8,128)(2,1)S(1)}, u32[]{:S(2)}, u32[]{:S(2)}) collective-permute-start(bf16[16,32,128]{2,1,0:T(8,128)(2,1)S(1)} %get-tuple-element.32), channel_id=1, source_target_pairs={{2,4},{4,2},{3,5},{5,3},{6,8},{8,6},{7,9},{9,7},{10,12},{12,10},{1... | collective-permute-start | bytes 393224 | tf_op jit(solution)/shard_map/ppermute | solution.py:22
  28.6 7.0 %collective-permute-start.4 = (bf16[16,32,128]{2,1,0:T(8,128)(2,1)S(1)}, bf16[16,32,128]{2,1,0:T(8,128)(2,1)S(1)}, u32[]{:S(2)}, u32[]{:S(2)}) collective-permute-start(bf16[16,32,128]{2,1,0:T(8,128)(2,1)S(1)} %get-tuple-element.33), channel_id=1, source_target_pairs={{2,4},{4,2},{3,5},{5,3},{6,8},{8,6},{7,9},{9,7},{10,12},{12,10},{1... | collective-permute-start | bytes 393224 | tf_op jit(solution)/shard_map/ppermute | solution.py:22
  36.6 8.0 %collective-permute-start.5 = (bf16[16,32,128]{2,1,0:T(8,128)(2,1)S(1)}, bf16[16,32,128]{2,1,0:T(8,128)(2,1)S(1)}, u32[]{:S(2)}, u32[]{:S(2)}) collective-permute-start(bf16[16,32,128]{2,1,0:T(8,128)(2,1)S(1)} %get-tuple-element.35), channel_id=1, source_target_pairs={{2,4},{4,2},{3,5},{5,3},{6,8},{8,6},{7,9},{9,7},{10,12},{12,10},{1... | collective-permute-start | bytes 393224 | tf_op jit(solution)/shard_map/ppermute | solution.py:22
  45.4 6.6 %collective-permute-start.6 = (bf16[16,32,128]{2,1,0:T(8,128)(2,1)S(1)}, bf16[16,32,128]{2,1,0:T(8,128)(2,1)S(1)}, u32[]{:S(2)}, u32[]{:S(2)}) collective-permute-start(bf16[16,32,128]{2,1,0:T(8,128)(2,1)S(1)} %get-tuple-element.37), channel_id=1, source_target_pairs={{2,4},{4,2},{3,5},{5,3},{6,8},{8,6},{7,9},{9,7},{10,12},{12,10},{1... | collective-permute-start | bytes 393224 | tf_op jit(solution)/shard_map/ppermute | solution.py:22
  53.0 8.9 %collective-permute-start.7 = (bf16[16,32,128]{2,1,0:T(8,128)(2,1)S(1)}, bf16[16,32,128]{2,1,0:T(8,128)(2,1)S(1)}, u32[]{:S(2)}, u32[]{:S(2)}) collective-permute-start(bf16[16,32,128]{2,1,0:T(8,128)(2,1)S(1)} %get-tuple-element.39), channel_id=1, source_target_pairs={{2,4},{4,2},{3,5},{5,3},{6,8},{8,6},{7,9},{9,7},{10,12},{12,10},{1... | collective-permute-start | bytes 393224 | tf_op jit(solution)/shard_map/ppermute | solution.py:22
  62.7 7.4 %collective-permute-start.8 = (bf16[16,32,128]{2,1,0:T(8,128)(2,1)S(1)}, bf16[16,32,128]{2,1,0:T(8,128)(2,1)S(1)}, u32[]{:S(2)}, u32[]{:S(2)}) collective-permute-start(bf16[16,32,128]{2,1,0:T(8,128)(2,1)S(1)} %get-tuple-element.41), channel_id=1, source_target_pairs={{2,4},{4,2},{3,5},{5,3},{6,8},{8,6},{7,9},{9,7},{10,12},{12,10},{1... | collective-permute-start | bytes 393224 | tf_op jit(solution)/shard_map/ppermute | solution.py:22
  71.0 8.3 %collective-permute-start.9 = (bf16[16,32,128]{2,1,0:T(8,128)(2,1)S(1)}, bf16[16,32,128]{2,1,0:T(8,128)(2,1)S(1)}, u32[]{:S(2)}, u32[]{:S(2)}) collective-permute-start(bf16[16,32,128]{2,1,0:T(8,128)(2,1)S(1)} %get-tuple-element.43), channel_id=1, source_target_pairs={{2,4},{4,2},{3,5},{5,3},{6,8},{8,6},{7,9},{9,7},{10,12},{12,10},{1... | collective-permute-start | bytes 393224 | tf_op jit(solution)/shard_map/ppermute | solution.py:22
  80.2 9.7 %collective-permute-start.10 = (bf16[16,32,128]{2,1,0:T(8,128)(2,1)S(1)}, bf16[16,32,128]{2,1,0:T(8,128)(2,1)S(1)}, u32[]{:S(2)}, u32[]{:S(2)}) collective-permute-start(bf16[16,32,128]{2,1,0:T(8,128)(2,1)S(1)} %get-tuple-element.45), channel_id=1, source_target_pairs={{2,4},{4,2},{3,5},{5,3},{6,8},{8,6},{7,9},{9,7},{10,12},{12,10},{1... | collective-permute-start | bytes 393224 | tf_op jit(solution)/shard_map/ppermute | solution.py:22
  90.8 7.9 %collective-permute-start.11 = (bf16[16,32,128]{2,1,0:T(8,128)(2,1)S(1)}, bf16[16,32,128]{2,1,0:T(8,128)(2,1)S(1)}, u32[]{:S(2)}, u32[]{:S(2)}) collective-permute-start(bf16[16,32,128]{2,1,0:T(8,128)(2,1)S(1)} %get-tuple-element.47), channel_id=1, source_target_pairs={{2,4},{4,2},{3,5},{5,3},{6,8},{8,6},{7,9},{9,7},{10,12},{12,10},{1... | collective-permute-start | bytes 393224 | tf_op jit(solution)/shard_map/ppermute | solution.py:22
  99.6 7.3 %collective-permute-start.12 = (bf16[16,32,128]{2,1,0:T(8,128)(2,1)S(1)}, bf16[16,32,128]{2,1,0:T(8,128)(2,1)S(1)}, u32[]{:S(2)}, u32[]{:S(2)}) collective-permute-start(bf16[16,32,128]{2,1,0:T(8,128)(2,1)S(1)} %get-tuple-element.49), channel_id=1, source_target_pairs={{2,4},{4,2},{3,5},{5,3},{6,8},{8,6},{7,9},{9,7},{10,12},{12,10},{1... | collective-permute-start | bytes 393224 | tf_op jit(solution)/shard_map/ppermute | solution.py:22
  107.8 9.6 %collective-permute-start.13 = (bf16[16,32,128]{2,1,0:T(8,128)(2,1)S(1)}, bf16[16,32,128]{2,1,0:T(8,128)(2,1)S(1)}, u32[]{:S(2)}, u32[]{:S(2)}) collective-permute-start(bf16[16,32,128]{2,1,0:T(8,128)(2,1)S(1)} %step.20), channel_id=1, source_target_pairs={{2,4},{4,2},{3,5},{5,3},{6,8},{8,6},{7,9},{9,7},{10,12},{12,10},{1... | collective-permute-start | bytes 393224 | tf_op jit(solution)/shard_map/ppermute | solution.py:22
